TPU v7x, 512 devices: a whole 4x4x16 slice. The times are simulated.
512 devices in a mesh: leaf: 512 (over y, z, x, core).
Axes of the slice: x: 4, y: 4, z: 16, core: 2. Of those that a mesh axis runs over, the one named last changes fastest.
Arguments:
- sources: float32 [16, 1048576], P(None, 'leaf'), may hold values from -6 to 6
- leaf_cluster_basis: float32 [8192, 64, 128], P('leaf'), may hold values from -0.5 to 0.5
- local_transfer: float32 [15360, 4096], P('leaf'), may hold values from -0.5 to 0.5
- far_coupling: float32 [15360, 3, 4096], P('leaf'), may hold values from -0.5 to 0.5
- far_partner: int32 [15360, 3], P('leaf'), may hold values from 0 to 8191
- far_count: int32 [15360], P('leaf'), may hold values from 1 to 3
- top_transfer: float32 [512, 9, 4096], P('leaf'), may hold values from -0.5 to 0.5
- top_coupling: float32 [512, 9, 2, 4096], P('leaf'), may hold values from -0.75 to 0.75
- near_block: float32 [8192, 2, 128, 128], P('leaf'), may hold values from -0.375 to 0.375
- near_partner: int32 [8192, 2], P('leaf'), may hold values from 0 to 8191, as said below
- near_count: int32 [8192], P('leaf'), may hold values from 1 to 2
Outputs:
- product: float32 [16, 1048576], P(None, 'leaf')
Inputs may be any that keep to these rules, and one draw needn't show every extreme that they name: `near_partner`: slot 0 of each row is the row's own leaf; every other entry is a leaf 1 to 8 positions away from it.
All inputs are finite; a program needn't handle non-finite values.
Results may differ from a plain program's by a relative error of at most 0.0003.
Values sent between devices are 32-bit elements; how exact they have to be, the bound alone decides.
No kernel may reach another device: no remote copies, remote signals or barrier semaphores. Data moves between devices by JAX's collectives and lax.ppermute only.
A program may use at most 64 MiB of HBM per device.

v0:
```python
import jax
import jax.numpy as jnp
from jax import lax
from jax.sharding import PartitionSpec as P

HIGH_ACCURACY = lax.Precision.HIGHEST


def with_halo(block, sides, width):
    for axis, dim in sides:
        count = lax.axis_size(axis)
        forward = [(i, i + 1) for i in range(count - 1)]
        backward = [(target, source) for source, target in forward]
        low = lax.ppermute(
            lax.slice_in_dim(block, block.shape[dim] - width, None, axis=dim), axis, forward
        )
        high = lax.ppermute(lax.slice_in_dim(block, 0, width, axis=dim), axis, backward)
        block = jnp.concatenate([low, block, high], axis=dim)
    return block


def shifted(shard, axis, by):
    peers = lax.axis_size(axis)
    pairs = [(i, i + by) for i in range(peers) if 0 <= i + by < peers]
    return lax.ppermute(shard, axis, pairs)


def on_device(
    sources,
    leaf_cluster_basis,
    local_transfer,
    far_coupling,
    far_partner,
    far_count,
    top_transfer,
    top_coupling,
    near_block,
    near_partner,
    near_count,
):
    vectors = sources.shape[0]
    leaves, basis_rank, leaf_size = leaf_cluster_basis.shape
    local_count = local_transfer.shape[0]
    far_slots = far_partner.shape[1]
    near_slots = near_partner.shape[1]
    device_list = lax.axis_size("leaf")
    device_index = lax.axis_index("leaf")
    leaf_entries = sources.reshape(vectors, leaves, leaf_size)
    present_value = jnp.einsum(
        "ztq,tfq->tzf", leaf_entries, leaf_cluster_basis, precision=HIGH_ACCURACY
    )
    transfers = local_transfer.reshape(local_count, basis_rank, basis_rank)
    layout = []
    offset = 0
    clusters = leaves
    while clusters >= 2:
        layout.append((clusters, offset))
        offset += clusters
        clusters = clusters // 2
    coefficients = []
    for clusters, offset in layout:
        coefficients.append(present_value)
        carried = jnp.einsum(
            "nsr,nrq->nsq",
            present_value,
            transfers[offset : offset + clusters],
            precision=HIGH_ACCURACY,
        )
        present_value = carried.reshape(clusters // 2, 2, vectors, basis_rank).sum(axis=1)
    stacked = jnp.concatenate(
        [coefs.reshape(coefs.shape[0], vectors * basis_rank) for coefs in coefficients], axis=0
    )
    extended_coefs = with_halo(stacked, (("leaf", 0),), local_count)
    far_terms = []
    for level_number, (clusters, offset) in enumerate(layout):
        partners = far_partner[offset : offset + clusters]
        places = (
            (partners // clusters - device_index + 1) * local_count + offset + partners % clusters
        )
        picked = extended_coefs[places].reshape(clusters, far_slots, vectors, basis_rank)
        present = (
            jnp.arange(far_slots)[None, :] < far_count[offset : offset + clusters, None]
        ).astype(jnp.float32)
        blocks = far_coupling[offset : offset + clusters].reshape(
            clusters, far_slots, basis_rank, basis_rank
        )
        far_terms.append(
            jnp.einsum(
                "npsr,nprq->nsq",
                picked * present[:, :, None, None],
                blocks,
                precision=HIGH_ACCURACY,
            )
        )
    levels_top = device_list.bit_length() - 1
    top_steps = top_transfer.reshape(levels_top, basis_rank, basis_rank)
    siblings = top_coupling.reshape(levels_top, 2, basis_rank, basis_rank)
    window = present_value[0]
    left_terms = []
    right_terms = []
    for level in range(1, levels_top + 1):
        extent = 2 ** (level - 1)
        carried = jnp.dot(window, top_steps[level - 1], precision=HIGH_ACCURACY)
        payload = jnp.concatenate([window, carried], axis=1)
        arrived = shifted(payload, "leaf", -extent)
        left_terms.append(
            jnp.dot(arrived[:, :basis_rank], siblings[level - 1, 0], precision=HIGH_ACCURACY)
        )
        right_terms.append(jnp.dot(window, siblings[level - 1, 1], precision=HIGH_ACCURACY))
        window = carried + arrived[:, basis_rank:]
    level_y = jnp.zeros((vectors, basis_rank), jnp.float32)
    for level in range(levels_top, 0, -1):
        extent = 2 ** (level - 1)
        outgoing = jnp.concatenate([level_y, right_terms[level - 1]], axis=1)
        arrived = shifted(outgoing, "leaf", extent)
        step_matrix = top_steps[level - 1]
        local_next = (
            jnp.dot(level_y, step_matrix.T, precision=HIGH_ACCURACY) + left_terms[level - 1]
        )
        remote_next = (
            jnp.dot(arrived[:, :basis_rank], step_matrix.T, precision=HIGH_ACCURACY)
            + arrived[:, basis_rank:]
        )
        is_right = device_index % 2**level == extent
        level_y = jnp.where(is_right, remote_next, local_next)
    present_value = level_y[None]
    for (clusters, offset), coupled in reversed(list(zip(layout, far_terms))):
        spread = jnp.repeat(present_value, 2, axis=0)
        present_value = (
            jnp.einsum(
                "nsq,nrq->nsr",
                spread,
                transfers[offset : offset + clusters],
                precision=HIGH_ACCURACY,
            )
            + coupled
        )
    distant_field = jnp.einsum(
        "pvx,pxb->vpb", present_value, leaf_cluster_basis, precision=HIGH_ACCURACY
    )
    extent = leaves
    extended = with_halo(sources, (("leaf", 1),), extent * leaf_size)
    extended = extended.reshape(vectors, leaves + 2 * extent, leaf_size)
    places = near_partner - (device_index * leaves - extent)
    picked = extended[:, places]
    present = (jnp.arange(near_slots)[None, :] < near_count[:, None]).astype(jnp.float32)
    near_field = jnp.einsum(
        "lpkj,slpj->slk", near_block, picked * present[None, :, :, None], precision=HIGH_ACCURACY
    )
    return (distant_field + near_field).reshape(vectors, leaves * leaf_size)


def solution(mesh):
    placed = (
        P(None, "leaf"),
        P("leaf", None, None),
        P("leaf", None),
        P("leaf", None, None),
        P("leaf", None),
        P("leaf"),
        P("leaf", None, None),
        P("leaf", None, None, None),
        P("leaf", None, None, None),
        P("leaf", None),
        P("leaf"),
    )
    return jax.shard_map(
        on_device, mesh=mesh, in_specs=placed, out_specs=P(None, "leaf"), check_vma=False
    )
```

profile of v0, /device:TPU:24, one launch (start us, length us, event | category | flops | bytes accessed | tf_op | source)
XLA Modules:
  0.0 264.7 jit_solution(13859297195790106834)
XLA Ops:
  1.4 1.9 fusion.24
  5.7 1.9 collective-permute-start.18
  7.6 13.2 %collective-permute-start.19 = (f32[30,1024]{1,0:T(8,128)}, f32[30,1024]{1,0:T(8,128)}, u32[]{:S(2)}, u32[]{:S(2)}) collective-permute-start(f32[30,1024]{1,0:T(8,128)} %pad_maximum_fusion), channel_id=1, source_target_pairs={{1,0},{2,1},{3,2},{4,3},{5,4},{6,5},{7,6},{8,7},{9,8},{10,9},{11,1... | collective-permute-start | bytes 368648 | tf_op jit(solution)/shard_map/ppermute | solution.py:17
  20.8 1.9 collective-permute-start.20
  22.8 7.9 %collective-permute-start.21 = (f32[16,2048]{1,0:T(8,128)}, f32[16,2048]{1,0:T(8,128)}, u32[]{:S(2)}, u32[]{:S(2)}) collective-permute-start(f32[16,2048]{1,0:T(8,128)} %param.11), channel_id=1, source_target_pairs={{1,0},{2,1},{3,2},{4,3},{5,4},{6,5},{7,6},{8,7},{9,8},{10,9},{11,1... | collective-permute-start | bytes 393224 | tf_op jit(solution)/shard_map/ppermute | solution.py:17
  33.8 1.9 collective-permute-start
  35.7 1.3 compare_select_fusion.3
  37.0 1.3 compare_select_fusion.2
  40.9 1.3 compare_select_fusion.1
  44.8 1.3 reshape.210
  57.4 1.3 fusion.69
  59.6 1.3 fusion.70
  61.5 1.7 slice.340
  63.1 1.7 slice.343
  64.9 1.8 slice.346
  67.8 1.4 squeeze.92
  69.2 1.4 squeeze.93
  70.6 1.4 squeeze.94
  72.0 1.4 squeeze.95
  73.4 1.4 squeeze.96
  74.8 1.4 squeeze.97
  76.2 1.4 squeeze.98
  77.6 1.7 reshape.217
  79.4 1.9 reshape.220
  81.3 2.2 reshape.223
  83.5 1.8 reshape.226
  88.1 1.9 collective-permute-start.1
  90.1 1.5 fusion.32
  91.6 2.1 collective-permute-done.1
  95.6 1.9 collective-permute-start.2
  98.4 4.2 %collective-permute-done.2 = f32[16,128]{1,0:T(8,128)S(1)} collective-permute-done((f32[16,128]{1,0:T(8,128)S(1)}, f32[16,128]{1,0:T(8,128)S(1)}, u32[]{:S(2)}, u32[]{:S(2)}) %collective-permute-start.2) | collective-permute-done | bytes 8224 | tf_op jit(solution)/shard_map/ppermute | solution.py:25
  104.6 2.0 collective-permute-start.3
  107.5 2.6 collective-permute-done.3
  112.1 2.4 collective-permute-start.4
  115.5 3.1 %collective-permute-done.4 = f32[16,128]{1,0:T(8,128)S(1)} collective-permute-done((f32[16,128]{1,0:T(8,128)S(1)}, f32[16,128]{1,0:T(8,128)S(1)}, u32[]{:S(2)}, u32[]{:S(2)}) %collective-permute-start.4) | collective-permute-done | bytes 8224 | tf_op jit(solution)/shard_map/ppermute | solution.py:25
  120.5 5.8 %collective-permute-start.5 = (f32[16,128]{1,0:T(8,128)S(1)}, f32[16,128]{1,0:T(8,128)S(1)}, u32[]{:S(2)}, u32[]{:S(2)}) collective-permute-start(f32[16,128]{1,0:T(8,128)S(1)} %pad_maximum_fusion.6), channel_id=1, source_target_pairs={{32,0},{33,1},{34,2},{35,3},{36,4},{37,5},{38,6},{39,7},{40,8},{41... | collective-permute-start | bytes 24584 | tf_op jit(solution)/shard_map/ppermute | solution.py:25
  127.2 2.8 %collective-permute-done.5 = f32[16,128]{1,0:T(8,128)S(1)} collective-permute-done((f32[16,128]{1,0:T(8,128)S(1)}, f32[16,128]{1,0:T(8,128)S(1)}, u32[]{:S(2)}, u32[]{:S(2)}) %collective-permute-start.5) | collective-permute-done | bytes 8224 | tf_op jit(solution)/shard_map/ppermute | solution.py:25
  131.9 8.7 %collective-permute-start.6 = (f32[16,128]{1,0:T(8,128)S(1)}, f32[16,128]{1,0:T(8,128)S(1)}, u32[]{:S(2)}, u32[]{:S(2)}) collective-permute-start(f32[16,128]{1,0:T(8,128)S(1)} %pad_maximum_fusion.7), channel_id=1, source_target_pairs={{64,0},{65,1},{66,2},{67,3},{68,4},{69,5},{70,6},{71,7},{72,8},{73... | collective-permute-start | bytes 24584 | tf_op jit(solution)/shard_map/ppermute | solution.py:25
  141.6 4.6 %collective-permute-done.6 = f32[16,128]{1,0:T(8,128)S(1)} collective-permute-done((f32[16,128]{1,0:T(8,128)S(1)}, f32[16,128]{1,0:T(8,128)S(1)}, u32[]{:S(2)}, u32[]{:S(2)}) %collective-permute-start.6) | collective-permute-done | bytes 8224 | tf_op jit(solution)/shard_map/ppermute | solution.py:25
  148.1 2.4 collective-permute-start.7
  153.8 4.7 %collective-permute-start.9 = (f32[16,128]{1,0:T(8,128)S(1)}, f32[16,128]{1,0:T(8,128)S(1)}, u32[]{:S(2)}, u32[]{:S(2)}) collective-permute-start(f32[16,128]{1,0:T(8,128)S(1)} %pad_maximum_fusion.9), channel_id=1, source_target_pairs={{256,0},{257,1},{258,2},{259,3},{260,4},{261,5},{262,6},{263,7},{2... | collective-permute-start | bytes 24584 | tf_op jit(solution)/shard_map/ppermute | solution.py:25
  162.0 4.8 %collective-permute-done.8 = f32[16,128]{1,0:T(8,128)S(1)} collective-permute-done((f32[16,128]{1,0:T(8,128)S(1)}, f32[16,128]{1,0:T(8,128)S(1)}, u32[]{:S(2)}, u32[]{:S(2)}) %collective-permute-start.8) | collective-permute-done | bytes 8224 | tf_op jit(solution)/shard_map/ppermute | solution.py:25
  168.6 4.1 %collective-permute-done.10 = f32[16,128]{1,0:T(8,128)S(1)} collective-permute-done((f32[16,128]{1,0:T(8,128)S(1)}, f32[16,128]{1,0:T(8,128)S(1)}, u32[]{:S(2)}, u32[]{:S(2)}) %collective-permute-start.10) | collective-permute-done | bytes 8224 | tf_op jit(solution)/shard_map/ppermute | solution.py:25
  172.9 9.7 %collective-permute-start.11 = (f32[16,128]{1,0:T(8,128)S(1)}, f32[16,128]{1,0:T(8,128)S(1)}, u32[]{:S(2)}, u32[]{:S(2)}) collective-permute-start(f32[16,128]{1,0:T(8,128)S(1)} %pad_maximum_fusion.11), channel_id=1, source_target_pairs={{0,64},{1,65},{2,66},{3,67},{4,68},{5,69},{6,70},{7,71},{8,72},{9,... | collective-permute-start | bytes 24584 | tf_op jit(solution)/shard_map/ppermute | solution.py:25
  182.8 5.2 %collective-permute-done.11 = f32[16,128]{1,0:T(8,128)S(1)} collective-permute-done((f32[16,128]{1,0:T(8,128)S(1)}, f32[16,128]{1,0:T(8,128)S(1)}, u32[]{:S(2)}, u32[]{:S(2)}) %collective-permute-start.11) | collective-permute-done | bytes 8224 | tf_op jit(solution)/shard_map/ppermute | solution.py:25
  188.3 3.5 %collective-permute-start.12 = (f32[16,128]{1,0:T(8,128)S(1)}, f32[16,128]{1,0:T(8,128)S(1)}, u32[]{:S(2)}, u32[]{:S(2)}) collective-permute-start(f32[16,128]{1,0:T(8,128)S(1)} %pad_maximum_fusion.12), channel_id=1, source_target_pairs={{0,32},{1,33},{2,34},{3,35},{4,36},{5,37},{6,38},{7,39},{8,40},{9,... | collective-permute-start | bytes 24584 | tf_op jit(solution)/shard_map/ppermute | solution.py:25
  192.0 6.7 %collective-permute-done.12 = f32[16,128]{1,0:T(8,128)S(1)} collective-permute-done((f32[16,128]{1,0:T(8,128)S(1)}, f32[16,128]{1,0:T(8,128)S(1)}, u32[]{:S(2)}, u32[]{:S(2)}) %collective-permute-start.12) | collective-permute-done | bytes 8224 | tf_op jit(solution)/shard_map/ppermute | solution.py:25
  198.9 1.9 collective-permute-start.13
  201.0 6.5 %collective-permute-done.13 = f32[16,128]{1,0:T(8,128)S(1)} collective-permute-done((f32[16,128]{1,0:T(8,128)S(1)}, f32[16,128]{1,0:T(8,128)S(1)}, u32[]{:S(2)}, u32[]{:S(2)}) %collective-permute-start.13) | collective-permute-done | bytes 8224 | tf_op jit(solution)/shard_map/ppermute | solution.py:25
  207.7 2.4 collective-permute-start.14
  210.2 5.1 %collective-permute-done.14 = f32[16,128]{1,0:T(8,128)S(1)} collective-permute-done((f32[16,128]{1,0:T(8,128)S(1)}, f32[16,128]{1,0:T(8,128)S(1)}, u32[]{:S(2)}, u32[]{:S(2)}) %collective-permute-start.14) | collective-permute-done | bytes 8224 | tf_op jit(solution)/shard_map/ppermute | solution.py:25
  215.6 3.2 %collective-permute-start.15 = (f32[16,128]{1,0:T(8,128)S(1)}, f32[16,128]{1,0:T(8,128)S(1)}, u32[]{:S(2)}, u32[]{:S(2)}) collective-permute-start(f32[16,128]{1,0:T(8,128)S(1)} %pad_maximum_fusion.15), channel_id=1, source_target_pairs={{0,4},{1,5},{2,6},{3,7},{4,8},{5,9},{6,10},{7,11},{8,12},{9,13},{1... | collective-permute-start | bytes 24584 | tf_op jit(solution)/shard_map/ppermute | solution.py:25
  219.0 6.7 %collective-permute-done.15 = f32[16,128]{1,0:T(8,128)S(1)} collective-permute-done((f32[16,128]{1,0:T(8,128)S(1)}, f32[16,128]{1,0:T(8,128)S(1)}, u32[]{:S(2)}, u32[]{:S(2)}) %collective-permute-start.15) | collective-permute-done | bytes 8224 | tf_op jit(solution)/shard_map/ppermute | solution.py:25
  226.5 3.4 %collective-permute-start.16 = (f32[16,128]{1,0:T(8,128)}, f32[16,128]{1,0:T(8,128)}, u32[]{:S(2)}, u32[]{:S(2)}) collective-permute-start(f32[16,128]{1,0:T(8,128)} %pad_maximum_fusion.16), channel_id=1, source_target_pairs={{0,2},{1,3},{2,4},{3,5},{4,6},{5,7},{6,8},{7,9},{8,10},{9,11},{10,... | collective-permute-start | bytes 24584 | tf_op jit(solution)/shard_map/ppermute | solution.py:25
  230.7 2.3 concatenate.83
  234.4 1.3 gather_fusion.1
  235.7 1.6 reshape.219
  237.3 1.6 gather_fusion.3
  238.9 1.8 reshape.225
  240.7 2.1 convolution_bitcast_fusion.2
  242.9 3.8 %fusion.3 = f32[16,16,64]{2,1,0:T(8,128)} fusion(f32[16,3,64,64]{3,2,0,1:T(8,128)} %reshape.226, f32[16,3,16,64]{3,2,1,0:T(8,128)} %reshape.225, f32[16,3]{1,0:T(8,128)S(1)} %copy-done.35), kind=kOutput, calls=%fused_computation.11 | convolution fusion | flops 37797888 | bytes 1048768 | tf_op jit(solution)/shard_map/npsr,nprq->nsq/dot_general | solution.py:88
  250.1 1.9 collective-permute-start.17
  254.8 2.7 %convolution_bitcast_fusion = f32[16,16,128]{2,1,0:T(8,128)S(1)} fusion(f32[16,2,128,128]{3,2,1,0:T(8,128)S(1)} %copy-done, f32[16,2,16,128]{3,2,1,0:T(8,128)S(1)} %bitcast.185, f32[16,2]{1,0:T(8,128)} %fusion.70), kind=kOutput, calls=%fused_computation.7 | convolution fusion | flops 100728832 | bytes 2490496 | tf_op jit(solution)/shard_map/lpkj,slpj->slk/dot_general | solution.py:147
  257.5 2.1 collective-permute-done.17
  (233 shorter events, 69.3 us)
Async XLA Ops:
  0.0 254.8 %copy-start = (f32[16,2,128,128]{3,2,1,0:T(8,128)S(1)}, f32[16,2,128,128]{3,2,1,0:T(8,128)}, u32[]{:S(2)}) copy-start(f32[16,2,128,128]{3,2,1,0:T(8,128)} %param.19) | copy-start | bytes 6291460
  3.4 42.8 %copy-start.10 = (f32[16,1024]{1,0:T(8,128)}, f32[16,1024]{1,0:T(8,128)S(1)}, u32[]{:S(2)}) copy-start(f32[16,1024]{1,0:T(8,128)S(1)} %reshape.212) | copy-start | bytes 196612
  3.9 28.0 %copy-start.30 = (f32[1,9,4096]{2,0,1:T(1,128)S(1)}, f32[1,9,4096]{2,0,1:T(1,128)}, u32[]{:S(2)}) copy-start(f32[1,9,4096]{2,0,1:T(1,128)} %param.17) | copy-start | bytes 442372
  4.0 39.5 %copy-start.3 = (f32[8,64,64]{2,1,0:T(8,128)}, f32[8,64,64]{2,1,0:T(8,128)S(1)}, u32[]{:S(2)}) copy-start(f32[8,64,64]{2,1,0:T(8,128)S(1)} %slice.271) | copy-start | bytes 393220
  4.1 39.4 %copy-start.27 = (f32[8,1024]{1,0:T(8,128)}, f32[8,1024]{1,0:T(8,128)S(1)}, u32[]{:S(2)}) copy-start(f32[8,1024]{1,0:T(8,128)S(1)} %reshape.213) | copy-start | bytes 98308
  5.0 17.8 %copy-start.32 = (f32[2,1024]{1,0:T(2,128)}, f32[2,1024]{1,0:T(2,128)S(1)}, u32[]{:S(2)}) copy-start(f32[2,1024]{1,0:T(2,128)S(1)} %reshape.215) | copy-start | bytes 24580
  5.7 225.0 %collective-permute-start.18 = (f32[30,1024]{1,0:T(8,128)}, f32[30,1024]{1,0:T(8,128)}, u32[]{:S(2)}, u32[]{:S(2)}) collective-permute-start(f32[30,1024]{1,0:T(8,128)} %pad_maximum_fusion), channel_id=1, source_target_pairs={{0,1},{1,2},{2,3},{3,4},{4,5},{5,6},{6,7},{7,8},{8,9},{9,10},{10,1... | collective-permute-start | bytes 368648 | tf_op jit(solution)/shard_map/ppermute | solution.py:14
  7.6 223.1 %collective-permute-start.19 = (f32[30,1024]{1,0:T(8,128)}, f32[30,1024]{1,0:T(8,128)}, u32[]{:S(2)}, u32[]{:S(2)}) collective-permute-start(f32[30,1024]{1,0:T(8,128)} %pad_maximum_fusion), channel_id=1, source_target_pairs={{1,0},{2,1},{3,2},{4,3},{5,4},{6,5},{7,6},{8,7},{9,8},{10,9},{11,1... | collective-permute-start | bytes 368648 | tf_op jit(solution)/shard_map/ppermute | solution.py:17
  20.8 232.0 %collective-permute-start.20 = (f32[16,2048]{1,0:T(8,128)}, f32[16,2048]{1,0:T(8,128)}, u32[]{:S(2)}, u32[]{:S(2)}) collective-permute-start(f32[16,2048]{1,0:T(8,128)} %param.11), channel_id=1, source_target_pairs={{0,1},{1,2},{2,3},{3,4},{4,5},{5,6},{6,7},{7,8},{8,9},{9,10},{10,1... | collective-permute-start | bytes 393224 | tf_op jit(solution)/shard_map/ppermute | solution.py:14
  22.8 230.0 %collective-permute-start.21 = (f32[16,2048]{1,0:T(8,128)}, f32[16,2048]{1,0:T(8,128)}, u32[]{:S(2)}, u32[]{:S(2)}) collective-permute-start(f32[16,2048]{1,0:T(8,128)} %param.11), channel_id=1, source_target_pairs={{1,0},{2,1},{3,2},{4,3},{5,4},{6,5},{7,6},{8,7},{9,8},{10,9},{11,1... | collective-permute-start | bytes 393224 | tf_op jit(solution)/shard_map/ppermute | solution.py:17
  31.7 33.2 %copy-start.12 = (f32[2,64,64]{2,1,0:T(8,128)}, f32[2,64,64]{2,1,0:T(8,128)S(1)}, u32[]{:S(2)}) copy-start(f32[2,64,64]{2,1,0:T(8,128)S(1)} %slice.275) | copy-start | bytes 98308
  33.0 10.6 %copy-start.15 = (f32[64,64]{1,0:T(8,128)}, f32[64,64]{1,0:T(8,128)S(1)}, u32[]{:S(2)}) copy-start(f32[64,64]{1,0:T(8,128)S(1)} %squeeze.91) | copy-start | bytes 49156
  33.1 31.8 %copy-start.34 = (f32[16,64]{1,0:T(8,128)}, f32[16,64]{1,0:T(8,128)S(1)}, u32[]{:S(2)}) copy-start(f32[16,64]{1,0:T(8,128)S(1)} %fusion.103) | copy-start | bytes 12292
  33.8 51.6 %collective-permute-start = (f32[16,128]{1,0:T(8,128)}, f32[16,128]{1,0:T(8,128)}, u32[]{:S(2)}, u32[]{:S(2)}) collective-permute-start(f32[16,128]{1,0:T(8,128)} %pad_maximum_fusion.1), channel_id=1, source_target_pairs={{1,0},{2,1},{3,2},{4,3},{5,4},{6,5},{7,6},{8,7},{9,8},{10,9},{11,1... | collective-permute-start | bytes 24584 | tf_op jit(solution)/shard_map/ppermute | solution.py:25
  46.2 18.7 %copy-start.2 = (f32[9,2,64,64]{3,2,1,0:T(8,128)}, f32[9,2,64,64]{3,2,1,0:T(8,128)S(1)}, u32[]{:S(2)}) copy-start(f32[9,2,64,64]{3,2,1,0:T(8,128)S(1)} %reshape.210) | copy-start | bytes 884740
  46.2 18.6 %copy-start.25 = (f32[64,64]{1,0:T(8,128)}, f32[64,64]{1,0:T(8,128)S(1)}, u32[]{:S(2)}) copy-start(f32[64,64]{1,0:T(8,128)S(1)} %squeeze.100) | copy-start | bytes 49156
  85.3 75.9 %copy-start.36 = (f32[16,64]{1,0:T(8,128)S(1)}, f32[16,64]{1,0:T(8,128)}, u32[]{:S(2)}) copy-start(f32[16,64]{1,0:T(8,128)} %fusion.71) | copy-start | bytes 12292
  85.3 81.6 %copy-start.26 = (f32[64,64]{1,0:T(8,128)S(1)}, f32[64,64]{1,0:T(8,128)}, u32[]{:S(2)}) copy-start(f32[64,64]{1,0:T(8,128)} %copy-done.25) | copy-start | bytes 49156
  85.3 83.1 %copy-start.24 = (f32[64,64]{1,0:T(8,128)S(1)}, f32[64,64]{1,0:T(8,128)}, u32[]{:S(2)}) copy-start(f32[64,64]{1,0:T(8,128)} %squeeze.98) | copy-start | bytes 49156
  85.3 97.4 %copy-start.23 = (f32[64,64]{1,0:T(8,128)S(1)}, f32[64,64]{1,0:T(8,128)}, u32[]{:S(2)}) copy-start(f32[64,64]{1,0:T(8,128)} %squeeze.97) | copy-start | bytes 49156
  85.3 106.5 %copy-start.22 = (f32[64,64]{1,0:T(8,128)S(1)}, f32[64,64]{1,0:T(8,128)}, u32[]{:S(2)}) copy-start(f32[64,64]{1,0:T(8,128)} %squeeze.96) | copy-start | bytes 49156
  85.3 115.5 %copy-start.21 = (f32[64,64]{1,0:T(8,128)S(1)}, f32[64,64]{1,0:T(8,128)}, u32[]{:S(2)}) copy-start(f32[64,64]{1,0:T(8,128)} %squeeze.95) | copy-start | bytes 49156
  85.3 124.8 %copy-start.20 = (f32[64,64]{1,0:T(8,128)S(1)}, f32[64,64]{1,0:T(8,128)}, u32[]{:S(2)}) copy-start(f32[64,64]{1,0:T(8,128)} %squeeze.94) | copy-start | bytes 49156
  85.3 133.5 %copy-start.19 = (f32[64,64]{1,0:T(8,128)S(1)}, f32[64,64]{1,0:T(8,128)}, u32[]{:S(2)}) copy-start(f32[64,64]{1,0:T(8,128)} %squeeze.93) | copy-start | bytes 49156
  85.3 144.6 %copy-start.17 = (f32[64,64]{1,0:T(8,128)S(1)}, f32[64,64]{1,0:T(8,128)}, u32[]{:S(2)}) copy-start(f32[64,64]{1,0:T(8,128)} %squeeze.92) | copy-start | bytes 49156
  85.3 145.3 %copy-start.11 = (f32[16,1024]{1,0:T(8,128)S(1)}, f32[16,1024]{1,0:T(8,128)}, u32[]{:S(2)}) copy-start(f32[16,1024]{1,0:T(8,128)} %copy-done.10) | copy-start | bytes 196612
  85.3 145.3 %copy-start.28 = (f32[8,1024]{1,0:T(8,128)S(1)}, f32[8,1024]{1,0:T(8,128)}, u32[]{:S(2)}) copy-start(f32[8,1024]{1,0:T(8,128)} %copy-done.27) | copy-start | bytes 98308
  85.3 145.3 %copy-start.33 = (f32[2,1024]{1,0:T(2,128)S(1)}, f32[2,1024]{1,0:T(2,128)}, u32[]{:S(2)}) copy-start(f32[2,1024]{1,0:T(2,128)} %copy-done.32) | copy-start | bytes 24580
  88.1 5.5 %collective-permute-start.1 = (f32[16,128]{1,0:T(8,128)S(1)}, f32[16,128]{1,0:T(8,128)S(1)}, u32[]{:S(2)}, u32[]{:S(2)}) collective-permute-start(f32[16,128]{1,0:T(8,128)S(1)} %pad_maximum_fusion.2), channel_id=1, source_target_pairs={{2,0},{3,1},{4,2},{5,3},{6,4},{7,5},{8,6},{9,7},{10,8},{11,9},{12,... | collective-permute-start | bytes 24584 | tf_op jit(solution)/shard_map/ppermute | solution.py:25
  95.6 7.0 %collective-permute-start.2 = (f32[16,128]{1,0:T(8,128)S(1)}, f32[16,128]{1,0:T(8,128)S(1)}, u32[]{:S(2)}, u32[]{:S(2)}) collective-permute-start(f32[16,128]{1,0:T(8,128)S(1)} %pad_maximum_fusion.3), channel_id=1, source_target_pairs={{4,0},{5,1},{6,2},{7,3},{8,4},{9,5},{10,6},{11,7},{12,8},{13,9},{1... | collective-permute-start | bytes 24584 | tf_op jit(solution)/shard_map/ppermute | solution.py:25
  104.6 5.5 %collective-permute-start.3 = (f32[16,128]{1,0:T(8,128)S(1)}, f32[16,128]{1,0:T(8,128)S(1)}, u32[]{:S(2)}, u32[]{:S(2)}) collective-permute-start(f32[16,128]{1,0:T(8,128)S(1)} %pad_maximum_fusion.4), channel_id=1, source_target_pairs={{8,0},{9,1},{10,2},{11,3},{12,4},{13,5},{14,6},{15,7},{16,8},{17,9... | collective-permute-start | bytes 24584 | tf_op jit(solution)/shard_map/ppermute | solution.py:25
  112.1 6.4 %collective-permute-start.4 = (f32[16,128]{1,0:T(8,128)S(1)}, f32[16,128]{1,0:T(8,128)S(1)}, u32[]{:S(2)}, u32[]{:S(2)}) collective-permute-start(f32[16,128]{1,0:T(8,128)S(1)} %pad_maximum_fusion.5), channel_id=1, source_target_pairs={{16,0},{17,1},{18,2},{19,3},{20,4},{21,5},{22,6},{23,7},{24,8},{25... | collective-permute-start | bytes 24584 | tf_op jit(solution)/shard_map/ppermute | solution.py:25
  120.5 9.5 %collective-permute-start.5 = (f32[16,128]{1,0:T(8,128)S(1)}, f32[16,128]{1,0:T(8,128)S(1)}, u32[]{:S(2)}, u32[]{:S(2)}) collective-permute-start(f32[16,128]{1,0:T(8,128)S(1)} %pad_maximum_fusion.6), channel_id=1, source_target_pairs={{32,0},{33,1},{34,2},{35,3},{36,4},{37,5},{38,6},{39,7},{40,8},{41... | collective-permute-start | bytes 24584 | tf_op jit(solution)/shard_map/ppermute | solution.py:25
  131.9 14.3 %collective-permute-start.6 = (f32[16,128]{1,0:T(8,128)S(1)}, f32[16,128]{1,0:T(8,128)S(1)}, u32[]{:S(2)}, u32[]{:S(2)}) collective-permute-start(f32[16,128]{1,0:T(8,128)S(1)} %pad_maximum_fusion.7), channel_id=1, source_target_pairs={{64,0},{65,1},{66,2},{67,3},{68,4},{69,5},{70,6},{71,7},{72,8},{73... | collective-permute-start | bytes 24584 | tf_op jit(solution)/shard_map/ppermute | solution.py:25
  148.1 3.7 %collective-permute-start.7 = (f32[16,128]{1,0:T(8,128)S(1)}, f32[16,128]{1,0:T(8,128)S(1)}, u32[]{:S(2)}, u32[]{:S(2)}) collective-permute-start(f32[16,128]{1,0:T(8,128)S(1)} %pad_maximum_fusion.8), channel_id=1, source_target_pairs={{128,0},{129,1},{130,2},{131,3},{132,4},{133,5},{134,6},{135,7},{1... | collective-permute-start | bytes 24584 | tf_op jit(solution)/shard_map/ppermute | solution.py:25
  153.8 6.0 %collective-permute-start.9 = (f32[16,128]{1,0:T(8,128)S(1)}, f32[16,128]{1,0:T(8,128)S(1)}, u32[]{:S(2)}, u32[]{:S(2)}) collective-permute-start(f32[16,128]{1,0:T(8,128)S(1)} %pad_maximum_fusion.9), channel_id=1, source_target_pairs={{256,0},{257,1},{258,2},{259,3},{260,4},{261,5},{262,6},{263,7},{2... | collective-permute-start | bytes 24584 | tf_op jit(solution)/shard_map/ppermute | solution.py:25
  159.8 7.0 %collective-permute-start.8 = (f32[16,128]{1,0:T(8,128)S(1)}, f32[16,128]{1,0:T(8,128)S(1)}, u32[]{:S(2)}, u32[]{:S(2)}) collective-permute-start(f32[16,128]{1,0:T(8,128)S(1)} %concatenate.72), channel_id=1, source_target_pairs={{0,256},{1,257},{2,258},{3,259},{4,260},{5,261},{6,262},{7,263},{8... | collective-permute-start | bytes 24584 | tf_op jit(solution)/shard_map/ppermute | solution.py:25
  167.1 5.5 %collective-permute-start.10 = (f32[16,128]{1,0:T(8,128)S(1)}, f32[16,128]{1,0:T(8,128)S(1)}, u32[]{:S(2)}, u32[]{:S(2)}) collective-permute-start(f32[16,128]{1,0:T(8,128)S(1)} %pad_maximum_fusion.10), channel_id=1, source_target_pairs={{0,128},{1,129},{2,130},{3,131},{4,132},{5,133},{6,134},{7,135},{8... | collective-permute-start | bytes 24584 | tf_op jit(solution)/shard_map/ppermute | solution.py:25
  172.9 15.2 %collective-permute-start.11 = (f32[16,128]{1,0:T(8,128)S(1)}, f32[16,128]{1,0:T(8,128)S(1)}, u32[]{:S(2)}, u32[]{:S(2)}) collective-permute-start(f32[16,128]{1,0:T(8,128)S(1)} %pad_maximum_fusion.11), channel_id=1, source_target_pairs={{0,64},{1,65},{2,66},{3,67},{4,68},{5,69},{6,70},{7,71},{8,72},{9,... | collective-permute-start | bytes 24584 | tf_op jit(solution)/shard_map/ppermute | solution.py:25
  188.3 10.3 %collective-permute-start.12 = (f32[16,128]{1,0:T(8,128)S(1)}, f32[16,128]{1,0:T(8,128)S(1)}, u32[]{:S(2)}, u32[]{:S(2)}) collective-permute-start(f32[16,128]{1,0:T(8,128)S(1)} %pad_maximum_fusion.12), channel_id=1, source_target_pairs={{0,32},{1,33},{2,34},{3,35},{4,36},{5,37},{6,38},{7,39},{8,40},{9,... | collective-permute-start | bytes 24584 | tf_op jit(solution)/shard_map/ppermute | solution.py:25
  198.9 8.6 %collective-permute-start.13 = (f32[16,128]{1,0:T(8,128)S(1)}, f32[16,128]{1,0:T(8,128)S(1)}, u32[]{:S(2)}, u32[]{:S(2)}) collective-permute-start(f32[16,128]{1,0:T(8,128)S(1)} %pad_maximum_fusion.13), channel_id=1, source_target_pairs={{0,16},{1,17},{2,18},{3,19},{4,20},{5,21},{6,22},{7,23},{8,24},{9,... | collective-permute-start | bytes 24584 | tf_op jit(solution)/shard_map/ppermute | solution.py:25
  207.7 7.7 %collective-permute-start.14 = (f32[16,128]{1,0:T(8,128)S(1)}, f32[16,128]{1,0:T(8,128)S(1)}, u32[]{:S(2)}, u32[]{:S(2)}) collective-permute-start(f32[16,128]{1,0:T(8,128)S(1)} %pad_maximum_fusion.14), channel_id=1, source_target_pairs={{0,8},{1,9},{2,10},{3,11},{4,12},{5,13},{6,14},{7,15},{8,16},{9,17... | collective-permute-start | bytes 24584 | tf_op jit(solution)/shard_map/ppermute | solution.py:25
  215.6 10.1 %collective-permute-start.15 = (f32[16,128]{1,0:T(8,128)S(1)}, f32[16,128]{1,0:T(8,128)S(1)}, u32[]{:S(2)}, u32[]{:S(2)}) collective-permute-start(f32[16,128]{1,0:T(8,128)S(1)} %pad_maximum_fusion.15), channel_id=1, source_target_pairs={{0,4},{1,5},{2,6},{3,7},{4,8},{5,9},{6,10},{7,11},{8,12},{9,13},{1... | collective-permute-start | bytes 24584 | tf_op jit(solution)/shard_map/ppermute | solution.py:25
  226.5 21.9 %collective-permute-start.16 = (f32[16,128]{1,0:T(8,128)}, f32[16,128]{1,0:T(8,128)}, u32[]{:S(2)}, u32[]{:S(2)}) collective-permute-start(f32[16,128]{1,0:T(8,128)} %pad_maximum_fusion.16), channel_id=1, source_target_pairs={{0,2},{1,3},{2,4},{3,5},{4,6},{5,7},{6,8},{7,9},{8,10},{9,11},{10,... | collective-permute-start | bytes 24584 | tf_op jit(solution)/shard_map/ppermute | solution.py:25
  235.7 5.0 %copy-start.7 = (f32[4,3,64,64]{3,2,0,1:T(8,128)S(1)}, f32[4,3,64,64]{3,2,0,1:T(8,128)}, u32[]{:S(2)}) copy-start(f32[4,3,64,64]{3,2,0,1:T(8,128)} %reshape.220) | copy-start | bytes 589828
  235.7 5.0 %copy-start.43 = (f32[4,3]{1,0:T(4,128)S(1)}, f32[4,3]{1,0:T(4,128)}, u32[]{:S(2)}) copy-start(f32[4,3]{1,0:T(4,128)} %fusion.95) | copy-start | bytes 148
  237.3 5.5 %copy-start.35 = (f32[16,3]{1,0:T(8,128)S(1)}, f32[16,3]{1,0:T(8,128)}, u32[]{:S(2)}) copy-start(f32[16,3]{1,0:T(8,128)} %fusion.69) | copy-start | bytes 580
  240.7 5.9 %copy-start.8 = (f32[2,3,64,64]{3,2,0,1:T(8,128)S(1)}, f32[2,3,64,64]{3,2,0,1:T(8,128)}, u32[]{:S(2)}) copy-start(f32[2,3,64,64]{3,2,0,1:T(8,128)} %reshape.217) | copy-start | bytes 294916
  240.7 5.9 %copy-start.29 = (f32[2,3,16,64]{3,2,1,0:T(8,128)S(1)}, f32[2,3,16,64]{3,2,1,0:T(8,128)}, u32[]{:S(2)}) copy-start(f32[2,3,16,64]{3,2,1,0:T(8,128)} %reshape.216) | copy-start | bytes 73732
  240.7 5.9 %copy-start.44 = (f32[2,3]{1,0:T(2,128)S(1)}, f32[2,3]{1,0:T(2,128)}, u32[]{:S(2)}) copy-start(f32[2,3]{1,0:T(2,128)} %compare_convert_fusion) | copy-start | bytes 76
  242.8 5.6 %copy-start.18 = (f32[64,64]{1,0:T(8,128)S(1)}, f32[64,64]{1,0:T(8,128)}, u32[]{:S(2)}) copy-start(f32[64,64]{1,0:T(8,128)} %squeeze.92) | copy-start | bytes 49156
  242.8 5.6 %copy-start.37 = (f32[16,64]{1,0:T(8,128)S(1)}, f32[16,64]{1,0:T(8,128)}, u32[]{:S(2)}) copy-start(f32[16,64]{1,0:T(8,128)} %convolution_add_fusion.6) | copy-start | bytes 12292
  242.8 6.6 %copy-start.39 = (f32[16,64]{1,0:T(8,128)S(1)}, f32[16,64]{1,0:T(8,128)}, u32[]{:S(2)}) copy-start(f32[16,64]{1,0:T(8,128)} %fusion.33) | copy-start | bytes 12292
  242.8 9.2 %copy-start.16 = (f32[64,64]{1,0:T(8,128)S(1)}, f32[64,64]{1,0:T(8,128)}, u32[]{:S(2)}) copy-start(f32[64,64]{1,0:T(8,128)} %copy-done.15) | copy-start | bytes 49156
  242.9 9.2 %copy-start.40 = (f32[16,64]{1,0:T(8,128)S(1)}, f32[16,64]{1,0:T(8,128)}, u32[]{:S(2)}) copy-start(f32[16,64]{1,0:T(8,128)} %fusion.32) | copy-start | bytes 12292
  250.1 9.5 %collective-permute-start.17 = (f32[16,128]{1,0:T(8,128)}, f32[16,128]{1,0:T(8,128)}, u32[]{:S(2)}, u32[]{:S(2)}) collective-permute-start(f32[16,128]{1,0:T(8,128)} %pad_maximum_fusion.17), channel_id=1, source_target_pairs={{0,1},{1,2},{2,3},{3,4},{4,5},{5,6},{6,7},{7,8},{8,9},{9,10},{10,1... | collective-permute-start | bytes 24584 | tf_op jit(solution)/shard_map/ppermute | solution.py:25
  253.9 6.7 %copy-start.13 = (f32[2,64,64]{2,1,0:T(8,128)S(1)}, f32[2,64,64]{2,1,0:T(8,128)}, u32[]{:S(2)}) copy-start(f32[2,64,64]{2,1,0:T(8,128)} %copy-done.12) | copy-start | bytes 98308
  253.9 6.9 %copy-start.31 = (f32[4,16,64]{2,1,0:T(8,128)S(1)}, f32[4,16,64]{2,1,0:T(8,128)}, u32[]{:S(2)}) copy-start(f32[4,16,64]{2,1,0:T(8,128)} %convolution_bitcast_fusion.2) | copy-start | bytes 49156
  254.7 6.4 %copy-start.4 = (f32[8,64,64]{2,1,0:T(8,128)S(1)}, f32[8,64,64]{2,1,0:T(8,128)}, u32[]{:S(2)}) copy-start(f32[8,64,64]{2,1,0:T(8,128)} %copy-done.3) | copy-start | bytes 393220
  254.8 6.9 %copy-start.1 = (f32[8,3,64,64]{3,2,0,1:T(8,128)S(1)}, f32[8,3,64,64]{3,2,0,1:T(8,128)}, u32[]{:S(2)}) copy-start(f32[8,3,64,64]{3,2,0,1:T(8,128)} %reshape.223) | copy-start | bytes 1179652
  254.8 6.9 %copy-start.9 = (f32[8,3,16,64]{3,2,1,0:T(8,128)S(1)}, f32[8,3,16,64]{3,2,1,0:T(8,128)}, u32[]{:S(2)}) copy-start(f32[8,3,16,64]{3,2,1,0:T(8,128)} %reshape.222) | copy-start | bytes 294916
  254.8 6.9 %copy-start.41 = (f32[8,3]{1,0:T(8,128)S(1)}, f32[8,3]{1,0:T(8,128)}, u32[]{:S(2)}) copy-start(f32[8,3]{1,0:T(8,128)} %fusion.73) | copy-start | bytes 292
  257.5 5.1 %copy-start.14 = (f32[16,16,64]{2,1,0:T(8,128)S(1)}, f32[16,16,64]{2,1,0:T(8,128)}, u32[]{:S(2)}) copy-start(f32[16,16,64]{2,1,0:T(8,128)} %fusion.3) | copy-start | bytes 196612
  257.5 6.0 %copy-start.6 = (f32[16,64,128]{2,1,0:T(8,128)S(1)}, f32[16,64,128]{2,1,0:T(8,128)}, u32[]{:S(2)}) copy-start(f32[16,64,128]{2,1,0:T(8,128)} %param.12) | copy-start | bytes 1572868
  (5 other events, 16.3 us)
where the time goes:
time: 269 us; the launch traced here: 265 us
  starting transfers between devices  85.2 us (32%)
  waiting for transfers between devices  61.6 us (23%)
  local copies, waits for them, and re-layouts  49.8 us (19%)
  matrix products  45.2 us (17%)
  other arithmetic  22.1 us (8%)
    ppermute x18, waiting for transfers between devices, shifted(): return lax.ppermute(shard, axis, pairs)  61.6 us
    ppermute x18, starting transfers between devices, shifted(): return lax.ppermute(shard, axis, pairs)  60.3 us
    ppermute x2, starting transfers between devices, with_halo(): lax.ppermute(lax.slice_in_dim(block, 0, width, axis=dim), axis, backward)  21.1 us
    squeeze x8, local copies, waits for them, and re-layouts, on_device(): carried = jnp.dot(window, top_steps[level - 1], precision=HIGH_ACCURACY)  9.87 us
    dot_general x9, matrix products, on_device(): jnp.dot(arrived[:, :basis_rank], siblings[level - 1, 0], precision=HIGH_A...  8.67 us
    dot_general x9, matrix products, on_device(): jnp.dot(window, siblings[level - 1, 1], precision=HIGH_ACCURACY)  7.89 us
    reshape x4, local copies, waits for them, and re-layouts, on_device(): far_coupling[offset:offset + clusters]  7.64 us
    dot_general x9, matrix products, on_device(): carried = jnp.dot(window, top_steps[level - 1], precision=HIGH_ACCURACY)  7.36 us
  transfers between devices with their start and end apart: 22, of which 16 were waited for; matrix products, arithmetic and copies ran while one was open for 40% of the time, Pallas kernels for 0%

commit v1 on v0

v1 whole, which is shorter than its diff:
```python
import jax
import jax.numpy as jnp
from jax import lax
from jax.experimental import pallas as pl
from jax.experimental.pallas import tpu as pltpu
from jax.sharding import PartitionSpec as P

F32 = jnp.float32
BF16 = jnp.bfloat16
RANK = 64
LEAVES = 16
POINTS = 128
LOCAL = 30
SLOTS = 3
NEAR = 2
REACH = 8
GROUP_BITS = 4
TOP_BITS = 9
GROUP = 1 << GROUP_BITS
GROUPS = 1 << (TOP_BITS - GROUP_BITS)
LAYOUT = ((16, 0), (8, 16), (4, 24), (2, 28))
VMEM_BYTES = 48 * 1024 * 1024


def split(x):
    high = x.astype(BF16)
    return high, (x - high.astype(F32)).astype(BF16)


def lanes(rows):
    return lax.broadcasted_iota(jnp.int32, (rows, 128), 1)


def table_form(table):
    high, low = split(table)
    return jnp.concatenate([high, low, high, low], axis=0)


def coef_form(packed):
    lane = lanes(8)
    even = 2 * (lane % 32)
    parts = [
        jnp.take_along_axis(packed, even + shift, axis=1) for shift in (0, 64, 1, 65)
    ]
    full = jnp.concatenate(parts, axis=0)
    high, low = split(full)
    return jnp.where(lanes(32) < 64, high.astype(F32), low.astype(F32)).astype(BF16)


def dot(a, b):
    return lax.dot_general(a, b, (((1,), (0,)), ((), ())), preferred_element_type=F32)


def dot_t(a, b):
    return lax.dot_general(a, b, (((1,), (1,)), ((), ())), preferred_element_type=F32)


def fold(out):
    left = lanes(8) < 64
    straight = jnp.where(left, out[0:8], out[24:32])
    crossed = jnp.where(left, out[8:16], out[16:24])
    return straight + pltpu.roll(crossed, 64, 1)


def times(packed, table):
    return fold(dot(coef_form(packed), table_form(table)))


def row_form(packed):
    left = lanes(8) < 64
    turned = pltpu.roll(packed, 64, 1)
    zero = jnp.zeros_like(packed)
    full = jnp.concatenate(
        [
            jnp.where(left, packed, zero),
            jnp.where(left, turned, zero),
            jnp.where(left, zero, turned),
            jnp.where(left, zero, packed),
        ],
        axis=0,
    )
    return split(full)


def weave(even_odd):
    lane = lanes(8)
    place = (lane % 64) // 2
    wide = jnp.concatenate([even_odd] * 4, axis=1)
    pick = [jnp.take_along_axis(wide[8 * k : 8 * k + 8], place, axis=1) for k in range(4)]
    even = lane % 2 == 0
    return jnp.where(
        lane < 64, jnp.where(even, pick[0], pick[2]), jnp.where(even, pick[1], pick[3])
    )


def times_t_raw(rows, high, low):
    row_high, row_low = rows
    both = dot_t(jnp.concatenate([row_high, row_low], axis=0), high)
    return both[:32] + both[32:] + dot_t(row_high, low)


def times_t(packed, table):
    high, low = split(table)
    return weave(times_t_raw(row_form(packed), high, low))


def unpack(packed):
    return jnp.concatenate([packed[:, :RANK], packed[:, RANK:]], axis=0)


def pack(value):
    return jnp.concatenate([value[:8], value[8:]], axis=1)


def up_kernel(sources, basis, transfer, coefs, root, tables):
    table = transfer[...].reshape(LOCAL, 32, 128)
    for row in range(LOCAL):
        high, low = split(table[row])
        tables[row, 0:32] = high
        tables[row, 32:64] = low
    for leaf in range(LEAVES):
        high, low = split(sources[:, leaf * POINTS : (leaf + 1) * POINTS])
        basis_high, basis_low = split(basis[leaf])
        both = dot_t(jnp.concatenate([high, low], axis=0), basis_high)
        coefs[leaf] = pack(both[:16] + both[16:] + dot_t(high, basis_low))
    for level, (clusters, offset) in enumerate(LAYOUT):
        for parent in range(clusters // 2):
            first = offset + 2 * parent
            left = jnp.concatenate(
                [coef_form(coefs[first]), coef_form(coefs[first + 1])], axis=1
            )
            halves = [tables[first], tables[first], tables[first + 1], tables[first + 1]]
            value = fold(dot(left, jnp.concatenate(halves, axis=0)))
            if clusters > 2:
                coefs[offset + clusters + parent] = value
            else:
                root[...] = value


def near_kernel(partner, count, device, own, low, high, block, out, leaves):
    for leaf in range(LEAVES):
        leaves[REACH + leaf] = own[:, leaf * POINTS : (leaf + 1) * POINTS]
    for leaf in range(REACH):
        leaves[leaf] = low[:, leaf * POINTS : (leaf + 1) * POINTS]
        leaves[REACH + LEAVES + leaf] = high[:, leaf * POINTS : (leaf + 1) * POINTS]
    first = device[0] * LEAVES - REACH
    for leaf in range(LEAVES):
        total = None
        for slot in range(NEAR):
            place = jnp.clip(partner[leaf, slot] - first, 0, LEAVES + 2 * REACH - 1)
            used = (slot < count[leaf]).astype(F32)
            picked_high, picked_low = split(leaves[place] * used)
            block_high, block_low = split(block[leaf, slot])
            both = dot_t(jnp.concatenate([picked_high, picked_low], axis=0), block_high)
            value = both[:16] + both[16:] + dot_t(picked_high, block_low)
            total = value if total is None else total + value
        out[:, leaf * POINTS : (leaf + 1) * POINTS] = total


def far_kernel(partner, count, device, own, low, high, coupling, out, extended):
    extended[0:LOCAL] = low[...]
    extended[LOCAL : 2 * LOCAL] = own[...]
    extended[2 * LOCAL : 3 * LOCAL] = high[...]
    tables = [coupling[slot].reshape(LOCAL, 32, 128) for slot in range(SLOTS)]
    for clusters, offset in LAYOUT:
        for cluster in range(clusters):
            row = offset + cluster
            left = []
            right = []
            for slot in range(SLOTS):
                index = partner[row, slot]
                side = jnp.clip(index // clusters - device[0] + 1, 0, 2)
                place = side * LOCAL + offset + index % clusters
                used = (slot < count[row]).astype(F32)
                left.append(coef_form(extended[place] * used))
                right.append(table_form(tables[slot][row]))
            out[row] = fold(dot(jnp.concatenate(left, axis=1), jnp.concatenate(right, axis=0)))


def share_kernel(member, root, own, table, blocks, chain):
    value = root[...]
    chain[0] = value
    for level in range(GROUP_BITS):
        value = times(value, own[...] if level == 0 else table[level - 1])
        if level + 1 < GROUP_BITS:
            chain[level + 1] = value
    for other in range(GROUP):
        apart = member[0] ^ other
        level = sum((apart >= (1 << bit)).astype(jnp.int32) for bit in range(1, GROUP_BITS))
        blocks[other, 0:8] = chain[level]
        blocks[other, 8:16] = value


def rise_kernel(position, arrived, own, table, sibling, blocks, chain):
    member = position[0]
    for level in range(GROUP_BITS):
        total = None
        for apart in range(1 << level, 2 << level):
            value = arrived[member ^ apart, 0:8]
            total = value if total is None else total + value
        sibling[level] = total
    value = arrived[0, 8:16]
    for other in range(1, GROUP):
        value = value + arrived[other, 8:16]
    steps = TOP_BITS - GROUP_BITS
    chain[0] = value
    for level in range(steps - 1):
        value = times(value, own[...] if level == 0 else table[level - 1])
        chain[level + 1] = value
    for other in range(GROUPS):
        apart = position[1] ^ other
        level = sum((apart >= (1 << bit)).astype(jnp.int32) for bit in range(1, steps))
        blocks[other] = chain[level]


def turn_kernel(position, arrived, own, table, out):
    steps = TOP_BITS - GROUP_BITS
    group = position[1]
    value = None
    terms = []
    for level in range(steps):
        total = None
        for apart in range(1 << level, 2 << level):
            piece = arrived[group ^ apart]
            total = piece if total is None else total + piece
        terms.append(times(total, table[steps - 2 + steps - 1 - level]))
    value = terms[steps - 1]
    for level in range(steps - 2, -1, -1):
        value = times_t(value, own[...] if level == 0 else table[level - 1]) + terms[level]
    for other in range(GROUP):
        out[other] = value


def down_kernel(arrived, sibling, own, table, tables, far, basis, near, out, fields):
    value = arrived[0]
    terms = [
        times(sibling[level], table[GROUP_BITS - 1 + GROUP_BITS - 1 - level])
        for level in range(GROUP_BITS)
    ]
    for level in range(GROUP_BITS - 1, -1, -1):
        value = times_t(value, own[...] if level == 0 else table[level - 1]) + terms[level]
    parents = [value]
    for clusters, offset in reversed(LAYOUT):
        following = []
        for parent in range(clusters // 2):
            first = offset + 2 * parent
            high = jnp.concatenate([tables[first, 0:32], tables[first + 1, 0:32]], axis=0)
            low = jnp.concatenate([tables[first, 32:64], tables[first + 1, 32:64]], axis=0)
            raw = times_t_raw(row_form(parents[parent]), high, low)
            following.append(weave(raw[:, 0:32]) + far[first])
            following.append(weave(raw[:, 32:64]) + far[first + 1])
        parents = following
    for leaf in range(LEAVES):
        high, low = split(unpack(parents[leaf]))
        basis_high, basis_low = split(basis[leaf])
        both = dot(jnp.concatenate([high, low], axis=0), basis_high)
        place = slice(leaf * POINTS, (leaf + 1) * POINTS)
        out[:, place] = both[:16] + both[16:] + dot(high, basis_low) + near[:, place]


def call(kernel, name, outs, args, scalars=0, scratch=()):
    vmem = pl.BlockSpec(memory_space=pltpu.VMEM)
    smem = pl.BlockSpec(memory_space=pltpu.SMEM)
    single = not isinstance(outs, list)
    result = pl.pallas_call(
        kernel,
        out_shape=outs,
        in_specs=[smem] * scalars + [vmem] * (len(args) - scalars),
        out_specs=vmem if single else [vmem] * len(outs),
        scratch_shapes=list(scratch),
        compiler_params=pltpu.CompilerParams(vmem_limit_bytes=VMEM_BYTES),
        name=name,
    )(*args)
    return result


def shape(*dims, dtype=F32):
    return jax.ShapeDtypeStruct(dims, dtype)


def permute(value, pairs):
    return lax.ppermute(value, "leaf", pairs)


def hand_down(table, other, device, bit, low, high):
    count = lax.axis_size("leaf")
    pairs = [(i, i + (1 << bit)) for i in range(0, count, 2 << bit)]
    payload = jnp.concatenate([table[low : high - 1], other[None]], axis=0)
    arrived = permute(payload, pairs)
    right = (device >> bit) & 1 == 1
    merged = jnp.where(right, arrived, table[low:high])
    return jnp.concatenate([table[:low], merged, table[high:]], axis=0)


def on_device(
    sources,
    leaf_cluster_basis,
    local_transfer,
    far_coupling,
    far_partner,
    far_count,
    top_transfer,
    top_coupling,
    near_block,
    near_partner,
    near_count,
):
    count = lax.axis_size("leaf")
    device = lax.axis_index("leaf").astype(jnp.int32)
    member = device % GROUP
    group = device // GROUP
    index = device.reshape(1)
    position = jnp.stack([member, group])
    forward = [(i, i + 1) for i in range(count - 1)]
    backward = [(i + 1, i) for i in range(count - 1)]

    reach = REACH * POINTS
    source_low = permute(sources[:, -reach:], forward)
    source_high = permute(sources[:, :reach], backward)

    transfers = top_transfer.reshape(TOP_BITS, 32, 128)
    couplings = top_coupling.reshape(TOP_BITS, 2, 32, 128)
    left = couplings[:, 0]
    right = couplings[:, 1]
    own_low = transfers[0]
    own_high = transfers[GROUP_BITS]
    group_table = jnp.concatenate(
        [transfers[1:GROUP_BITS], left[:GROUP_BITS][::-1]], axis=0
    )
    top_table = jnp.concatenate(
        [transfers[GROUP_BITS + 1 : TOP_BITS - 1], left[GROUP_BITS:][::-1]], axis=0
    )

    coefs, root, tables = call(
        up_kernel,
        "upward",
        [shape(LOCAL, 8, 128), shape(8, 128), shape(LOCAL, 64, 128, dtype=BF16)],
        [sources, leaf_cluster_basis, local_transfer],
    )
    coef_low = permute(coefs, forward)
    coef_high = permute(coefs, backward)

    for bit in range(TOP_BITS - 1, GROUP_BITS - 1, -1):
        low = bit - GROUP_BITS
        high = TOP_BITS - GROUP_BITS - 2 + TOP_BITS - bit
        low = min(low, TOP_BITS - GROUP_BITS - 2)
        top_table = hand_down(top_table, right[bit], device, bit, low, high)
    for bit in range(GROUP_BITS - 1, -1, -1):
        high = GROUP_BITS - 1 + GROUP_BITS - bit
        group_table = hand_down(group_table, right[bit], device, bit, bit, high)

    near = call(
        near_kernel,
        "near_field",
        shape(16, LEAVES * POINTS),
        [near_partner, near_count, index, sources, source_low, source_high, near_block],
        scalars=3,
        scratch=[pltpu.VMEM((LEAVES + 2 * REACH, 16, POINTS), F32)],
    )
    far = call(
        far_kernel,
        "far_field",
        shape(LOCAL, 8, 128),
        [
            far_partner,
            far_count,
            index,
            coefs,
            coef_low,
            coef_high,
            far_coupling.transpose(1, 0, 2),
        ],
        scalars=3,
        scratch=[pltpu.VMEM((3 * LOCAL, 8, 128), F32)],
    )

    shares = call(
        share_kernel,
        "group_shares",
        shape(GROUP, 16, 128),
        [position, root, own_low, group_table],
        scalars=1,
        scratch=[pltpu.VMEM((GROUP_BITS, 8, 128), F32)],
    )
    in_group = [list(range(first, first + GROUP)) for first in range(0, count, GROUP)]
    across = [list(range(first, count, GROUP)) for first in range(GROUP)]
    arrived = lax.all_to_all(shares, "leaf", 0, 0, axis_index_groups=in_group)
    sibling, rising = call(
        rise_kernel,
        "top_shares",
        [shape(GROUP_BITS, 8, 128), shape(GROUPS, 8, 128)],
        [position, arrived, own_high, top_table],
        scalars=1,
        scratch=[pltpu.VMEM((TOP_BITS - GROUP_BITS, 8, 128), F32)],
    )
    arrived = lax.all_to_all(rising, "leaf", 0, 0, axis_index_groups=across)
    turned = call(
        turn_kernel,
        "top_turn",
        shape(GROUP, 8, 128),
        [position, arrived, own_high, top_table],
        scalars=1,
    )
    arrived = lax.all_to_all(turned, "leaf", 0, 0, axis_index_groups=in_group)
    return call(
        down_kernel,
        "downward",
        shape(16, LEAVES * POINTS),
        [arrived, sibling, own_low, group_table, tables, far, leaf_cluster_basis, near],
        scratch=[pltpu.VMEM((LOCAL, 8, 128), F32)],
    )


def solution(mesh):
    placed = (
        P(None, "leaf"),
        P("leaf", None, None),
        P("leaf", None),
        P("leaf", None, None),
        P("leaf", None),
        P("leaf"),
        P("leaf", None, None),
        P("leaf", None, None, None),
        P("leaf", None, None, None),
        P("leaf", None),
        P("leaf"),
    )
    return jax.shard_map(
        on_device, mesh=mesh, in_specs=placed, out_specs=P(None, "leaf"), check_vma=False
    )
```

time: 269 us -> 115 us (0.43)
  the two profiles are of different devices: /device:TPU:24 before, /device:TPU:8 now
where the time goes in v1:
time: 115 us; the launch traced here: 114 us
  starting transfers between devices  60 us (52%)
  waiting for transfers between devices  22 us (19%)
  Pallas kernels  17.5 us (15%)
  local copies, waits for them, and re-layouts  12.7 us (11%)
  other arithmetic  1.68 us (1%)
    ppermute x13, starting transfers between devices, permute(): return lax.ppermute(value, 'leaf', pairs)  39.1 us
    pallas_call x7, Pallas kernels, call(): pl.pallas_call(kernel, out_shape=outs, in_specs=[smem] * scalars + [vmem]...  17.5 us
    all_to_all x1, starting transfers between devices, on_device(): arrived = lax.all_to_all(rising, 'leaf', 0, 0, axis_index_groups=across)  14 us
    ppermute x13, waiting for transfers between devices, permute(): return lax.ppermute(value, 'leaf', pairs)  9.98 us
    all_to_all x1, waiting for transfers between devices, on_device(): arrived = lax.all_to_all(rising, 'leaf', 0, 0, axis_index_groups=across)  9.21 us
    unnamed x40, local copies, waits for them, and re-layouts  8.3 us
    all_to_all x1, starting transfers between devices, on_device(): arrived = lax.all_to_all(shares, 'leaf', 0, 0, axis_index_groups=in_group)  3.51 us
    all_to_all x1, starting transfers between devices, on_device(): arrived = lax.all_to_all(turned, 'leaf', 0, 0, axis_index_groups=in_group)  3.5 us
  transfers between devices with their start and end apart: 16, of which 6 were waited for; matrix products, arithmetic and copies ran while one was open for 6% of the time, Pallas kernels for 10%

profile of v1, /device:TPU:8, one launch (start us, length us, event | category | flops | bytes accessed | tf_op | source)
XLA Modules:
  0.0 114.3 jit_solution(11284751706153707793)
XLA Ops:
  0.0 1.3 %reshape.37 = f32[9,2,32,128]{3,2,1,0:T(8,128)S(1)} reshape(f32[1,9,2,4096]{3,2,1,0:T(2,128)} %param.18) | data formatting | bytes 589824 | tf_op jit(solution)/shard_map/reshape | solution.py:322
  1.3 0.6 slice_bitcast_fusion.5
  1.9 3.8 %collective-permute-start = (f32[1,32,128]{2,1,0:T(8,128)S(1)}, f32[1,32,128]{2,1,0:T(8,128)S(1)}, u32[]{:S(2)}, u32[]{:S(2)}) collective-permute-start(f32[1,32,128]{2,1,0:T(8,128)S(1)} %get-tuple-element.25), channel_id=1, source_target_pairs={{0,8},{16,24},{32,40},{48,56},{64,72},{80,88},{96,104},{112,120},{... | collective-permute-start | bytes 49160 | tf_op jit(solution)/shard_map/ppermute | solution.py:282
  5.8 0.7 collective-permute-start.4
  6.5 0.8 fusion.9
  7.3 0.8 fusion.8
  8.1 0.8 fusion.7
  8.9 0.1 pad_add_fusion.member.position
  9.0 0.0 copy-done.3
  9.1 2.0 %upward.1 = (f32[30,8,128]{2,1,0:T(8,128)}, f32[8,128]{1,0:T(8,128)S(1)}, bf16[30,64,128]{2,1,0:T(8,128)(2,1)S(1)}) custom-call(f32[16,2048]{1,0:T(8,128)S(1)} %copy-done.3, f32[16,64,128]{2,1,0:T(8,128)S(1)} %copy-done, f32[30,4096]{1,0:T(8,128)S(1)} %copy-done.4), custom_call_target="tpu_custom_call" | custom-call | tf_op jit(solution)/shard_map/upward/pallas_call | solution.py:265
  11.0 0.0 collective-permute-done
  11.0 0.0 collective-permute-done.4
  11.1 1.3 %collective-permute-start.5 = (f32[2,32,128]{2,1,0:T(8,128)S(1)}, f32[2,32,128]{2,1,0:T(8,128)S(1)}, u32[]{:S(2)}, u32[]{:S(2)}) collective-permute-start(f32[2,32,128]{2,1,0:T(8,128)S(1)} %pad_maximum_fusion.17), channel_id=1, source_target_pairs={{0,128},{256,384}} | collective-permute-start | bytes 98312 | tf_op jit(solution)/shard_map/ppermute | solution.py:282
  12.4 1.3 %collective-permute-start.1 = (f32[3,32,128]{2,1,0:T(8,128)S(1)}, f32[3,32,128]{2,1,0:T(8,128)S(1)}, u32[]{:S(2)}, u32[]{:S(2)}) collective-permute-start(f32[3,32,128]{2,1,0:T(8,128)S(1)} %pad_maximum_fusion.15), channel_id=1, source_target_pairs={{0,4},{8,12},{16,20},{24,28},{32,36},{40,44},{48,52},{56,60},{64,6... | collective-permute-start | bytes 147464 | tf_op jit(solution)/shard_map/ppermute | solution.py:282
  13.7 5.4 %collective-permute-done.5 = f32[2,32,128]{2,1,0:T(8,128)S(1)} collective-permute-done((f32[2,32,128]{2,1,0:T(8,128)S(1)}, f32[2,32,128]{2,1,0:T(8,128)S(1)}, u32[]{:S(2)}, u32[]{:S(2)}) %collective-permute-start.5) | collective-permute-done | bytes 32800 | tf_op jit(solution)/shard_map/ppermute | solution.py:282
  19.1 10.2 %collective-permute-start.6 = (f32[4,32,128]{2,1,0:T(8,128)S(1)}, f32[4,32,128]{2,1,0:T(8,128)S(1)}, u32[]{:S(2)}, u32[]{:S(2)}) collective-permute-start(f32[4,32,128]{2,1,0:T(8,128)S(1)} %pad_maximum_fusion.12), channel_id=1, source_target_pairs={{0,64},{128,192},{256,320},{384,448}} | collective-permute-start | bytes 196616 | tf_op jit(solution)/shard_map/ppermute | solution.py:282
  29.3 0.0 collective-permute-done.1
  29.3 0.0 copy-start.1
  29.3 1.4 %collective-permute-start.2 = (f32[5,32,128]{2,1,0:T(8,128)S(1)}, f32[5,32,128]{2,1,0:T(8,128)S(1)}, u32[]{:S(2)}, u32[]{:S(2)}) collective-permute-start(f32[5,32,128]{2,1,0:T(8,128)S(1)} %pad_maximum_fusion.9), channel_id=1, source_target_pairs={{0,2},{4,6},{8,10},{12,14},{16,18},{20,22},{24,26},{28,30},{32,34}... | collective-permute-start | bytes 245768 | tf_op jit(solution)/shard_map/ppermute | solution.py:282
  30.8 0.4 collective-permute-done.6
  31.2 1.6 %collective-permute-done.2 = f32[5,32,128]{2,1,0:T(8,128)S(1)} collective-permute-done((f32[5,32,128]{2,1,0:T(8,128)S(1)}, f32[5,32,128]{2,1,0:T(8,128)S(1)}, u32[]{:S(2)}, u32[]{:S(2)}) %collective-permute-start.2) | collective-permute-done | bytes 81952 | tf_op jit(solution)/shard_map/ppermute | solution.py:282
  32.9 1.3 %collective-permute-start.3 = (f32[7,32,128]{2,1,0:T(8,128)S(1)}, f32[7,32,128]{2,1,0:T(8,128)S(1)}, u32[]{:S(2)}, u32[]{:S(2)}) collective-permute-start(f32[7,32,128]{2,1,0:T(8,128)S(1)} %pad_maximum_fusion.2), channel_id=1, source_target_pairs={{0,1},{2,3},{4,5},{6,7},{8,9},{10,11},{12,13},{14,15},{16,17},{18,... | collective-permute-start | bytes 344072 | tf_op jit(solution)/shard_map/ppermute | solution.py:282
  34.2 0.7 pad_maximum_fusion.6
  34.9 1.9 %collective-permute-start.7 = (f32[6,32,128]{2,1,0:T(8,128)S(1)}, f32[6,32,128]{2,1,0:T(8,128)}, u32[]{:S(2)}, u32[]{:S(2)}) collective-permute-start(f32[6,32,128]{2,1,0:T(8,128)S(1)} %pad_maximum_fusion.6), channel_id=1, source_target_pairs={{0,32},{64,96},{128,160},{192,224},{256,288},{320,352},{384,416},{... | collective-permute-start | bytes 294920 | tf_op jit(solution)/shard_map/ppermute | solution.py:282
  36.8 0.0 collective-permute-done.3
  36.8 0.7 maximum_select_fusion.1.table
  37.6 2.3 %group_shares.1 = f32[16,16,128]{2,1,0:T(8,128)} custom-call(s32[2]{0:T(128)S(1)} %pad_add_fusion.member.position, f32[8,128]{1,0:T(8,128)S(1)} %get-tuple-element.10.root, f32[32,128]{1,0:T(8,128)S(1)} %bitcast.55, f32[7,32,128]{2,1,0:T(8,128)S(1)} %maximum_select_fusion.1.table), custom_call_target="tpu_custom_call" | custom-call | tf_op jit(solution)/shard_map/group_shares/pallas_call | solution.py:265
  39.8 3.5 %all-to-all-start = ((f32[16,16,128]{2,1,0:T(8,128)}), f32[16,16,128]{2,1,0:T(8,128)S(1)}, u32[]{:S(2)}, u32[]{:S(2)}) async-start(f32[16,16,128]{2,1,0:T(8,128)} %group_shares.1), calls=%async_computation | async-start | bytes 262144 | tf_op jit(solution)/shard_map/all_to_all | solution.py:387
  43.3 0.0 collective-permute-done.7
  43.4 1.3 %collective-permute-start.8 = (f32[8,32,128]{2,1,0:T(8,128)S(1)}, f32[8,32,128]{2,1,0:T(8,128)S(1)}, u32[]{:S(2)}, u32[]{:S(2)}) collective-permute-start(f32[8,32,128]{2,1,0:T(8,128)S(1)} %pad_maximum_fusion), channel_id=1, source_target_pairs={{0,16},{32,48},{64,80},{96,112},{128,144},{160,176},{192,208},{224... | collective-permute-start | bytes 393224 | tf_op jit(solution)/shard_map/ppermute | solution.py:282
  44.7 2.5 %collective-permute-done.8 = f32[8,32,128]{2,1,0:T(8,128)S(1)} collective-permute-done((f32[8,32,128]{2,1,0:T(8,128)S(1)}, f32[8,32,128]{2,1,0:T(8,128)S(1)}, u32[]{:S(2)}, u32[]{:S(2)}) %collective-permute-start.8) | collective-permute-done | bytes 131104 | tf_op jit(solution)/shard_map/ppermute | solution.py:282
  47.2 2.8 %all-to-all-done.arrived = f32[16,16,128]{2,1,0:T(8,128)S(1)} async-done(((f32[16,16,128]{2,1,0:T(8,128)}), f32[16,16,128]{2,1,0:T(8,128)S(1)}, u32[]{:S(2)}, u32[]{:S(2)}) %all-to-all-start) | async-done | bytes 131104 | tf_op jit(solution)/shard_map/all_to_all | solution.py:387
  50.0 2.3 %top_shares.1 = (f32[4,8,128]{2,1,0:T(8,128)S(1)}, f32[32,8,128]{2,1,0:T(8,128)}) custom-call(s32[2]{0:T(128)S(1)} %pad_add_fusion.member.position, f32[16,16,128]{2,1,0:T(8,128)S(1)} %all-to-all-done.arrived, f32[32,128]{1,0:T(8,128)S(1)} %bitcast.57, f32[8,32,128]{2,1,0:T(8,128)S(1)} %maximum_select_fusion.table), custom_call_target="tpu_custom_call" | custom-call | tf_op jit(solution)/shard_map/top_shares/pallas_call | solution.py:265
  52.3 0.6 copy-done.15
  52.9 14.0 %all-to-all-start.1 = ((f32[32,8,128]{2,1,0:T(8,128)}), f32[32,8,128]{2,1,0:T(8,128)S(1)}, u32[]{:S(2)}, u32[]{:S(2)}) async-start(f32[32,8,128]{2,1,0:T(8,128)} %get-tuple-element.11), calls=%async_computation.1 | async-start | bytes 262144 | tf_op jit(solution)/shard_map/all_to_all | solution.py:396
  66.9 4.2 %collective-permute-start.10 = (f32[30,8,128]{2,1,0:T(8,128)}, f32[30,8,128]{2,1,0:T(8,128)}, u32[]{:S(2)}, u32[]{:S(2)}) collective-permute-start(f32[30,8,128]{2,1,0:T(8,128)} %get-tuple-element.14.own), channel_id=1, source_target_pairs={{1,0},{2,1},{3,2},{4,3},{5,4},{6,5},{7,6},{8,7},{9,8},{10,9},{11,1... | collective-permute-start | bytes 368648 | tf_op jit(solution)/shard_map/ppermute | solution.py:282
  71.1 1.9 %collective-permute-start.9 = (f32[30,8,128]{2,1,0:T(8,128)}, f32[30,8,128]{2,1,0:T(8,128)}, u32[]{:S(2)}, u32[]{:S(2)}) collective-permute-start(f32[30,8,128]{2,1,0:T(8,128)} %get-tuple-element.14.own), channel_id=1, source_target_pairs={{0,1},{1,2},{2,3},{3,4},{4,5},{5,6},{6,7},{7,8},{8,9},{9,10},{10,1... | collective-permute-start | bytes 368648 | tf_op jit(solution)/shard_map/ppermute | solution.py:282
  73.1 9.2 %all-to-all-done.1.arrived = f32[32,8,128]{2,1,0:T(8,128)S(1)} async-done(((f32[32,8,128]{2,1,0:T(8,128)}), f32[32,8,128]{2,1,0:T(8,128)S(1)}, u32[]{:S(2)}, u32[]{:S(2)}) %all-to-all-start.1) | async-done | bytes 131104 | tf_op jit(solution)/shard_map/all_to_all | solution.py:396
  82.3 2.8 %top_turn.1 = f32[16,8,128]{2,1,0:T(8,128)} custom-call(s32[2]{0:T(128)S(1)} %pad_add_fusion.member.position, f32[32,8,128]{2,1,0:T(8,128)S(1)} %all-to-all-done.1.arrived, f32[32,128]{1,0:T(8,128)S(1)} %bitcast.58, f32[8,32,128]{2,1,0:T(8,128)S(1)} %maximum_select_fusion.table), custom_call_target="tpu_custom_call" | custom-call | tf_op jit(solution)/shard_map/top_turn/pallas_call | solution.py:265
  85.1 3.5 %all-to-all-start.2 = ((f32[16,8,128]{2,1,0:T(8,128)}), f32[16,8,128]{2,1,0:T(8,128)S(1)}, u32[]{:S(2)}, u32[]{:S(2)}) async-start(f32[16,8,128]{2,1,0:T(8,128)} %top_turn.1), calls=%async_computation.2 | async-start | bytes 131072 | tf_op jit(solution)/shard_map/all_to_all | solution.py:404
  88.6 2.2 %collective-permute-start.11 = (f32[16,1024]{1,0:T(8,128)S(1)}, f32[16,1024]{1,0:T(8,128)S(1)}, u32[]{:S(2)}, u32[]{:S(2)}) collective-permute-start(f32[16,1024]{1,0:T(8,128)S(1)} %get-tuple-element.41), channel_id=1, source_target_pairs={{0,1},{1,2},{2,3},{3,4},{4,5},{5,6},{6,7},{7,8},{8,9},{9,10},{10,1... | collective-permute-start | bytes 196616 | tf_op jit(solution)/shard_map/ppermute | solution.py:282
  90.8 7.6 %collective-permute-start.12 = (f32[16,1024]{1,0:T(8,128)S(1)}, f32[16,1024]{1,0:T(8,128)S(1)}, u32[]{:S(2)}, u32[]{:S(2)}) collective-permute-start(f32[16,1024]{1,0:T(8,128)S(1)} %get-tuple-element.40), channel_id=1, source_target_pairs={{1,0},{2,1},{3,2},{4,3},{5,4},{6,5},{7,6},{8,7},{9,8},{10,9},{11,1... | collective-permute-start | bytes 196616 | tf_op jit(solution)/shard_map/ppermute | solution.py:282
  98.4 1.4 %copy.13.partner = s32[30,3]{1,0:T(8,128)} copy(s32[30,3]{0,1:T(4,128)} %param.15) | data formatting | bytes 720 | tf_op args[4]
  99.8 1.4 %copy.14.partner = s32[16,2]{1,0:T(8,128)} copy(s32[16,2]{0,1:T(2,128)} %param.20) | data formatting | bytes 256 | tf_op args[9]
  101.2 0.0 collective-permute-done.11.low
  101.2 0.6 copy-done.9
  101.8 0.0 collective-permute-done.12.high
  101.8 0.6 copy-done.11
  102.4 0.8 copy-done.10
  103.3 0.8 copy-done.12
  104.1 0.7 copy-done.14
  104.8 0.7 copy-done.17
  105.5 1.9 %near_field.1.near = f32[16,2048]{1,0:T(8,128)S(1)} custom-call(s32[16,2]{1,0:T(8,128)S(1)} %copy-done.14, s32[16]{0:T(128)S(1)} %copy-done.17, s32[1]{0:T(128)} %bitcast.28.device, f32[16,2048]{1,0:T(8,128)S(1)} %copy-done.3, f32[16,1024]{1,0:T(8,128)S(1)} %copy-done.10, f32[16,1024]{1,0:T(8,128)S(1)} %copy-done.12, f32[16,2,128,128]{3,2,1,0:T(8,128)S(1)} %copy-done.1), custom_call_target="tpu_custom_call" | custom-call | tf_op jit(solution)/shard_map/near_field/pallas_call | solution.py:265
  107.3 0.0 copy-start.16
  107.3 0.0 collective-permute-done.10.high
  107.4 0.0 collective-permute-done.9.low
  107.4 0.0 copy-done.2
  107.4 0.0 copy-done.13
  107.4 0.0 copy-start.18
  107.4 0.6 copy-done.18
  108.0 2.3 %far_field.1.far = f32[30,8,128]{2,1,0:T(8,128)S(1)} custom-call(s32[30,3]{1,0:T(8,128)S(1)} %copy-done.13, s32[30]{0:T(128)S(1)} %copy-done.18, s32[1]{0:T(128)} %bitcast.28.device, f32[30,8,128]{2,1,0:T(8,128)} %get-tuple-element.14.own, f32[30,8,128]{2,1,0:T(8,128)} %collective-permute-done.9.low, f32[30,8,128]{2,1,0:T(8,128)} %collective-permute-done.10.high, ...), custom_call_target="tpu_custom_call" | custom-call | tf_op jit(solution)/shard_map/far_field/pallas_call | solution.py:265
  110.4 0.0 all-to-all-done.2.arrived
  110.4 0.0 copy-done.8
  110.4 3.9 %downward.1 = f32[16,2048]{1,0:T(8,128)} custom-call(f32[16,8,128]{2,1,0:T(8,128)S(1)} %all-to-all-done.2.arrived, f32[4,8,128]{2,1,0:T(8,128)S(1)} %copy-done.16, f32[32,128]{1,0:T(8,128)S(1)} %bitcast.56, f32[7,32,128]{2,1,0:T(8,128)S(1)} %maximum_select_fusion.1.table, bf16[30,64,128]{2,1,0:T(8,128)(2,1)S(1)} %copy-done.6, ...), custom_call_target="tpu_custom_call" | custom-call | tf_op jit(solution)/shard_map/downward/pallas_call | solution.py:265
  (45 shorter events, 0.2 us)
Async XLA Ops:
  0.0 9.0 %copy-start.3 = (f32[16,2048]{1,0:T(8,128)S(1)}, f32[16,2048]{1,0:T(8,128)}, u32[]{:S(2)}) copy-start(f32[16,2048]{1,0:T(8,128)} %own.1) | copy-start | bytes 393220
  0.0 9.0 %copy-start = (f32[16,64,128]{2,1,0:T(8,128)S(1)}, f32[16,64,128]{2,1,0:T(8,128)}, u32[]{:S(2)}) copy-start(f32[16,64,128]{2,1,0:T(8,128)} %basis.3) | copy-start | bytes 1572868
  0.0 9.1 %copy-start.4 = (f32[30,4096]{1,0:T(8,128)S(1)}, f32[30,4096]{1,0:T(8,128)}, u32[]{:S(2)}) copy-start(f32[30,4096]{1,0:T(8,128)} %transfer.1) | copy-start | bytes 1474564
  1.9 9.1 %collective-permute-start = (f32[1,32,128]{2,1,0:T(8,128)S(1)}, f32[1,32,128]{2,1,0:T(8,128)S(1)}, u32[]{:S(2)}, u32[]{:S(2)}) collective-permute-start(f32[1,32,128]{2,1,0:T(8,128)S(1)} %get-tuple-element.25), channel_id=1, source_target_pairs={{0,8},{16,24},{32,40},{48,56},{64,72},{80,88},{96,104},{112,120},{... | collective-permute-start | bytes 49160 | tf_op jit(solution)/shard_map/ppermute | solution.py:282
  5.8 5.3 %collective-permute-start.4 = (f32[1,32,128]{2,1,0:T(8,128)S(1)}, f32[1,32,128]{2,1,0:T(8,128)S(1)}, u32[]{:S(2)}, u32[]{:S(2)}) collective-permute-start(f32[1,32,128]{2,1,0:T(8,128)S(1)} %get-tuple-element.20), channel_id=1, source_target_pairs={{0,256}} | collective-permute-start | bytes 49160 | tf_op jit(solution)/shard_map/ppermute | solution.py:282
  8.9 30.9 %copy-start.7 = (f32[1,1,4096]{2,0,1:T(1,128)}, f32[1,1,4096]{2,0,1:T(1,128)S(1)}, u32[]{:S(2)}) copy-start(f32[1,1,4096]{2,0,1:T(1,128)S(1)} %get-tuple-element.35) | copy-start | bytes 49156
  11.0 25.8 %copy-start.5 = (bf16[30,64,128]{2,1,0:T(8,128)(2,1)}, bf16[30,64,128]{2,1,0:T(8,128)(2,1)S(1)}, u32[]{:S(2)}) copy-start(bf16[30,64,128]{2,1,0:T(8,128)(2,1)S(1)} %get-tuple-element.13.tables) | copy-start | bytes 1474564
  11.1 8.1 %collective-permute-start.5 = (f32[2,32,128]{2,1,0:T(8,128)S(1)}, f32[2,32,128]{2,1,0:T(8,128)S(1)}, u32[]{:S(2)}, u32[]{:S(2)}) collective-permute-start(f32[2,32,128]{2,1,0:T(8,128)S(1)} %pad_maximum_fusion.17), channel_id=1, source_target_pairs={{0,128},{256,384}} | collective-permute-start | bytes 98312 | tf_op jit(solution)/shard_map/ppermute | solution.py:282
  12.4 16.9 %collective-permute-start.1 = (f32[3,32,128]{2,1,0:T(8,128)S(1)}, f32[3,32,128]{2,1,0:T(8,128)S(1)}, u32[]{:S(2)}, u32[]{:S(2)}) collective-permute-start(f32[3,32,128]{2,1,0:T(8,128)S(1)} %pad_maximum_fusion.15), channel_id=1, source_target_pairs={{0,4},{8,12},{16,20},{24,28},{32,36},{40,44},{48,52},{56,60},{64,6... | collective-permute-start | bytes 147464 | tf_op jit(solution)/shard_map/ppermute | solution.py:282
  19.1 12.0 %collective-permute-start.6 = (f32[4,32,128]{2,1,0:T(8,128)S(1)}, f32[4,32,128]{2,1,0:T(8,128)S(1)}, u32[]{:S(2)}, u32[]{:S(2)}) collective-permute-start(f32[4,32,128]{2,1,0:T(8,128)S(1)} %pad_maximum_fusion.12), channel_id=1, source_target_pairs={{0,64},{128,192},{256,320},{384,448}} | collective-permute-start | bytes 196616 | tf_op jit(solution)/shard_map/ppermute | solution.py:282
  29.3 73.1 %copy-start.1 = (f32[16,2,128,128]{3,2,1,0:T(8,128)S(1)}, f32[16,2,128,128]{3,2,1,0:T(8,128)}, u32[]{:S(2)}) copy-start(f32[16,2,128,128]{3,2,1,0:T(8,128)} %block.1) | copy-start | bytes 6291460
  29.3 3.5 %collective-permute-start.2 = (f32[5,32,128]{2,1,0:T(8,128)S(1)}, f32[5,32,128]{2,1,0:T(8,128)S(1)}, u32[]{:S(2)}, u32[]{:S(2)}) collective-permute-start(f32[5,32,128]{2,1,0:T(8,128)S(1)} %pad_maximum_fusion.9), channel_id=1, source_target_pairs={{0,2},{4,6},{8,10},{12,14},{16,18},{20,22},{24,26},{28,30},{32,34}... | collective-permute-start | bytes 245768 | tf_op jit(solution)/shard_map/ppermute | solution.py:282
  32.9 4.0 %collective-permute-start.3 = (f32[7,32,128]{2,1,0:T(8,128)S(1)}, f32[7,32,128]{2,1,0:T(8,128)S(1)}, u32[]{:S(2)}, u32[]{:S(2)}) collective-permute-start(f32[7,32,128]{2,1,0:T(8,128)S(1)} %pad_maximum_fusion.2), channel_id=1, source_target_pairs={{0,1},{2,3},{4,5},{6,7},{8,9},{10,11},{12,13},{14,15},{16,17},{18,... | collective-permute-start | bytes 344072 | tf_op jit(solution)/shard_map/ppermute | solution.py:282
  34.9 8.4 %collective-permute-start.7 = (f32[6,32,128]{2,1,0:T(8,128)S(1)}, f32[6,32,128]{2,1,0:T(8,128)}, u32[]{:S(2)}, u32[]{:S(2)}) collective-permute-start(f32[6,32,128]{2,1,0:T(8,128)S(1)} %pad_maximum_fusion.6), channel_id=1, source_target_pairs={{0,32},{64,96},{128,160},{192,224},{256,288},{320,352},{384,416},{... | collective-permute-start | bytes 294920 | tf_op jit(solution)/shard_map/ppermute | solution.py:282
  39.8 10.2 %all-to-all-start = ((f32[16,16,128]{2,1,0:T(8,128)}), f32[16,16,128]{2,1,0:T(8,128)S(1)}, u32[]{:S(2)}, u32[]{:S(2)}) async-start(f32[16,16,128]{2,1,0:T(8,128)} %group_shares.1), calls=%async_computation | async-start | bytes 262144 | tf_op jit(solution)/shard_map/all_to_all | solution.py:387
  43.4 3.8 %collective-permute-start.8 = (f32[8,32,128]{2,1,0:T(8,128)S(1)}, f32[8,32,128]{2,1,0:T(8,128)S(1)}, u32[]{:S(2)}, u32[]{:S(2)}) collective-permute-start(f32[8,32,128]{2,1,0:T(8,128)S(1)} %pad_maximum_fusion), channel_id=1, source_target_pairs={{0,16},{32,48},{64,80},{96,112},{128,144},{160,176},{192,208},{224... | collective-permute-start | bytes 393224 | tf_op jit(solution)/shard_map/ppermute | solution.py:282
  52.3 0.6 copy-start.15
  52.9 29.3 %all-to-all-start.1 = ((f32[32,8,128]{2,1,0:T(8,128)}), f32[32,8,128]{2,1,0:T(8,128)S(1)}, u32[]{:S(2)}, u32[]{:S(2)}) async-start(f32[32,8,128]{2,1,0:T(8,128)} %get-tuple-element.11), calls=%async_computation.1 | async-start | bytes 262144 | tf_op jit(solution)/shard_map/all_to_all | solution.py:396
  66.9 40.4 %collective-permute-start.10 = (f32[30,8,128]{2,1,0:T(8,128)}, f32[30,8,128]{2,1,0:T(8,128)}, u32[]{:S(2)}, u32[]{:S(2)}) collective-permute-start(f32[30,8,128]{2,1,0:T(8,128)} %get-tuple-element.14.own), channel_id=1, source_target_pairs={{1,0},{2,1},{3,2},{4,3},{5,4},{6,5},{7,6},{8,7},{9,8},{10,9},{11,1... | collective-permute-start | bytes 368648 | tf_op jit(solution)/shard_map/ppermute | solution.py:282
  71.1 36.2 %collective-permute-start.9 = (f32[30,8,128]{2,1,0:T(8,128)}, f32[30,8,128]{2,1,0:T(8,128)}, u32[]{:S(2)}, u32[]{:S(2)}) collective-permute-start(f32[30,8,128]{2,1,0:T(8,128)} %get-tuple-element.14.own), channel_id=1, source_target_pairs={{0,1},{1,2},{2,3},{3,4},{4,5},{5,6},{6,7},{7,8},{8,9},{9,10},{10,1... | collective-permute-start | bytes 368648 | tf_op jit(solution)/shard_map/ppermute | solution.py:282
  85.1 25.2 %all-to-all-start.2 = ((f32[16,8,128]{2,1,0:T(8,128)}), f32[16,8,128]{2,1,0:T(8,128)S(1)}, u32[]{:S(2)}, u32[]{:S(2)}) async-start(f32[16,8,128]{2,1,0:T(8,128)} %top_turn.1), calls=%async_computation.2 | async-start | bytes 131072 | tf_op jit(solution)/shard_map/all_to_all | solution.py:404
  88.6 12.5 %collective-permute-start.11 = (f32[16,1024]{1,0:T(8,128)S(1)}, f32[16,1024]{1,0:T(8,128)S(1)}, u32[]{:S(2)}, u32[]{:S(2)}) collective-permute-start(f32[16,1024]{1,0:T(8,128)S(1)} %get-tuple-element.41), channel_id=1, source_target_pairs={{0,1},{1,2},{2,3},{3,4},{4,5},{5,6},{6,7},{7,8},{8,9},{9,10},{10,1... | collective-permute-start | bytes 196616 | tf_op jit(solution)/shard_map/ppermute | solution.py:282
  90.8 10.9 %collective-permute-start.12 = (f32[16,1024]{1,0:T(8,128)S(1)}, f32[16,1024]{1,0:T(8,128)S(1)}, u32[]{:S(2)}, u32[]{:S(2)}) collective-permute-start(f32[16,1024]{1,0:T(8,128)S(1)} %get-tuple-element.40), channel_id=1, source_target_pairs={{1,0},{2,1},{3,2},{4,3},{5,4},{6,5},{7,6},{8,7},{9,8},{10,9},{11,1... | collective-permute-start | bytes 196616 | tf_op jit(solution)/shard_map/ppermute | solution.py:282
  101.2 6.2 %copy-start.2 = (f32[30,3,4096]{2,0,1:T(8,128)S(1)}, f32[30,3,4096]{2,0,1:T(8,128)}, u32[]{:S(2)}) copy-start(f32[30,3,4096]{2,0,1:T(8,128)} %param.14) | copy-start | bytes 4423684
  101.2 0.6 copy-start.9
  101.8 0.6 copy-start.11
  102.4 0.8 copy-start.10
  103.3 0.8 copy-start.12
  104.1 0.7 copy-start.14
  104.8 0.7 copy-start.17
  105.5 1.9 %copy-start.13 = (s32[30,3]{1,0:T(8,128)S(1)}, s32[30,3]{1,0:T(8,128)}, u32[]{:S(2)}) copy-start(s32[30,3]{1,0:T(8,128)} %copy.13.partner) | copy-start | bytes 1084
  105.5 4.9 %copy-start.6 = (bf16[30,64,128]{2,1,0:T(8,128)(2,1)S(1)}, bf16[30,64,128]{2,1,0:T(8,128)(2,1)}, u32[]{:S(2)}) copy-start(bf16[30,64,128]{2,1,0:T(8,128)(2,1)} %copy-done.5) | copy-start | bytes 1474564
  107.3 3.1 %copy-start.8 = (f32[1,1,4096]{2,0,1:T(1,128)S(1)}, f32[1,1,4096]{2,0,1:T(1,128)}, u32[]{:S(2)}) copy-start(f32[1,1,4096]{2,0,1:T(1,128)} %copy-done.7) | copy-start | bytes 49156
  107.3 3.1 %copy-start.16 = (f32[4,8,128]{2,1,0:T(8,128)S(1)}, f32[4,8,128]{2,1,0:T(8,128)}, u32[]{:S(2)}) copy-start(f32[4,8,128]{2,1,0:T(8,128)} %copy-done.15) | copy-start | bytes 49156
  107.4 0.7 copy-start.18

commit v2 on v1

v2 whole, which is shorter than its diff:
```python
import jax
import jax.numpy as jnp
from jax import lax
from jax.experimental import pallas as pl
from jax.experimental.pallas import tpu as pltpu
from jax.sharding import PartitionSpec as P

F32 = jnp.float32
BF16 = jnp.bfloat16
RANK = 64
LEAVES = 16
POINTS = 128
LOCAL = 30
SLOTS = 3
NEAR = 2
REACH = 8
GROUP_BITS = 4
TOP_BITS = 9
GROUP = 1 << GROUP_BITS
TOP_STEPS = TOP_BITS - GROUP_BITS
GROUPS = 1 << TOP_STEPS
PORTER = 1
SPLIT = 2
LAYOUT = ((16, 0), (8, 16), (4, 24), (2, 28))
VMEM_BYTES = 20 * 1024 * 1024


def split(x):
    high = x.astype(BF16)
    return high, (x - high.astype(F32)).astype(BF16)


def lanes(rows):
    return lax.broadcasted_iota(jnp.int32, (rows, 128), 1)


def table_form(table):
    high, low = split(table)
    return jnp.concatenate([high, low, high, low], axis=0)


def coef_form(packed):
    lane = lanes(8)
    even = 2 * (lane % 32)
    parts = [
        jnp.take_along_axis(packed, even + shift, axis=1) for shift in (0, 64, 1, 65)
    ]
    full = jnp.concatenate(parts, axis=0)
    high, low = split(full)
    return jnp.where(lanes(32) < 64, high.astype(F32), low.astype(F32)).astype(BF16)


def dot(a, b):
    return lax.dot_general(a, b, (((1,), (0,)), ((), ())), preferred_element_type=F32)


def dot_t(a, b):
    return lax.dot_general(a, b, (((1,), (1,)), ((), ())), preferred_element_type=F32)


def fold(out):
    left = lanes(8) < 64
    straight = jnp.where(left, out[0:8], out[24:32])
    crossed = jnp.where(left, out[8:16], out[16:24])
    return straight + pltpu.roll(crossed, 64, 1)


def times(packed, table):
    return fold(dot(coef_form(packed), table_form(table)))


def row_form(packed):
    left = lanes(8) < 64
    turned = pltpu.roll(packed, 64, 1)
    zero = jnp.zeros_like(packed)
    full = jnp.concatenate(
        [
            jnp.where(left, packed, zero),
            jnp.where(left, turned, zero),
            jnp.where(left, zero, turned),
            jnp.where(left, zero, packed),
        ],
        axis=0,
    )
    return split(full)


def weave(even_odd):
    lane = lanes(8)
    place = (lane % 64) // 2
    wide = jnp.concatenate([even_odd] * 4, axis=1)
    pick = [jnp.take_along_axis(wide[8 * k : 8 * k + 8], place, axis=1) for k in range(4)]
    even = lane % 2 == 0
    return jnp.where(
        lane < 64, jnp.where(even, pick[0], pick[2]), jnp.where(even, pick[1], pick[3])
    )


def times_t_raw(rows, high, low):
    row_high, row_low = rows
    both = dot_t(jnp.concatenate([row_high, row_low], axis=0), high)
    return both[:32] + both[32:] + dot_t(row_high, low)


def times_t(packed, table):
    high, low = split(table)
    return weave(times_t_raw(row_form(packed), high, low))


def unpack(packed):
    return jnp.concatenate([packed[:, :RANK], packed[:, RANK:]], axis=0)


def pack(value):
    return jnp.concatenate([value[:8], value[8:]], axis=1)


def place_of_device():
    device = lax.axis_index("leaf").astype(jnp.int32)
    return device, device & (GROUP - 1), device >> GROUP_BITS


def up_kernel(sources, basis, transfer, coefs, root, tables, forward, backward):
    table = transfer[...].reshape(LOCAL, 32, 128)
    for row in range(LOCAL):
        high, low = split(table[row])
        tables[row, 0:32] = high
        tables[row, 32:64] = low
    for leaf in range(LEAVES):
        entries = sources[:, leaf * POINTS : (leaf + 1) * POINTS]
        edge, place = (backward, leaf) if leaf < REACH else (forward, leaf - REACH)
        edge[LOCAL + 2 * place] = entries[:8]
        edge[LOCAL + 2 * place + 1] = entries[8:]
        high, low = split(entries)
        basis_high, basis_low = split(basis[leaf])
        both = dot_t(jnp.concatenate([high, low], axis=0), basis_high)
        coefs[leaf] = pack(both[:16] + both[16:] + dot_t(high, basis_low))
    for level, (clusters, offset) in enumerate(LAYOUT):
        for parent in range(clusters // 2):
            first = offset + 2 * parent
            left = jnp.concatenate(
                [coef_form(coefs[first]), coef_form(coefs[first + 1])], axis=1
            )
            halves = [tables[first], tables[first], tables[first + 1], tables[first + 1]]
            value = fold(dot(left, jnp.concatenate(halves, axis=0)))
            if clusters > 2:
                coefs[offset + clusters + parent] = value
            else:
                root[...] = value
    forward[0:LOCAL] = coefs[...]
    backward[0:LOCAL] = coefs[...]


def near_kernel(partner, count, own, low, high, block, out, leaves):
    for leaf in range(LEAVES):
        leaves[REACH + leaf] = own[:, leaf * POINTS : (leaf + 1) * POINTS]
    for leaf in range(REACH):
        for half in range(2):
            rows = slice(8 * half, 8 * half + 8)
            leaves[leaf, rows] = low[LOCAL + 2 * leaf + half]
            leaves[REACH + LEAVES + leaf, rows] = high[LOCAL + 2 * leaf + half]
    first = place_of_device()[0] * LEAVES - REACH
    for leaf in range(LEAVES):
        total = None
        for slot in range(NEAR):
            place = jnp.clip(partner[slot, leaf] - first, 0, LEAVES + 2 * REACH - 1)
            used = (slot < count[leaf]).astype(F32)
            picked_high, picked_low = split(leaves[place] * used)
            block_high, block_low = split(block[leaf, slot])
            both = dot_t(jnp.concatenate([picked_high, picked_low], axis=0), block_high)
            value = both[:16] + both[16:] + dot_t(picked_high, block_low)
            total = value if total is None else total + value
        out[:, leaf * POINTS : (leaf + 1) * POINTS] = total


def far_kernel(partner, count, own, low, high, coupling, out, extended):
    device = place_of_device()[0]
    extended[0:LOCAL] = low[0:LOCAL]
    extended[LOCAL : 2 * LOCAL] = own[...]
    extended[2 * LOCAL : 3 * LOCAL] = high[0:LOCAL]
    tables = [coupling[slot].reshape(LOCAL, 32, 128) for slot in range(SLOTS)]
    for clusters, offset in LAYOUT:
        for cluster in range(clusters):
            row = offset + cluster
            left = []
            right = []
            for slot in range(SLOTS):
                index = partner[slot, row]
                side = jnp.clip(index // clusters - device + 1, 0, 2)
                place = side * LOCAL + offset + index % clusters
                used = (slot < count[row]).astype(F32)
                left.append(coef_form(extended[place] * used))
                right.append(table_form(tables[slot][row]))
            out[row] = fold(dot(jnp.concatenate(left, axis=1), jnp.concatenate(right, axis=0)))


def gather_tables(transfers, couplings, group_raw, high_raw, low_raw, group_pay):
    for level in range(GROUP_BITS):
        group_raw[level] = transfers[level]
        for side in range(2):
            group_raw[GROUP_BITS * (1 + side) + level] = couplings[level, :, side, :]
    for level in range(TOP_STEPS):
        half, (transfer, *sides) = top_place(level)
        raw = (low_raw, high_raw)[half]
        if transfer is not None:
            raw[transfer] = transfers[GROUP_BITS + level]
        for side in range(2):
            raw[sides[side]] = couplings[GROUP_BITS + level, :, side, :]
    group_pay[0] = couplings[GROUP_BITS - 1, :, 1, :]


def group_place(level):
    return level, GROUP_BITS + level, 2 * GROUP_BITS + level


def top_place(level):
    if level < SPLIT:
        return 0, (level, SPLIT + level, 2 * SPLIT + level)
    place = level - SPLIT
    size = TOP_STEPS - SPLIT
    transfer = place if level < TOP_STEPS - 1 else None
    return 1, (transfer, size - 1 + place, 2 * size - 1 + place)


def group_entries(raw, level):
    _, left, right = group_place(level)
    above = raw[level + 1] if level + 1 < GROUP_BITS else None
    return above, raw[left], raw[right]


def top_entries(raws, level):
    half, (_, left, right) = top_place(level)
    above = None
    if level + 2 < TOP_STEPS:
        upper, (transfer, _, _) = top_place(level + 1)
        above = raws[upper][transfer]
    return above, raws[half][left], raws[half][right]


def write_payload(entries, live, pay):
    above, _, right = entries
    place = 0
    if above is not None:
        pay[0] = above
        place = 1
    if live is not None:
        pay[place : place + live.shape[0]] = live[...]
        place += live.shape[0]
    pay[place] = right


def merge(entries, live, arrived, out, flag):
    above, left, _ = entries
    size = out.shape[0]
    right_child = flag == 1
    start = 0
    if above is not None:
        out[0] = jnp.where(right_child, arrived[0], above)
        start = 1
    for entry in range(start, size - 1):
        out[entry] = jnp.where(right_child, arrived[entry], live[entry - start])
    out[size - 1] = jnp.where(right_child, arrived[size - 1], left)


def call(kernel, name, outs, args, scalars=0, scratch=(), after=(), flops=0):
    vmem = pl.BlockSpec(memory_space=pltpu.VMEM)
    smem = pl.BlockSpec(memory_space=pltpu.SMEM)
    spare = pl.BlockSpec(memory_space=pl.ANY)
    given = len(args)

    def body(*refs):
        kernel(*refs[:given], *refs[given + len(after) :])

    single = not isinstance(outs, list)
    return pl.pallas_call(
        body,
        out_shape=outs,
        in_specs=[smem] * scalars + [vmem] * (given - scalars) + [spare] * len(after),
        out_specs=vmem if single else [vmem] * len(outs),
        scratch_shapes=list(scratch),
        compiler_params=pltpu.CompilerParams(vmem_limit_bytes=VMEM_BYTES),
        cost_estimate=pl.CostEstimate(
            flops=flops, bytes_accessed=flops // 400, transcendentals=0
        ),
        name=name,
    )(*args, *after)


def shape(*dims, dtype=F32):
    return jax.ShapeDtypeStruct(dims, dtype)


def permute(value, pairs):
    return lax.ppermute(value, "leaf", pairs)


def step_pairs(count, bit, member=0):
    return [(i + member, i + member + (1 << bit)) for i in range(0, count, 2 << bit)]


def group_size(bit):
    return 2 * (GROUP_BITS - bit) - 1


def top_size(bit):
    left = TOP_BITS - bit
    return left + max(left - 2, 0)


def share_kernel(root, raw, live, arrived, blocks, table, chain):
    _, member, _ = place_of_device()
    merge(group_entries(raw, 0), live, arrived, table, member & 1)
    value = root[...]
    chain[0] = value
    for level in range(GROUP_BITS):
        value = times(value, raw[0] if level == 0 else table[level - 1])
        if level + 1 < GROUP_BITS:
            chain[level + 1] = value
    for other in range(GROUP):
        apart = member ^ other
        level = sum((apart >= (1 << bit)).astype(jnp.int32) for bit in range(1, GROUP_BITS))
        blocks[other, 0:8] = chain[level]
        blocks[other, 8:16] = value


def rise_kernel(given, low_raw, high_raw, live, arrived, sibling, blocks, table, chain):
    _, member, group = place_of_device()
    merge(top_entries((low_raw, high_raw), 0), live, arrived, table, group & 1)
    for level in range(GROUP_BITS):
        total = None
        for apart in range(1 << level, 2 << level):
            value = given[member ^ apart, 0:8]
            total = value if total is None else total + value
        sibling[level] = total
    value = given[0, 8:16]
    for other in range(1, GROUP):
        value = value + given[other, 8:16]
    chain[0] = value
    for level in range(TOP_STEPS - 1):
        value = times(value, low_raw[0] if level == 0 else table[level - 1])
        chain[level + 1] = value
    for other in range(GROUPS):
        apart = group ^ other
        level = sum((apart >= (1 << bit)).astype(jnp.int32) for bit in range(1, TOP_STEPS))
        blocks[other] = chain[level]


def turn_kernel(given, raw, table, out):
    _, _, group = place_of_device()
    terms = []
    for level in range(TOP_STEPS):
        total = None
        for apart in range(1 << level, 2 << level):
            piece = given[group ^ apart]
            total = piece if total is None else total + piece
        terms.append(times(total, table[2 * TOP_STEPS - 3 - level]))
    value = terms[TOP_STEPS - 1]
    for level in range(TOP_STEPS - 2, -1, -1):
        value = times_t(value, raw[0] if level == 0 else table[level - 1]) + terms[level]
    for other in range(GROUP):
        out[other] = value


def down_kernel(given, sibling, raw, table, tables, far, basis, near, out):
    value = given[PORTER]
    terms = [
        times(sibling[level], table[2 * GROUP_BITS - 2 - level]) for level in range(GROUP_BITS)
    ]
    for level in range(GROUP_BITS - 1, -1, -1):
        value = times_t(value, raw[0] if level == 0 else table[level - 1]) + terms[level]
    parents = [value]
    for clusters, offset in reversed(LAYOUT):
        following = []
        for parent in range(clusters // 2):
            first = offset + 2 * parent
            high = jnp.concatenate([tables[first, 0:32], tables[first + 1, 0:32]], axis=0)
            low = jnp.concatenate([tables[first, 32:64], tables[first + 1, 32:64]], axis=0)
            out_pair = times_t_raw(row_form(parents[parent]), high, low)
            following.append(weave(out_pair[:, 0:32]) + far[first])
            following.append(weave(out_pair[:, 32:64]) + far[first + 1])
        parents = following
    for leaf in range(LEAVES):
        high, low = split(unpack(parents[leaf]))
        basis_high, basis_low = split(basis[leaf])
        both = dot(jnp.concatenate([high, low], axis=0), basis_high)
        place = slice(leaf * POINTS, (leaf + 1) * POINTS)
        out[:, place] = both[:16] + both[16:] + dot(high, basis_low) + near[:, place]


def on_device(
    sources,
    leaf_cluster_basis,
    local_transfer,
    far_coupling,
    far_partner,
    far_count,
    top_transfer,
    top_coupling,
    near_block,
    near_partner,
    near_count,
):
    count = lax.axis_size("leaf")
    forward = [(i, i + 1) for i in range(count - 1)]
    backward = [(i + 1, i) for i in range(count - 1)]

    transfers = top_transfer.reshape(TOP_BITS, 32, 128)
    couplings = top_coupling.reshape(TOP_BITS, 2, 32, 128).transpose(0, 2, 1, 3)
    size = TOP_STEPS - SPLIT
    group_raw, high_raw, low_raw, group_pay = call(
        gather_tables,
        "top_tables",
        [
            shape(3 * GROUP_BITS, 32, 128),
            shape(3 * size - 1, 32, 128),
            shape(3 * SPLIT, 32, 128),
            shape(1, 32, 128),
        ],
        [transfers, couplings],
        flops=1 << 30,
    )
    to_porter = [(i, i + PORTER) for i in range(0, count, GROUP)]
    high_raw = permute(high_raw, to_porter)
    group_in = permute(group_pay, step_pairs(count, GROUP_BITS - 1))
    low_raw = permute(low_raw, to_porter)

    coefs, root, tables, low_edge, high_edge = call(
        up_kernel,
        "upward",
        [
            shape(LOCAL, 8, 128),
            shape(8, 128),
            shape(LOCAL, 64, 128, dtype=BF16),
            shape(LOCAL + 2 * REACH, 8, 128),
            shape(LOCAL + 2 * REACH, 8, 128),
        ],
        [sources, leaf_cluster_basis, local_transfer],
        flops=2 << 30,
    )
    low = permute(low_edge, forward)
    high = permute(high_edge, backward)

    group_live = None
    top_live = None
    top_in = None
    for step in range(GROUP_BITS - 1):
        bit = GROUP_BITS - 1 - step
        top_bit = TOP_BITS - step

        def joint(*refs, bit=bit, top_bit=top_bit, step=step):
            refs = list(refs)
            raw, arrived = refs.pop(0), refs.pop(0)
            live = refs.pop(0) if step else None
            raws = (None, refs.pop(0))
            upper_arrived = refs.pop(0) if step else None
            upper_live = refs.pop(0) if step > 1 else None
            out, pay = refs.pop(0), refs.pop(0)
            _, member, group = place_of_device()
            merge(group_entries(raw, bit), live, arrived, out, (member >> bit) & 1)
            write_payload(group_entries(raw, bit - 1), out, pay)
            upper_out = None
            level = top_bit - GROUP_BITS
            if step:
                upper_out = refs.pop(0)
                entries = top_entries(raws, level)
                merge(entries, upper_live, upper_arrived, upper_out, (group >> level) & 1)
            write_payload(top_entries(raws, level - 1), upper_out, refs.pop(0))

        args = [group_raw, group_in]
        if step:
            args.append(group_live)
        args.append(high_raw)
        if step:
            args.append(top_in)
        if step > 1:
            args.append(top_live)
        outs = [shape(group_size(bit), 32, 128), shape(group_size(bit - 1), 32, 128)]
        if step:
            outs.append(shape(top_size(top_bit), 32, 128))
        outs.append(shape(top_size(top_bit - 1), 32, 128))
        results = list(call(joint, f"hand_down_{step}", outs, args, flops=1 << 29))
        group_live, group_pay = results[0], results[1]
        if step:
            top_live = results[2]
        top_pay = results[-1]
        group_in = permute(group_pay, step_pairs(count, bit - 1))
        top_in = permute(top_pay, step_pairs(count, top_bit - 1, PORTER))

    def step_up(bit, live, arrived, after=()):
        def lone(low, high, live, arrived, out, pay):
            level = bit - GROUP_BITS
            _, _, group = place_of_device()
            merge(top_entries((low, high), level), live, arrived, out, (group >> level) & 1)
            write_payload(top_entries((low, high), level - 1), out, pay)

        return call(
            lone,
            f"hand_down_top_{bit}",
            [shape(top_size(bit), 32, 128), shape(top_size(bit - 1), 32, 128)],
            [low_raw, high_raw, live, arrived],
            flops=1 << 29,
            after=after,
        )

    bit = TOP_BITS - GROUP_BITS + 1
    top_live, top_pay = step_up(bit, top_live, top_in)
    shares, group_table = call(
        share_kernel,
        "group_shares",
        [shape(GROUP, 16, 128), shape(2 * GROUP_BITS - 1, 32, 128)],
        [root, group_raw, group_live, group_in],
        scratch=[pltpu.VMEM((GROUP_BITS, 8, 128), F32)],
        after=[top_live],
        flops=2 << 30,
    )
    in_group = [list(range(first, first + GROUP)) for first in range(0, count, GROUP)]
    across = [list(range(first, count, GROUP)) for first in range(GROUP)]
    group_given = lax.all_to_all(shares, "leaf", 0, 0, axis_index_groups=in_group)
    top_in = permute(top_pay, step_pairs(count, bit - 1, PORTER))
    for bit in range(bit - 1, GROUP_BITS, -1):
        top_live, top_pay = step_up(bit, top_live, top_in)
        top_in = permute(top_pay, step_pairs(count, bit - 1, PORTER))

    sibling, rising, top_table = call(
        rise_kernel,
        "top_shares",
        [shape(GROUP_BITS, 8, 128), shape(GROUPS, 8, 128), shape(2 * TOP_STEPS - 2, 32, 128)],
        [group_given, low_raw, high_raw, top_live, top_in],
        scratch=[pltpu.VMEM((TOP_STEPS, 8, 128), F32)],
        flops=2 << 30,
    )
    top_given = lax.all_to_all(rising, "leaf", 0, 0, axis_index_groups=across)

    near = call(
        near_kernel,
        "near_field",
        shape(16, LEAVES * POINTS),
        [near_partner.T, near_count, sources, low, high, near_block],
        scalars=2,
        scratch=[pltpu.VMEM((LEAVES + 2 * REACH, 16, POINTS), F32)],
        flops=2 << 30,
    )
    far = call(
        far_kernel,
        "far_field",
        shape(LOCAL, 8, 128),
        [far_partner.T, far_count, coefs, low, high, far_coupling.transpose(1, 0, 2)],
        scalars=2,
        scratch=[pltpu.VMEM((3 * LOCAL, 8, 128), F32)],
        flops=2 << 30,
    )
    turned = call(
        turn_kernel,
        "top_turn",
        shape(GROUP, 8, 128),
        [top_given, low_raw, top_table],
        after=[near, far],
        flops=2 << 30,
    )
    given = lax.all_to_all(turned, "leaf", 0, 0, axis_index_groups=in_group)
    return call(
        down_kernel,
        "downward",
        shape(16, LEAVES * POINTS),
        [given, sibling, group_raw, group_table, tables, far, leaf_cluster_basis, near],
        flops=4 << 30,
    )


def solution(mesh):
    placed = (
        P(None, "leaf"),
        P("leaf", None, None),
        P("leaf", None),
        P("leaf", None, None),
        P("leaf", None),
        P("leaf"),
        P("leaf", None, None),
        P("leaf", None, None, None),
        P("leaf", None, None, None),
        P("leaf", None),
        P("leaf"),
    )
    return jax.shard_map(
        on_device, mesh=mesh, in_specs=placed, out_specs=P(None, "leaf"), check_vma=False
    )
```

time: 115 us -> 97.3 us (0.85)
  the two profiles are of different devices: /device:TPU:8 before, /device:TPU:1 now
where the time goes in v2:
time: 97.3 us; the launch traced here: 96.6 us
  starting transfers between devices  42.7 us (44%)
  waiting for transfers between devices  19.2 us (20%)
  Pallas kernels  14.6 us (15%)
  blocking collectives  10.8 us (11%)
  local copies, waits for them, and re-layouts  9.03 us (9%)
    ppermute x13, starting transfers between devices, permute(): return lax.ppermute(value, 'leaf', pairs)  25.7 us
    pallas_call x13, Pallas kernels, call(): pl.pallas_call(body, out_shape=outs, in_specs=[smem] * scalars + [vmem] *...  14.6 us
    all_to_all x1, starting transfers between devices, on_device(): top_given = lax.all_to_all(rising, 'leaf', 0, 0, axis_index_groups=across)  12.8 us
    all_to_all x1, blocking collectives, on_device(): given = lax.all_to_all(turned, 'leaf', 0, 0, axis_index_groups=in_group)  10.8 us
    ppermute x13, waiting for transfers between devices, permute(): return lax.ppermute(value, 'leaf', pairs)  9.76 us
    all_to_all x1, waiting for transfers between devices, on_device(): top_given = lax.all_to_all(rising, 'leaf', 0, 0, axis_index_groups=across)  9.46 us
    unnamed x62, local copies, waits for them, and re-layouts  9.03 us
    all_to_all x1, starting transfers between devices, on_device(): lax.all_to_all(shares, 'leaf', 0, 0, axis_index_groups=in_group)  4.2 us
  transfers between devices with their start and end apart: 15, of which 5 were waited for; matrix products, arithmetic and copies ran while one was open for 0% of the time, Pallas kernels for 7%

profile of v2, /device:TPU:1, one launch (start us, length us, event | category | flops | bytes accessed | tf_op | source)
XLA Modules:
  0.0 96.6 jit_solution(12892555672351259064)
XLA Ops:
  0.0 1.0 copy-done.4
  1.0 0.9 copy-done.5
  1.9 0.2 top_tables.1
  2.0 0.0 copy-start.19
  2.1 1.3 %collective-permute-start.1 = (f32[8,32,128]{2,1,0:T(8,128)S(1)}, f32[8,32,128]{2,1,0:T(8,128)S(1)}, u32[]{:S(2)}, u32[]{:S(2)}) collective-permute-start(f32[8,32,128]{2,1,0:T(8,128)S(1)} %get-tuple-element.37), channel_id=1, source_target_pairs={{0,1},{16,17},{32,33},{48,49},{64,65},{80,81},{96,97},{112,113},{1... | collective-permute-start | bytes 393224 | tf_op jit(solution)/shard_map/ppermute | solution.py:294
  3.4 0.7 collective-permute-start
  4.0 0.0 collective-permute-done.refs_1_
  4.0 7.0 %collective-permute-done.1.refs_2_.refs_3_.refs_1_ = f32[8,32,128]{2,1,0:T(8,128)S(1)} collective-permute-done((f32[8,32,128]{2,1,0:T(8,128)S(1)}, f32[8,32,128]{2,1,0:T(8,128)S(1)}, u32[]{:S(2)}, u32[]{:S(2)}) %collective-permute-start.1) | collective-permute-done | bytes 131104 | tf_op jit(solution)/shard_map/ppermute | solution.py:294
  11.1 0.0 copy-start.2
  11.1 0.0 copy-start.3
  11.1 0.0 copy-start.6
  11.1 0.8 collective-permute-start.2
  11.9 1.3 %collective-permute-start.3 = (f32[1,32,128]{2,1,0:T(8,128)S(1)}, f32[1,32,128]{2,1,0:T(8,128)S(1)}, u32[]{:S(2)}, u32[]{:S(2)}) collective-permute-start(f32[1,32,128]{2,1,0:T(8,128)S(1)} %get-tuple-element.40), channel_id=1, source_target_pairs={{1,257}} | collective-permute-start | bytes 49160 | tf_op jit(solution)/shard_map/ppermute | solution.py:294
  13.2 0.9 collective-permute-done.3.refs_4_
  14.1 0.0 collective-permute-done.2.refs_1_
  14.1 0.7 collective-permute-start.4
  14.8 1.3 %collective-permute-start.5 = (f32[2,32,128]{2,1,0:T(8,128)S(1)}, f32[2,32,128]{2,1,0:T(8,128)S(1)}, u32[]{:S(2)}, u32[]{:S(2)}) collective-permute-start(f32[2,32,128]{2,1,0:T(8,128)S(1)} %get-tuple-element.43), channel_id=1, source_target_pairs={{1,129},{257,385}} | collective-permute-start | bytes 98312 | tf_op jit(solution)/shard_map/ppermute | solution.py:294
  16.1 1.3 %collective-permute-start.7 = (f32[6,32,128]{2,1,0:T(8,128)S(1)}, f32[6,32,128]{2,1,0:T(8,128)S(1)}, u32[]{:S(2)}, u32[]{:S(2)}) collective-permute-start(f32[6,32,128]{2,1,0:T(8,128)S(1)} %get-tuple-element.47), channel_id=1, source_target_pairs={{0,1},{16,17},{32,33},{48,49},{64,65},{80,81},{96,97},{112,113},{1... | collective-permute-start | bytes 294920 | tf_op jit(solution)/shard_map/ppermute | solution.py:294
  17.4 0.0 collective-permute-done.5.refs_4_
  17.4 0.0 collective-permute-done.4.refs_1_
  17.4 8.4 %collective-permute-start.8 = (f32[4,32,128]{2,1,0:T(8,128)S(1)}, f32[4,32,128]{2,1,0:T(8,128)S(1)}, u32[]{:S(2)}, u32[]{:S(2)}) collective-permute-start(f32[4,32,128]{2,1,0:T(8,128)S(1)} %get-tuple-element.49), channel_id=1, source_target_pairs={{1,65},{129,193},{257,321},{385,449}} | collective-permute-start | bytes 196616 | tf_op jit(solution)/shard_map/ppermute | solution.py:294
  25.9 1.3 %collective-permute-start.6 = (f32[7,32,128]{2,1,0:T(8,128)S(1)}, f32[7,32,128]{2,1,0:T(8,128)S(1)}, u32[]{:S(2)}, u32[]{:S(2)}) collective-permute-start(f32[7,32,128]{2,1,0:T(8,128)S(1)} %get-tuple-element.46), channel_id=1, source_target_pairs={{0,1},{2,3},{4,5},{6,7},{8,9},{10,11},{12,13},{14,15},{16,17},{18,... | collective-permute-start | bytes 344072 | tf_op jit(solution)/shard_map/ppermute | solution.py:294
  27.2 0.0 copy-done.2
  27.2 0.0 copy-done.3
  27.2 0.0 copy-done.6
  27.2 1.6 %upward.1 = (f32[30,8,128]{2,1,0:T(8,128)S(1)}, f32[8,128]{1,0:T(8,128)S(1)}, bf16[30,64,128]{2,1,0:T(8,128)(2,1)S(1)}, f32[46,8,128]{2,1,0:T(8,128)S(1)}, f32[46,8,128]{2,1,0:T(8,128)S(1)}) custom-call(f32[16,2048]{1,0:T(8,128)S(1)} %copy-done.6, f32[16,64,128]{2,1,0:T(8,128)S(1)} %copy-done.3, f32[30,4096]{1,0:T(8,128)S(1)} %copy-done.2), custom_call_target="tpu_custom_call" | custom-call | flops 2147483648 | bytes 5368709 | tf_op jit(solution)/shard_map/upward/pallas_call | solution.py:275
  28.8 0.0 collective-permute-done.7.refs_0_.refs_1_
  28.8 0.0 copy-start.12
  28.8 0.0 collective-permute-done.8.refs_3_
  28.8 0.3 collective-permute-done.6.refs_3_
  29.1 0.0 copy-done.19
  29.1 1.7 %group_shares.1 = (f32[16,16,128]{2,1,0:T(8,128)}, f32[7,32,128]{2,1,0:T(8,128)S(1)}) custom-call(f32[8,128]{1,0:T(8,128)S(1)} %get-tuple-element.34.refs_0_, f32[12,32,128]{2,1,0:T(8,128)S(1)} %get-tuple-element.35.refs_0_.refs_1_.refs_2_, f32[5,32,128]{2,1,0:T(8,128)S(1)} %get-tuple-element.45.refs_2_, f32[7,32,128]{2,1,0:T(8,128)S(1)} %collective-permute-done.6.refs_3_, ...), custom_call_target="tpu_custom_call" | custom-call | flops 2147483648 | bytes 5368709 | tf_op jit(solution)/shard_map/group_shares/pallas_call | solution.py:275
  30.8 0.6 copy-done.29
  31.4 4.2 %all-to-all-start = ((f32[16,16,128]{2,1,0:T(8,128)}), f32[16,16,128]{2,1,0:T(8,128)S(1)}, u32[]{:S(2)}, u32[]{:S(2)}) async-start(f32[16,16,128]{2,1,0:T(8,128)} %get-tuple-element.51), calls=%async_computation | async-start | bytes 262144 | tf_op jit(solution)/shard_map/all_to_all | solution.py:518
  35.6 3.1 %collective-permute-start.9 = (f32[6,32,128]{2,1,0:T(8,128)S(1)}, f32[6,32,128]{2,1,0:T(8,128)S(1)}, u32[]{:S(2)}, u32[]{:S(2)}) collective-permute-start(f32[6,32,128]{2,1,0:T(8,128)S(1)} %get-tuple-element.52), channel_id=1, source_target_pairs={{1,33},{65,97},{129,161},{193,225},{257,289},{321,353},{385,417},{... | collective-permute-start | bytes 294920 | tf_op jit(solution)/shard_map/ppermute | solution.py:294
  38.7 1.6 %collective-permute-done.9.refs_3_ = f32[6,32,128]{2,1,0:T(8,128)S(1)} collective-permute-done((f32[6,32,128]{2,1,0:T(8,128)S(1)}, f32[6,32,128]{2,1,0:T(8,128)S(1)}, u32[]{:S(2)}, u32[]{:S(2)}) %collective-permute-start.9) | collective-permute-done | bytes 98336 | tf_op jit(solution)/shard_map/ppermute | solution.py:294
  40.3 0.0 copy-done.8
  40.4 0.6 copy-done.21
  41.0 1.3 %collective-permute-start.10 = (f32[8,32,128]{2,1,0:T(8,128)S(1)}, f32[8,32,128]{2,1,0:T(8,128)S(1)}, u32[]{:S(2)}, u32[]{:S(2)}) collective-permute-start(f32[8,32,128]{2,1,0:T(8,128)S(1)} %get-tuple-element.54), channel_id=1, source_target_pairs={{1,17},{33,49},{65,81},{97,113},{129,145},{161,177},{193,209},{225... | collective-permute-start | bytes 393224 | tf_op jit(solution)/shard_map/ppermute | solution.py:294
  42.3 1.9 %collective-permute-start.11 = (f32[46,8,128]{2,1,0:T(8,128)S(1)}, f32[46,8,128]{2,1,0:T(8,128)S(1)}, u32[]{:S(2)}, u32[]{:S(2)}) collective-permute-start(f32[46,8,128]{2,1,0:T(8,128)S(1)} %get-tuple-element.57), channel_id=1, source_target_pairs={{0,1},{1,2},{2,3},{3,4},{4,5},{5,6},{6,7},{7,8},{8,9},{9,10},{10,1... | collective-permute-start | bytes 565256 | tf_op jit(solution)/shard_map/ppermute | solution.py:294
  44.2 2.4 %collective-permute-start.12 = (f32[46,8,128]{2,1,0:T(8,128)S(1)}, f32[46,8,128]{2,1,0:T(8,128)S(1)}, u32[]{:S(2)}, u32[]{:S(2)}) collective-permute-start(f32[46,8,128]{2,1,0:T(8,128)S(1)} %get-tuple-element.58), channel_id=1, source_target_pairs={{1,0},{2,1},{3,2},{4,3},{5,4},{6,5},{7,6},{8,7},{9,8},{10,9},{11,1... | collective-permute-start | bytes 565256 | tf_op jit(solution)/shard_map/ppermute | solution.py:294
  46.7 0.0 collective-permute-done.10.refs_4_
  46.7 0.6 copy-done.10
  47.3 0.0 all-to-all-done.refs_0_
  47.3 0.9 copy-done.9
  48.2 0.9 copy-done.11
  49.1 0.9 copy-done.13
  50.0 0.9 copy-done.22
  50.9 1.8 %top_shares.1 = (f32[4,8,128]{2,1,0:T(8,128)S(1)}, f32[32,8,128]{2,1,0:T(8,128)}, f32[8,32,128]{2,1,0:T(8,128)S(1)}) custom-call(f32[16,16,128]{2,1,0:T(8,128)S(1)} %all-to-all-done.refs_0_, f32[6,32,128]{2,1,0:T(8,128)S(1)} %copy-done.13, f32[8,32,128]{2,1,0:T(8,128)S(1)} %copy-done.9, f32[6,32,128]{2,1,0:T(8,128)S(1)} %copy-done.22, ...), custom_call_target="tpu_custom_call" | custom-call | flops 2147483648 | bytes 5368709 | tf_op jit(solution)/shard_map/top_shares/pallas_call | solution.py:275
  52.7 0.7 copy-done.27
  53.4 12.8 %all-to-all-start.1 = ((f32[32,8,128]{2,1,0:T(8,128)}), f32[32,8,128]{2,1,0:T(8,128)S(1)}, u32[]{:S(2)}, u32[]{:S(2)}) async-start(f32[32,8,128]{2,1,0:T(8,128)} %get-tuple-element.55), calls=%async_computation.1 | async-start | bytes 262144 | tf_op jit(solution)/shard_map/all_to_all | solution.py:532
  66.1 0.0 collective-permute-done.11.refs_3_
  66.2 0.0 collective-permute-done.12.refs_4_
  66.2 0.0 copy-start.7
  66.2 0.9 copy-done.7
  67.1 1.7 %near_field.1.refs_3_.refs_7_ = f32[16,2048]{1,0:T(8,128)S(1)} custom-call(s32[2,16]{1,0:T(2,128)S(1)} %bitcast.11, s32[16]{0:T(128)S(1)} %copy-done.17, f32[16,2048]{1,0:T(8,128)S(1)} %copy-done.7, f32[46,8,128]{2,1,0:T(8,128)S(1)} %collective-permute-done.11.refs_3_, f32[46,8,128]{2,1,0:T(8,128)S(1)} %collective-permute-done.12.refs_4_, ...), custom_call_target="tpu_custom_call" | custom-call | flops 2147483648 | bytes 5368709 | tf_op jit(solution)/shard_map/near_field/pallas_call | solution.py:275
  68.9 0.0 copy-done.15
  68.9 1.9 %far_field.1.refs_4_.refs_5_ = f32[30,8,128]{2,1,0:T(8,128)S(1)} custom-call(s32[3,30]{1,0:T(4,128)S(1)} %bitcast.10, s32[30]{0:T(128)S(1)} %copy-done.18, f32[30,8,128]{2,1,0:T(8,128)S(1)} %copy-done.26, f32[46,8,128]{2,1,0:T(8,128)S(1)} %collective-permute-done.11.refs_3_, f32[46,8,128]{2,1,0:T(8,128)S(1)} %collective-permute-done.12.refs_4_, ...), custom_call_target="tpu_custom_call" | custom-call | flops 2147483648 | bytes 5368709 | tf_op jit(solution)/shard_map/far_field/pallas_call | solution.py:275
  70.8 9.5 %all-to-all-done.1.refs_0_ = f32[32,8,128]{2,1,0:T(8,128)S(1)} async-done(((f32[32,8,128]{2,1,0:T(8,128)}), f32[32,8,128]{2,1,0:T(8,128)S(1)}, u32[]{:S(2)}, u32[]{:S(2)}) %all-to-all-start.1) | async-done | bytes 131104 | tf_op jit(solution)/shard_map/all_to_all | solution.py:532
  80.3 1.7 %top_turn.1 = f32[16,8,128]{2,1,0:T(8,128)S(1)} custom-call(f32[32,8,128]{2,1,0:T(8,128)S(1)} %all-to-all-done.1.refs_0_, f32[6,32,128]{2,1,0:T(8,128)S(1)} %copy-done.14, f32[8,32,128]{2,1,0:T(8,128)S(1)} %copy-done.28, f32[16,2048]{1,0:T(8,128)S(1)} %near_field.1.refs_3_.refs_7_, f32[30,8,128]{2,1,0:T(8,128)S(1)} %far_field.1.refs_4_.refs_5_), custom_call_target="tpu_custom_call" | custom-call | flops 2147483648 | bytes 5368709 | tf_op jit(solution)/shard_map/top_turn/pallas_call | solution.py:275
  82.0 10.8 %all_to_all.15.refs_0_ = f32[16,8,128]{2,1,0:T(8,128)S(1)} all-to-all(f32[16,8,128]{2,1,0:T(8,128)S(1)} %top_turn.1), channel_id=1, replica_groups={{0,1,2,3,4,5,6,7,8,9,10,11,12,13,14,15},{16,17,18,19,20,21,22,23,24,25,..., dimensions={0} | all-to-all | bytes 131072 | tf_op jit(solution)/shard_map/all_to_all | solution.py:560
  92.7 0.0 copy-done.20
  92.7 0.0 copy-done.30
  92.7 3.9 %downward.1 = f32[16,2048]{1,0:T(8,128)} custom-call(f32[16,8,128]{2,1,0:T(8,128)S(1)} %all_to_all.15.refs_0_, f32[4,8,128]{2,1,0:T(8,128)S(1)} %get-tuple-element.60.refs_1_, f32[12,32,128]{2,1,0:T(8,128)S(1)} %copy-done.20, f32[7,32,128]{2,1,0:T(8,128)S(1)} %copy-done.30, bf16[30,64,128]{2,1,0:T(8,128)(2,1)S(1)} %copy-done.24, ...), custom_call_target="tpu_custom_call" | custom-call | flops 4294967296 | bytes 10737418 | tf_op jit(solution)/shard_map/downward/pallas_call | solution.py:275
  (42 shorter events, 0.2 us)
Async XLA Ops:
  0.0 1.0 copy-start.4
  1.0 0.9 copy-start.5
  2.0 27.0 %copy-start.19 = (f32[12,32,128]{2,1,0:T(8,128)}, f32[12,32,128]{2,1,0:T(8,128)S(1)}, u32[]{:S(2)}) copy-start(f32[12,32,128]{2,1,0:T(8,128)S(1)} %get-tuple-element.35.refs_0_.refs_1_.refs_2_) | copy-start | bytes 589828
  2.1 9.0 %collective-permute-start.1 = (f32[8,32,128]{2,1,0:T(8,128)S(1)}, f32[8,32,128]{2,1,0:T(8,128)S(1)}, u32[]{:S(2)}, u32[]{:S(2)}) collective-permute-start(f32[8,32,128]{2,1,0:T(8,128)S(1)} %get-tuple-element.37), channel_id=1, source_target_pairs={{0,1},{16,17},{32,33},{48,49},{64,65},{80,81},{96,97},{112,113},{1... | collective-permute-start | bytes 393224 | tf_op jit(solution)/shard_map/ppermute | solution.py:294
  3.4 0.7 collective-permute-start
  11.1 29.3 %copy-start.8 = (f32[8,32,128]{2,1,0:T(8,128)}, f32[8,32,128]{2,1,0:T(8,128)S(1)}, u32[]{:S(2)}) copy-start(f32[8,32,128]{2,1,0:T(8,128)S(1)} %collective-permute-done.1.refs_2_.refs_3_.refs_1_) | copy-start | bytes 393220
  11.1 16.1 %copy-start.2 = (f32[30,4096]{1,0:T(8,128)S(1)}, f32[30,4096]{1,0:T(8,128)}, u32[]{:S(2)}) copy-start(f32[30,4096]{1,0:T(8,128)} %refs_2_.2) | copy-start | bytes 1474564
  11.1 16.1 %copy-start.3 = (f32[16,64,128]{2,1,0:T(8,128)S(1)}, f32[16,64,128]{2,1,0:T(8,128)}, u32[]{:S(2)}) copy-start(f32[16,64,128]{2,1,0:T(8,128)} %refs_6_.1) | copy-start | bytes 1572868
  11.1 16.1 %copy-start.6 = (f32[16,2048]{1,0:T(8,128)S(1)}, f32[16,2048]{1,0:T(8,128)}, u32[]{:S(2)}) copy-start(f32[16,2048]{1,0:T(8,128)} %refs_2_.3) | copy-start | bytes 393220
  11.1 3.0 %collective-permute-start.2 = (f32[3,32,128]{2,1,0:T(8,128)S(1)}, f32[3,32,128]{2,1,0:T(8,128)S(1)}, u32[]{:S(2)}, u32[]{:S(2)}) collective-permute-start(f32[3,32,128]{2,1,0:T(8,128)S(1)} %get-tuple-element.38), channel_id=1, source_target_pairs={{0,4},{8,12},{16,20},{24,28},{32,36},{40,44},{48,52},{56,60},{64,6... | collective-permute-start | bytes 147464 | tf_op jit(solution)/shard_map/ppermute | solution.py:294
  11.9 2.1 %collective-permute-start.3 = (f32[1,32,128]{2,1,0:T(8,128)S(1)}, f32[1,32,128]{2,1,0:T(8,128)S(1)}, u32[]{:S(2)}, u32[]{:S(2)}) collective-permute-start(f32[1,32,128]{2,1,0:T(8,128)S(1)} %get-tuple-element.40), channel_id=1, source_target_pairs={{1,257}} | collective-permute-start | bytes 49160 | tf_op jit(solution)/shard_map/ppermute | solution.py:294
  14.1 3.3 %collective-permute-start.4 = (f32[5,32,128]{2,1,0:T(8,128)S(1)}, f32[5,32,128]{2,1,0:T(8,128)S(1)}, u32[]{:S(2)}, u32[]{:S(2)}) collective-permute-start(f32[5,32,128]{2,1,0:T(8,128)S(1)} %get-tuple-element.41), channel_id=1, source_target_pairs={{0,2},{4,6},{8,10},{12,14},{16,18},{20,22},{24,26},{28,30},{32,34}... | collective-permute-start | bytes 245768 | tf_op jit(solution)/shard_map/ppermute | solution.py:294
  14.8 2.6 %collective-permute-start.5 = (f32[2,32,128]{2,1,0:T(8,128)S(1)}, f32[2,32,128]{2,1,0:T(8,128)S(1)}, u32[]{:S(2)}, u32[]{:S(2)}) collective-permute-start(f32[2,32,128]{2,1,0:T(8,128)S(1)} %get-tuple-element.43), channel_id=1, source_target_pairs={{1,129},{257,385}} | collective-permute-start | bytes 98312 | tf_op jit(solution)/shard_map/ppermute | solution.py:294
  16.1 12.7 %collective-permute-start.7 = (f32[6,32,128]{2,1,0:T(8,128)S(1)}, f32[6,32,128]{2,1,0:T(8,128)S(1)}, u32[]{:S(2)}, u32[]{:S(2)}) collective-permute-start(f32[6,32,128]{2,1,0:T(8,128)S(1)} %get-tuple-element.47), channel_id=1, source_target_pairs={{0,1},{16,17},{32,33},{48,49},{64,65},{80,81},{96,97},{112,113},{1... | collective-permute-start | bytes 294920 | tf_op jit(solution)/shard_map/ppermute | solution.py:294
  17.4 11.4 %collective-permute-start.8 = (f32[4,32,128]{2,1,0:T(8,128)S(1)}, f32[4,32,128]{2,1,0:T(8,128)S(1)}, u32[]{:S(2)}, u32[]{:S(2)}) collective-permute-start(f32[4,32,128]{2,1,0:T(8,128)S(1)} %get-tuple-element.49), channel_id=1, source_target_pairs={{1,65},{129,193},{257,321},{385,449}} | collective-permute-start | bytes 196616 | tf_op jit(solution)/shard_map/ppermute | solution.py:294
  25.9 3.2 %collective-permute-start.6 = (f32[7,32,128]{2,1,0:T(8,128)S(1)}, f32[7,32,128]{2,1,0:T(8,128)S(1)}, u32[]{:S(2)}, u32[]{:S(2)}) collective-permute-start(f32[7,32,128]{2,1,0:T(8,128)S(1)} %get-tuple-element.46), channel_id=1, source_target_pairs={{0,1},{2,3},{4,5},{6,7},{8,9},{10,11},{12,13},{14,15},{16,17},{18,... | collective-permute-start | bytes 344072 | tf_op jit(solution)/shard_map/ppermute | solution.py:294
  28.8 2.0 %copy-start.23 = (bf16[30,64,128]{2,1,0:T(8,128)(2,1)}, bf16[30,64,128]{2,1,0:T(8,128)(2,1)S(1)}, u32[]{:S(2)}) copy-start(bf16[30,64,128]{2,1,0:T(8,128)(2,1)S(1)} %get-tuple-element.62.refs_4_) | copy-start | bytes 1474564
  28.8 2.0 %copy-start.25 = (f32[30,8,128]{2,1,0:T(8,128)}, f32[30,8,128]{2,1,0:T(8,128)S(1)}, u32[]{:S(2)}) copy-start(f32[30,8,128]{2,1,0:T(8,128)S(1)} %get-tuple-element.59.refs_2_) | copy-start | bytes 368644
  28.8 11.6 %copy-start.12 = (f32[6,32,128]{2,1,0:T(8,128)}, f32[6,32,128]{2,1,0:T(8,128)S(1)}, u32[]{:S(2)}) copy-start(f32[6,32,128]{2,1,0:T(8,128)S(1)} %collective-permute-done.7.refs_0_.refs_1_) | copy-start | bytes 294916
  30.8 0.6 copy-start.29
  31.4 15.9 %all-to-all-start = ((f32[16,16,128]{2,1,0:T(8,128)}), f32[16,16,128]{2,1,0:T(8,128)S(1)}, u32[]{:S(2)}, u32[]{:S(2)}) async-start(f32[16,16,128]{2,1,0:T(8,128)} %get-tuple-element.51), calls=%async_computation | async-start | bytes 262144 | tf_op jit(solution)/shard_map/all_to_all | solution.py:518
  35.6 4.7 %collective-permute-start.9 = (f32[6,32,128]{2,1,0:T(8,128)S(1)}, f32[6,32,128]{2,1,0:T(8,128)S(1)}, u32[]{:S(2)}, u32[]{:S(2)}) collective-permute-start(f32[6,32,128]{2,1,0:T(8,128)S(1)} %get-tuple-element.52), channel_id=1, source_target_pairs={{1,33},{65,97},{129,161},{193,225},{257,289},{321,353},{385,417},{... | collective-permute-start | bytes 294920 | tf_op jit(solution)/shard_map/ppermute | solution.py:294
  40.4 0.6 copy-start.21
  41.0 5.6 %collective-permute-start.10 = (f32[8,32,128]{2,1,0:T(8,128)S(1)}, f32[8,32,128]{2,1,0:T(8,128)S(1)}, u32[]{:S(2)}, u32[]{:S(2)}) collective-permute-start(f32[8,32,128]{2,1,0:T(8,128)S(1)} %get-tuple-element.54), channel_id=1, source_target_pairs={{1,17},{33,49},{65,81},{97,113},{129,145},{161,177},{193,209},{225... | collective-permute-start | bytes 393224 | tf_op jit(solution)/shard_map/ppermute | solution.py:294
  42.3 23.8 %collective-permute-start.11 = (f32[46,8,128]{2,1,0:T(8,128)S(1)}, f32[46,8,128]{2,1,0:T(8,128)S(1)}, u32[]{:S(2)}, u32[]{:S(2)}) collective-permute-start(f32[46,8,128]{2,1,0:T(8,128)S(1)} %get-tuple-element.57), channel_id=1, source_target_pairs={{0,1},{1,2},{2,3},{3,4},{4,5},{5,6},{6,7},{7,8},{8,9},{9,10},{10,1... | collective-permute-start | bytes 565256 | tf_op jit(solution)/shard_map/ppermute | solution.py:294
  44.2 21.9 %collective-permute-start.12 = (f32[46,8,128]{2,1,0:T(8,128)S(1)}, f32[46,8,128]{2,1,0:T(8,128)S(1)}, u32[]{:S(2)}, u32[]{:S(2)}) collective-permute-start(f32[46,8,128]{2,1,0:T(8,128)S(1)} %get-tuple-element.58), channel_id=1, source_target_pairs={{1,0},{2,1},{3,2},{4,3},{5,4},{6,5},{7,6},{8,7},{9,8},{10,9},{11,1... | collective-permute-start | bytes 565256 | tf_op jit(solution)/shard_map/ppermute | solution.py:294
  46.7 0.7 copy-start.10
  47.3 0.9 copy-start.9
  48.2 0.9 copy-start.11
  49.1 0.9 copy-start.13
  50.0 0.9 copy-start.22
  50.9 15.2 %copy-start = (f32[16,2,128,128]{3,2,1,0:T(8,128)S(1)}, f32[16,2,128,128]{3,2,1,0:T(8,128)}, u32[]{:S(2)}) copy-start(f32[16,2,128,128]{3,2,1,0:T(8,128)} %refs_5_.1) | copy-start | bytes 6291460
  50.9 15.3 %copy-start.16 = (s32[16,2]{0,1:T(2,128)S(1)}, s32[16,2]{0,1:T(2,128)}, u32[]{:S(2)}) copy-start(s32[16,2]{0,1:T(2,128)} %param.20) | copy-start | bytes 388
  50.9 15.3 %copy-start.17 = (s32[16]{0:T(128)S(1)}, s32[16]{0:T(128)}, u32[]{:S(2)}) copy-start(s32[16]{0:T(128)} %refs_1_.4) | copy-start | bytes 196
  52.7 0.7 copy-start.27
  53.4 26.9 %all-to-all-start.1 = ((f32[32,8,128]{2,1,0:T(8,128)}), f32[32,8,128]{2,1,0:T(8,128)S(1)}, u32[]{:S(2)}, u32[]{:S(2)}) async-start(f32[32,8,128]{2,1,0:T(8,128)} %get-tuple-element.55), calls=%async_computation.1 | async-start | bytes 262144 | tf_op jit(solution)/shard_map/all_to_all | solution.py:532
  66.2 0.9 copy-start.7
  67.1 1.8 %copy-start.1 = (f32[30,3,4096]{2,0,1:T(8,128)S(1)}, f32[30,3,4096]{2,0,1:T(8,128)}, u32[]{:S(2)}) copy-start(f32[30,3,4096]{2,0,1:T(8,128)} %param.14) | copy-start | bytes 4423684
  67.1 1.8 %copy-start.15 = (s32[30,3]{0,1:T(4,128)S(1)}, s32[30,3]{0,1:T(4,128)}, u32[]{:S(2)}) copy-start(s32[30,3]{0,1:T(4,128)} %param.15) | copy-start | bytes 1084
  67.1 1.8 %copy-start.18 = (s32[30]{0:T(128)S(1)}, s32[30]{0:T(128)}, u32[]{:S(2)}) copy-start(s32[30]{0:T(128)} %refs_1_.5) | copy-start | bytes 364
  67.1 1.8 %copy-start.26 = (f32[30,8,128]{2,1,0:T(8,128)S(1)}, f32[30,8,128]{2,1,0:T(8,128)}, u32[]{:S(2)}) copy-start(f32[30,8,128]{2,1,0:T(8,128)} %copy-done.25) | copy-start | bytes 368644
  68.9 11.3 %copy-start.14 = (f32[6,32,128]{2,1,0:T(8,128)S(1)}, f32[6,32,128]{2,1,0:T(8,128)}, u32[]{:S(2)}) copy-start(f32[6,32,128]{2,1,0:T(8,128)} %copy-done.12) | copy-start | bytes 294916
  68.9 11.3 %copy-start.28 = (f32[8,32,128]{2,1,0:T(8,128)S(1)}, f32[8,32,128]{2,1,0:T(8,128)}, u32[]{:S(2)}) copy-start(f32[8,32,128]{2,1,0:T(8,128)} %copy-done.27) | copy-start | bytes 393220
  80.3 12.4 %copy-start.20 = (f32[12,32,128]{2,1,0:T(8,128)S(1)}, f32[12,32,128]{2,1,0:T(8,128)}, u32[]{:S(2)}) copy-start(f32[12,32,128]{2,1,0:T(8,128)} %copy-done.19) | copy-start | bytes 589828
  80.3 12.4 %copy-start.24 = (bf16[30,64,128]{2,1,0:T(8,128)(2,1)S(1)}, bf16[30,64,128]{2,1,0:T(8,128)(2,1)}, u32[]{:S(2)}) copy-start(bf16[30,64,128]{2,1,0:T(8,128)(2,1)} %copy-done.23) | copy-start | bytes 1474564
  80.3 12.4 %copy-start.30 = (f32[7,32,128]{2,1,0:T(8,128)S(1)}, f32[7,32,128]{2,1,0:T(8,128)}, u32[]{:S(2)}) copy-start(f32[7,32,128]{2,1,0:T(8,128)} %copy-done.29) | copy-start | bytes 344068

commit v3 on v2

v3 whole, which is shorter than its diff:
```python
import jax
import jax.numpy as jnp
from jax import lax
from jax.experimental import pallas as pl
from jax.experimental.pallas import tpu as pltpu
from jax.sharding import PartitionSpec as P

F32 = jnp.float32
BF16 = jnp.bfloat16
RANK = 64
LEAVES = 16
POINTS = 128
LOCAL = 30
SLOTS = 3
NEAR = 2
REACH = 8
GROUP_BITS = 4
TOP_BITS = 9
GROUP = 1 << GROUP_BITS
PORTER = 1
LAYOUT = ((16, 0), (8, 16), (4, 24), (2, 28))
VMEM_BYTES = 20 * 1024 * 1024
WIDE_BYTES = 63 * 1024 * 1024


def split(x):
    high = x.astype(BF16)
    return high, (x - high.astype(F32)).astype(BF16)


def lanes(rows):
    return lax.broadcasted_iota(jnp.int32, (rows, 128), 1)


def table_form(table):
    high, low = split(table)
    return jnp.concatenate([high, low, high, low], axis=0)


def coef_form(packed):
    lane = lanes(packed.shape[0])
    even = 2 * (lane % 32)
    parts = [
        jnp.take_along_axis(packed, even + shift, axis=1) for shift in (0, 64, 1, 65)
    ]
    full = jnp.concatenate(parts, axis=0)
    high, low = split(full)
    return jnp.where(lanes(full.shape[0]) < 64, high.astype(F32), low.astype(F32)).astype(BF16)


def dot(a, b):
    return lax.dot_general(a, b, (((1,), (0,)), ((), ())), preferred_element_type=F32)


def dot_t(a, b):
    return lax.dot_general(a, b, (((1,), (1,)), ((), ())), preferred_element_type=F32)


def fold(out):
    rows = out.shape[0] // 4
    left = lanes(rows) < 64
    straight = jnp.where(left, out[0:rows], out[3 * rows :])
    crossed = jnp.where(left, out[rows : 2 * rows], out[2 * rows : 3 * rows])
    return straight + pltpu.roll(crossed, 64, 1)


def times(packed, table):
    return fold(dot(coef_form(packed), table_form(table)))


def row_form(packed):
    left = lanes(8) < 64
    turned = pltpu.roll(packed, 64, 1)
    zero = jnp.zeros_like(packed)
    full = jnp.concatenate(
        [
            jnp.where(left, packed, zero),
            jnp.where(left, turned, zero),
            jnp.where(left, zero, turned),
            jnp.where(left, zero, packed),
        ],
        axis=0,
    )
    return split(full)


def weave(even_odd):
    lane = lanes(8)
    place = (lane % 64) // 2
    wide = jnp.concatenate([even_odd] * 4, axis=1)
    pick = [jnp.take_along_axis(wide[8 * k : 8 * k + 8], place, axis=1) for k in range(4)]
    even = lane % 2 == 0
    return jnp.where(
        lane < 64, jnp.where(even, pick[0], pick[2]), jnp.where(even, pick[1], pick[3])
    )


def times_t_raw(rows, high, low):
    row_high, row_low = rows
    both = dot_t(jnp.concatenate([row_high, row_low], axis=0), high)
    return both[:32] + both[32:] + dot_t(row_high, low)


def times_t(packed, table):
    high, low = split(table)
    return weave(times_t_raw(row_form(packed), high, low))


def unpack(packed):
    return jnp.concatenate([packed[:, :RANK], packed[:, RANK:]], axis=0)


def pack(value):
    return jnp.concatenate([value[:8], value[8:]], axis=1)


def place_of_device():
    device = lax.axis_index("leaf").astype(jnp.int32)
    return device, device & (GROUP - 1), device >> GROUP_BITS


def up_kernel(sources, basis, transfer, coefs, root, tables):
    table = transfer[...].reshape(LOCAL, 32, 128)
    for row in range(LOCAL):
        high, low = split(table[row])
        tables[row, 0:32] = high
        tables[row, 32:64] = low
    for leaf in range(LEAVES):
        entries = sources[:, leaf * POINTS : (leaf + 1) * POINTS]
        high, low = split(entries)
        basis_high, basis_low = split(basis[leaf])
        both = dot_t(jnp.concatenate([high, low], axis=0), basis_high)
        coefs[leaf] = pack(both[:16] + both[16:] + dot_t(high, basis_low))
    for level, (clusters, offset) in enumerate(LAYOUT):
        for parent in range(clusters // 2):
            first = offset + 2 * parent
            left = jnp.concatenate(
                [coef_form(coefs[first]), coef_form(coefs[first + 1])], axis=1
            )
            halves = [tables[first], tables[first], tables[first + 1], tables[first + 1]]
            value = fold(dot(left, jnp.concatenate(halves, axis=0)))
            if clusters > 2:
                coefs[offset + clusters + parent] = value
            else:
                root[...] = value


def edge_kernel(sources, coefs, forward, backward):
    forward[0:LOCAL] = coefs[...]
    backward[0:LOCAL] = coefs[...]
    for leaf in range(LEAVES):
        edge, place = (backward, leaf) if leaf < REACH else (forward, leaf - REACH)
        entries = sources[:, leaf * POINTS : (leaf + 1) * POINTS]
        edge[LOCAL + 2 * place] = entries[:8]
        edge[LOCAL + 2 * place + 1] = entries[8:]


def near_kernel(partner, count, own, low, high, block, out, leaves):
    for leaf in range(LEAVES):
        leaves[REACH + leaf] = own[:, leaf * POINTS : (leaf + 1) * POINTS]
    for leaf in range(REACH):
        for half in range(2):
            rows = slice(8 * half, 8 * half + 8)
            leaves[leaf, rows] = low[LOCAL + 2 * leaf + half]
            leaves[REACH + LEAVES + leaf, rows] = high[LOCAL + 2 * leaf + half]
    first = place_of_device()[0] * LEAVES - REACH
    for leaf in range(LEAVES):
        total = None
        for slot in range(NEAR):
            place = jnp.clip(partner[slot, leaf] - first, 0, LEAVES + 2 * REACH - 1)
            used = (slot < count[leaf]).astype(F32)
            picked_high, picked_low = split(leaves[place] * used)
            block_high, block_low = split(block[leaf, slot])
            both = dot_t(jnp.concatenate([picked_high, picked_low], axis=0), block_high)
            value = both[:16] + both[16:] + dot_t(picked_high, block_low)
            total = value if total is None else total + value
        out[:, leaf * POINTS : (leaf + 1) * POINTS] = total


def far_kernel(partner, count, own, low, high, coupling, out, extended):
    device = place_of_device()[0]
    extended[0:LOCAL] = low[0:LOCAL]
    extended[LOCAL : 2 * LOCAL] = own[...]
    extended[2 * LOCAL : 3 * LOCAL] = high[0:LOCAL]
    tables = [coupling[slot].reshape(LOCAL, 32, 128) for slot in range(SLOTS)]
    for clusters, offset in LAYOUT:
        for cluster in range(clusters):
            row = offset + cluster
            left = []
            right = []
            for slot in range(SLOTS):
                index = partner[slot, row]
                side = jnp.clip(index // clusters - device + 1, 0, 2)
                place = side * LOCAL + offset + index % clusters
                used = (slot < count[row]).astype(F32)
                left.append(coef_form(extended[place] * used))
                right.append(table_form(tables[slot][row]))
            out[row] = fold(dot(jnp.concatenate(left, axis=1), jnp.concatenate(right, axis=0)))


def call(kernel, name, outs, args, lazy=(), scalars=0, scratch=(), after=(), flops=0):
    vmem = pl.BlockSpec(memory_space=pltpu.VMEM)
    smem = pl.BlockSpec(memory_space=pltpu.SMEM)
    spare = pl.BlockSpec(memory_space=pl.ANY)
    given, slow, spares = len(args), len(lazy), len(after)

    def body(*refs):
        own = refs[given + slow + spares :]
        copies = []
        getters = []
        if slow:
            own, targets, semaphores = own[: -slow - 1], own[-slow - 1 : -1], own[-1]
            for i, target in enumerate(targets):
                copies.append(
                    pltpu.make_async_copy(refs[given + i], target, semaphores.at[i])
                )
                copies[-1].start()
            waiting = set(range(slow))

            def getter(i):
                def get():
                    if i in waiting:
                        waiting.remove(i)
                        copies[i].wait()
                    return targets[i]

                return get

            getters = [getter(i) for i in range(slow)]
        kernel(*refs[:given], *getters, *own)
        for get in getters:
            get()

    buffers = [pltpu.VMEM(item.shape, item.dtype) for item in lazy]
    if lazy:
        buffers.append(pltpu.SemaphoreType.DMA((slow,)))
    result = pl.pallas_call(
        body,
        out_shape=list(outs),
        in_specs=[smem] * scalars + [vmem] * (given - scalars) + [spare] * (slow + spares),
        out_specs=[vmem] * len(outs),
        scratch_shapes=list(scratch) + buffers,
        compiler_params=pltpu.CompilerParams(
            vmem_limit_bytes=WIDE_BYTES if lazy else VMEM_BYTES
        ),
        cost_estimate=pl.CostEstimate(
            flops=flops, bytes_accessed=flops // 400, transcendentals=0
        ),
        name=name,
    )(*args, *lazy, *after)
    return result if len(result) > 1 else result[0]


def shape(*dims, dtype=F32):
    return jax.ShapeDtypeStruct(dims, dtype)


def permute(value, pairs):
    return lax.ppermute(value, "leaf", pairs)


def tables(size):
    return shape(size, 32, 128)


def prepare_kernel(transfers, couplings, group_raw, high_raw, low_raw, group_pay):

    def coupling(level, side):
        return couplings[level - 1, :, side, :]

    group_pay[0] = coupling(GROUP_BITS, 1)
    high_raw[0] = transfers[7]
    low_raw[0:3] = transfers[4:7]
    for side in range(2):
        for level in range(7, 10):
            high_raw[1 + 3 * side + level - 7] = coupling(level, side)
        for level in range(5, 7):
            low_raw[3 + 2 * side + level - 5] = coupling(level, side)
        for level in range(1, 5):
            group_raw[4 + 4 * side + level - 1] = coupling(level, side)
    group_raw[0:4] = transfers[0:4]


def choose(flag, first, second):
    return jnp.where(flag, first, second)


def merge_group(raw, bit, live, arrived, out):
    _, member, _ = place_of_device()
    right_child = ((member >> bit) & 1) == 1
    size = out.shape[0]
    start = 0
    if bit + 1 < GROUP_BITS:
        out[0] = choose(right_child, arrived[0], raw[bit + 1])
        start = 1
    for entry in range(start, size - 1):
        out[entry] = choose(right_child, arrived[entry], live[entry - start])
    out[size - 1] = choose(right_child, arrived[size - 1], raw[GROUP_BITS + bit])


def group_payload(raw, bit, live, pay):
    pay[0] = raw[bit + 1]
    size = live.shape[0]
    pay[1 : 1 + size] = live[...]
    pay[1 + size] = raw[2 * GROUP_BITS + bit]


def first_kernel(raw, arrived, high_raw, live, pay, high_pay):
    merge_group(raw, 3, None, arrived, live)
    group_payload(raw, 2, live, pay)
    high_pay[0] = high_raw[6]


def second_kernel(
    raw, arrived, live, low_raw, high_raw, high_in, out, pay, high_live, high_pay, low_pay
):
    merge_group(raw, 2, live, arrived, out)
    group_payload(raw, 1, out, pay)
    _, _, group = place_of_device()
    value = choose(((group >> 4) & 1) == 1, high_in[0], high_raw[3])
    high_live[0] = value
    high_pay[0] = value
    high_pay[1] = high_raw[5]
    low_pay[0] = low_raw[2]
    low_pay[1] = low_raw[6]


def line_kernel(high_raw, high_in, high_live, upper, high_pay):
    _, _, group = place_of_device()
    right_child = ((group >> 3) & 1) == 1
    ninth = choose(right_child, high_in[0], high_live[0])
    eighth = choose(right_child, high_in[1], high_raw[2])
    for target, side in ((upper, 1), (high_pay, 4)):
        target[0] = high_raw[0]
        target[1] = ninth
        target[2] = eighth
        target[3] = high_raw[side]


def third_kernel(raw, arrived, live, low_raw, low_in, out, pay, keep, low_pay):
    merge_group(raw, 1, live, arrived, out)
    group_payload(raw, 0, out, pay)
    _, _, group = place_of_device()
    second = ((group >> 1) & 1) == 1
    sixth = choose(second, low_in[0], low_raw[2])
    sixth_coupling = choose(second, low_in[1], low_raw[4])
    for target, side in ((keep, 3), (low_pay, 5)):
        target[0] = sixth
        target[1] = sixth_coupling
        target[2] = low_raw[1]
        target[3] = low_raw[side]
    keep[4] = low_raw[0]


def fourth_kernel(upper, near_in, far_in, out):
    _, _, group = place_of_device()
    place = group & 7
    for entry in range(4):
        out[entry] = choose(
            place == 2, near_in[entry], choose(place == 6, far_in[entry], upper[entry])
        )


def share_kernel(root, raw, live, arrived, blocks, table, chain):
    _, member, _ = place_of_device()
    merge_group(raw, 0, live, arrived, table)
    value = root[...]
    chain[0] = value
    for level in range(GROUP_BITS):
        value = times(value, raw[0] if level == 0 else table[level - 1])
        if level + 1 < GROUP_BITS:
            chain[level + 1] = value
    for other in range(GROUP):
        apart = member ^ other
        level = sum((apart >= (1 << bit)).astype(jnp.int32) for bit in range(1, GROUP_BITS))
        blocks[other, 0:8] = chain[level]
        blocks[other, 8:16] = value


def total_of(pieces):
    total = pieces[0]
    for piece in pieces[1:]:
        total = total + piece
    return total


def rise_kernel(given, keep, near_in, blocks, sibling, table, chain):
    _, member, group = place_of_device()
    place = group & 7
    odd = (place & 1) == 1
    for entry in range(4):
        table[entry] = choose(odd, near_in[entry], keep[entry])
    table[4] = keep[4]
    for level in range(GROUP_BITS):
        sibling[level] = total_of(
            [given[member ^ apart, 0:8] for apart in range(1 << level, 2 << level)]
        )
    value = total_of([given[other, 8:16] for other in range(GROUP)])
    chain[0] = value
    for level in range(3):
        value = times(value, table[4 - 2 * level])
        chain[level + 1] = value
    for other in range(8):
        apart = place ^ other
        level = sum((apart >= (1 << bit)).astype(jnp.int32) for bit in range(1, 3))
        blocks[other, 0:8] = chain[level]
        blocks[other, 8:16] = value


def fifth_kernel(upper, near_in, far_in, out):
    _, _, group = place_of_device()
    place = group & 7
    for entry in range(4):
        out[entry] = choose(
            (place & 1) == 1, near_in[entry], choose(place == 4, far_in[entry], upper[entry])
        )


def middle_kernel(given, upper, arrived, blocks, upper_out, sums):
    _, _, group = place_of_device()
    place, line = group & 7, group >> 3
    for level in range(3):
        sums[level] = total_of(
            [given[place ^ apart, 0:8] for apart in range(1 << level, 2 << level)]
        )
    value = total_of([given[other, 8:16] for other in range(8)])
    table = upper_out
    for entry in range(4):
        table[entry] = choose(place == 5, arrived[entry], upper[entry])
    raised = times(value, table[0])
    for other in range(4):
        blocks[other] = choose((line ^ other) >= 2, raised, value)


def top_sums_kernel(low, upper, sums, out):
    value = times(sums[2], upper[3])
    value = times_t(value, low[2]) + times(sums[1], low[1])
    out[0:8] = times_t(value, low[4]) + times(sums[0], low[3])
    out[8:40] = times(times(low[4], low[2]), low[0])
    for entry in range(3):
        out[40 + 32 * entry : 72 + 32 * entry] = upper[entry]


def turn_kernel(given, prepared, out):
    _, _, group = place_of_device()
    line = group >> 3
    seventh = times(given[line ^ 1], prepared[104:136])
    eighth = times(given[line ^ 2] + given[line ^ 3], prepared[72:104])
    value = times_t(eighth, prepared[40:72]) + seventh
    value = times_t(value, prepared[8:40]) + prepared[0:8]
    for other in range(GROUP):
        out[other] = value


def group_sums_kernel(sibling, raw, table, out):
    terms = [
        times(sibling[level], table[2 * GROUP_BITS - 2 - level]) for level in range(GROUP_BITS)
    ]
    value = terms[GROUP_BITS - 1]
    product = raw[0]
    for level in range(GROUP_BITS - 2, -1, -1):
        value = times_t(value, raw[0] if level == 0 else table[level - 1]) + terms[level]
    for level in range(1, GROUP_BITS):
        product = times(product, table[level - 1])
    out[0:8] = value
    out[8:40] = product


def down_kernel(given, prepared, forms, far, basis, near, out):
    prepared = prepared()
    value = times_t(given[PORTER], prepared[8:40]) + prepared[0:8]
    parents = [value]
    forms, far = forms(), far()
    for clusters, offset in reversed(LAYOUT):
        following = []
        for parent in range(clusters // 2):
            first = offset + 2 * parent
            high = jnp.concatenate([forms[first, 0:32], forms[first + 1, 0:32]], axis=0)
            low = jnp.concatenate([forms[first, 32:64], forms[first + 1, 32:64]], axis=0)
            out_pair = times_t_raw(row_form(parents[parent]), high, low)
            following.append(weave(out_pair[:, 0:32]) + far[first])
            following.append(weave(out_pair[:, 32:64]) + far[first + 1])
        parents = following
    basis, near = basis(), near()
    for leaf in range(LEAVES):
        high, low = split(unpack(parents[leaf]))
        basis_high, basis_low = split(basis[leaf])
        both = dot(jnp.concatenate([high, low], axis=0), basis_high)
        place = slice(leaf * POINTS, (leaf + 1) * POINTS)
        out[:, place] = both[:16] + both[16:] + dot(high, basis_low) + near[:, place]


def on_device(
    sources,
    leaf_cluster_basis,
    local_transfer,
    far_coupling,
    far_partner,
    far_count,
    top_transfer,
    top_coupling,
    near_block,
    near_partner,
    near_count,
):
    count = lax.axis_size("leaf")
    forward = [(i, i + 1) for i in range(count - 1)]
    backward = [(i + 1, i) for i in range(count - 1)]

    def handed(value, period, first, second):
        return permute(value, [(i + first, i + second) for i in range(0, count, period)])

    transfers = top_transfer.reshape(TOP_BITS, 32, 128)
    couplings = top_coupling.reshape(TOP_BITS, 2, 32, 128).transpose(0, 2, 1, 3)
    raw, high_raw, low_raw, pay = call(
        prepare_kernel,
        "top_tables",
        [tables(12), tables(7), tables(7), tables(1)],
        [transfers, couplings],
        flops=1 << 30,
    )
    high_raw = handed(high_raw, GROUP, 0, PORTER)
    group_in = handed(pay, 16, 0, 8)
    low_raw = handed(low_raw, GROUP, 0, PORTER)

    coefs, root, forms = call(
        up_kernel,
        "upward",
        [
            shape(LOCAL, 8, 128),
            shape(8, 128),
            shape(LOCAL, 64, 128, dtype=BF16),
        ],
        [sources, leaf_cluster_basis, local_transfer],
        flops=2 << 30,
    )
    live, pay, high_pay = call(
        first_kernel,
        "hand_down_1",
        [tables(1), tables(3), tables(1)],
        [raw, group_in, high_raw],
        flops=1 << 29,
    )
    group_in = handed(pay, 8, 0, 4)
    high_in = handed(high_pay, 512, PORTER, 256 + PORTER)
    live, pay, high_live, high_pay, low_pay = call(
        second_kernel,
        "hand_down_2",
        [tables(3), tables(5), tables(1), tables(2), tables(2)],
        [raw, group_in, live, low_raw, high_raw, high_in],
        after=[root],
        flops=1 << 29,
    )
    group_in = handed(pay, 4, 0, 2)
    high_in = handed(high_pay, 256, PORTER, 128 + PORTER)
    low_in = handed(low_pay, 64, PORTER, 32 + PORTER)
    upper, high_pay = call(
        line_kernel,
        "hand_down_line",
        [tables(4), tables(4)],
        [high_raw, high_in, high_live],
        flops=1 << 29,
    )
    near_in = handed(upper, 128, PORTER, 32 + PORTER)
    far_in = handed(high_pay, 128, PORTER, 96 + PORTER)
    upper = call(
        fourth_kernel, "hand_down_4", [tables(4)], [upper, near_in, far_in], flops=1 << 29
    )
    live, pay, keep, low_pay = call(
        third_kernel,
        "hand_down_3",
        [tables(5), tables(7), tables(5), tables(4)],
        [raw, group_in, live, low_raw, low_in],
        after=[upper],
        flops=1 << 29,
    )
    group_in = handed(pay, 2, 0, 1)
    low_in = handed(low_pay, 32, PORTER, 16 + PORTER)
    near_in = handed(upper, 32, PORTER, 16 + PORTER)
    far_in = handed(upper, 128, 96 + PORTER, 64 + PORTER)
    upper = call(
        fifth_kernel,
        "hand_down_5",
        [tables(4)],
        [upper, near_in, far_in],
        flops=1 << 29,
    )
    shares, group_table = call(
        share_kernel,
        "group_shares",
        [shape(GROUP, 16, 128), tables(7)],
        [root, raw, live, group_in],
        scratch=[pltpu.VMEM((GROUP_BITS, 8, 128), F32)],
        after=[upper],
        flops=2 << 30,
    )
    in_group = [list(range(first, first + GROUP)) for first in range(0, count, GROUP)]
    in_column = [
        list(range(line + member, line + 128, GROUP))
        for line in range(0, count, 128)
        for member in range(GROUP)
    ]
    in_line = [list(range(first, count, 128)) for first in range(128)]
    given = lax.all_to_all(shares, "leaf", 0, 0, axis_index_groups=in_group)
    blocks, sibling, low_table = call(
        rise_kernel,
        "column_shares",
        [shape(8, 16, 128), shape(GROUP_BITS, 8, 128), tables(5)],
        [given, keep, low_in],
        scratch=[pltpu.VMEM((4, 8, 128), F32)],
        flops=2 << 30,
    )
    given = lax.all_to_all(blocks, "leaf", 0, 0, axis_index_groups=in_column)
    low_edge, high_edge = call(
        edge_kernel,
        "edges",
        [shape(LOCAL + 2 * REACH, 8, 128)] * 2,
        [sources, coefs],
        after=[blocks],
        flops=1 << 29,
    )
    low_edge = permute(low_edge, forward)
    high_edge = permute(high_edge, backward)
    upper_in = handed(upper, 128, 64 + PORTER, 80 + PORTER)
    blocks, upper, sums = call(
        middle_kernel,
        "line_shares",
        [shape(4, 8, 128), tables(4), shape(3, 8, 128)],
        [given, upper, upper_in],
        flops=1 << 30,
    )
    given = lax.all_to_all(blocks, "leaf", 0, 0, axis_index_groups=in_line)

    near = call(
        near_kernel,
        "near_field",
        [shape(16, LEAVES * POINTS)],
        [near_partner.T, near_count, sources, low_edge, high_edge, near_block],
        scalars=2,
        scratch=[pltpu.VMEM((LEAVES + 2 * REACH, 16, POINTS), F32)],
        flops=2 << 30,
    )
    far = call(
        far_kernel,
        "far_field",
        [shape(LOCAL, 8, 128)],
        [far_partner.T, far_count, coefs, low_edge, high_edge, far_coupling.transpose(1, 0, 2)],
        scalars=2,
        scratch=[pltpu.VMEM((3 * LOCAL, 8, 128), F32)],
        after=[blocks],
        flops=2 << 30,
    )
    prepared = call(
        top_sums_kernel,
        "top_sums",
        [shape(136, 128)],
        [low_table, upper, sums],
        flops=1 << 30,
    )
    turned = call(
        turn_kernel,
        "top_turn",
        [shape(GROUP, 8, 128)],
        [given, prepared],
        after=[far],
        flops=2 << 30,
    )
    prepared = call(
        group_sums_kernel,
        "group_sums",
        [shape(40, 128)],
        [sibling, raw, group_table],
        flops=1 << 30,
    )
    given = lax.all_to_all(turned, "leaf", 0, 0, axis_index_groups=in_group)
    return call(
        down_kernel,
        "downward",
        [shape(16, LEAVES * POINTS)],
        [given],
        lazy=[prepared, forms, far, leaf_cluster_basis, near],
        flops=4 << 30,
    )


def solution(mesh):
    placed = (
        P(None, "leaf"),
        P("leaf", None, None),
        P("leaf", None),
        P("leaf", None, None),
        P("leaf", None),
        P("leaf"),
        P("leaf", None, None),
        P("leaf", None, None, None),
        P("leaf", None, None, None),
        P("leaf", None),
        P("leaf"),
    )
    return jax.shard_map(
        on_device, mesh=mesh, in_specs=placed, out_specs=P(None, "leaf"), check_vma=False
    )
```

time: 97.3 us -> 95.1 us (0.977)
  blocking collectives: 10.8 us -> 0 us
  starting transfers between devices: 42.7 us -> 49.6 us
  local copies, waits for them, and re-layouts: 9.03 us -> 3.84 us
  Pallas kernels: 14.6 us -> 18.4 us
  waiting for transfers between devices: 19.2 us -> 22.1 us
    all_to_all x1 -> x0, blocking collectives: 10.8 us -> none  [on_device(): given = lax.all_to_all(turned, 'leaf', 0, 0, axis_index_groups=in_group)]
    all_to_all x2 -> x4, starting transfers between devices: 17 us -> 24.4 us  [the longest x1 9.63 us: on_device(): given = lax.all_to_all(blocks, 'leaf', 0, 0, axis_index_groups=in_column)]
    unnamed x62 -> x32, local copies, waits for them, and re-layouts: 9.03 us -> 3.84 us
    pallas_call x13 -> x18, Pallas kernels: 14.6 us -> 18.4 us  [call(): pl.pallas_call(body, out_shape=list(outs), in_specs=[smem] * scalars + [v...]
    all_to_all x2 -> x4, waiting for transfers between devices: 9.46 us -> 12.2 us  [the longest x1 6.81 us: on_device(): given = lax.all_to_all(blocks, 'leaf', 0, 0, axis_index_groups=in_column)]
    ppermute x13 -> x17, starting transfers between devices: 25.7 us -> 25.2 us  [permute(): return lax.ppermute(value, 'leaf', pairs)]
    ppermute x13 -> x17, waiting for transfers between devices: 9.76 us -> 9.92 us  [permute(): return lax.ppermute(value, 'leaf', pairs)]
  transfers between devices with their start and end apart: 15 -> 21, of which waited for: 5 -> 8; matrix products, arithmetic and copies ran while one was open for 0% -> 0% of each run, Pallas kernels for 7% -> 9%
where the time goes in v3:
time: 95.1 us; the launch traced here: 94.3 us
  starting transfers between devices  49.6 us (52%)
  waiting for transfers between devices  22.1 us (23%)
  Pallas kernels  18.4 us (19%)
  local copies, waits for them, and re-layouts  3.84 us (4%)
    ppermute x17, starting transfers between devices, permute(): return lax.ppermute(value, 'leaf', pairs)  25.2 us
    pallas_call x18, Pallas kernels, call(): pl.pallas_call(body, out_shape=list(outs), in_specs=[smem] * scalars + [v...  18.4 us
    ppermute x17, waiting for transfers between devices, permute(): return lax.ppermute(value, 'leaf', pairs)  9.92 us
    all_to_all x1, starting transfers between devices, on_device(): given = lax.all_to_all(blocks, 'leaf', 0, 0, axis_index_groups=in_column)  9.63 us
    all_to_all x1, starting transfers between devices, on_device(): given = lax.all_to_all(turned, 'leaf', 0, 0, axis_index_groups=in_group)  7.14 us
    all_to_all x1, waiting for transfers between devices, on_device(): given = lax.all_to_all(blocks, 'leaf', 0, 0, axis_index_groups=in_column)  6.81 us
    all_to_all x1, starting transfers between devices, on_device(): given = lax.all_to_all(blocks, 'leaf', 0, 0, axis_index_groups=in_line)  4.18 us
    unnamed x32, local copies, waits for them, and re-layouts  3.84 us
  transfers between devices with their start and end apart: 21, of which 8 were waited for; matrix products, arithmetic and copies ran while one was open for 0% of the time, Pallas kernels for 9%

profile of v3, /device:TPU:1, one launch (start us, length us, event | category | flops | bytes accessed | tf_op | source)
XLA Modules:
  0.0 94.3 jit_solution(14113770599828387458)
XLA Ops:
  0.0 1.0 %copy-done.4 = f32[1,9,2,4096]{3,2,1,0:T(2,128)S(1)} copy-done((f32[1,9,2,4096]{3,2,1,0:T(2,128)S(1)}, f32[1,9,2,4096]{3,2,1,0:T(2,128)}, u32[]{:S(2)}) %copy-start.4) | copy-done | bytes 294936
  1.0 0.9 copy-done.5
  1.9 0.2 top_tables.1
  2.1 1.4 %collective-permute-start.1 = (f32[7,32,128]{2,1,0:T(8,128)S(1)}, f32[7,32,128]{2,1,0:T(8,128)S(1)}, u32[]{:S(2)}, u32[]{:S(2)}) collective-permute-start(f32[7,32,128]{2,1,0:T(8,128)S(1)} %get-tuple-element.39), channel_id=1, source_target_pairs={{0,1},{16,17},{32,33},{48,49},{64,65},{80,81},{96,97},{112,113},{1... | collective-permute-start | bytes 344072 | tf_op jit(solution)/shard_map/ppermute | solution.py:259
  3.5 0.7 collective-permute-start
  4.2 1.3 %collective-permute-start.3 = (f32[7,32,128]{2,1,0:T(8,128)S(1)}, f32[7,32,128]{2,1,0:T(8,128)S(1)}, u32[]{:S(2)}, u32[]{:S(2)}) collective-permute-start(f32[7,32,128]{2,1,0:T(8,128)S(1)} %get-tuple-element.42), channel_id=1, source_target_pairs={{0,1},{16,17},{32,33},{48,49},{64,65},{80,81},{96,97},{112,113},{1... | collective-permute-start | bytes 344072 | tf_op jit(solution)/shard_map/ppermute | solution.py:259
  5.5 0.0 collective-permute-done.refs_1_
  5.5 5.7 %collective-permute-done.1.refs_2_.refs_4_.refs_0_ = f32[7,32,128]{2,1,0:T(8,128)S(1)} collective-permute-done((f32[7,32,128]{2,1,0:T(8,128)S(1)}, f32[7,32,128]{2,1,0:T(8,128)S(1)}, u32[]{:S(2)}, u32[]{:S(2)}) %collective-permute-start.1) | collective-permute-done | bytes 114720 | tf_op jit(solution)/shard_map/ppermute | solution.py:259
  11.2 0.7 collective-permute-start.2
  11.8 1.3 %collective-permute-start.4 = (f32[1,32,128]{2,1,0:T(8,128)S(1)}, f32[1,32,128]{2,1,0:T(8,128)S(1)}, u32[]{:S(2)}, u32[]{:S(2)}) collective-permute-start(f32[1,32,128]{2,1,0:T(8,128)S(1)} %get-tuple-element.43), channel_id=1, source_target_pairs={{1,257}} | collective-permute-start | bytes 49160 | tf_op jit(solution)/shard_map/ppermute | solution.py:259
  13.1 0.0 copy-done.2
  13.2 0.0 copy-done.3
  13.2 0.0 copy-done.6
  13.2 1.6 %upward.1 = (f32[30,8,128]{2,1,0:T(8,128)S(1)}, f32[8,128]{1,0:T(8,128)S(1)}, bf16[30,64,128]{2,1,0:T(8,128)(2,1)S(1)}) custom-call(f32[16,2048]{1,0:T(8,128)S(1)} %copy-done.6, f32[16,64,128]{2,1,0:T(8,128)S(1)} %copy-done.3, f32[30,4096]{1,0:T(8,128)S(1)} %copy-done.2), custom_call_target="tpu_custom_call" | custom-call | flops 2147483648 | bytes 5368709 | tf_op jit(solution)/shard_map/upward/pallas_call | solution.py:237
  14.7 0.0 collective-permute-done.3.refs_3_
  14.7 0.0 collective-permute-done.4.refs_5_
  14.8 0.0 collective-permute-done.2.refs_1_
  14.8 1.3 %collective-permute-start.7 = (f32[2,32,128]{2,1,0:T(8,128)S(1)}, f32[2,32,128]{2,1,0:T(8,128)S(1)}, u32[]{:S(2)}, u32[]{:S(2)}) collective-permute-start(f32[2,32,128]{2,1,0:T(8,128)S(1)} %get-tuple-element.47), channel_id=1, source_target_pairs={{1,129},{257,385}} | collective-permute-start | bytes 98312 | tf_op jit(solution)/shard_map/ppermute | solution.py:259
  16.1 1.0 %collective-permute-done.7.refs_1_ = f32[2,32,128]{2,1,0:T(8,128)S(1)} collective-permute-done((f32[2,32,128]{2,1,0:T(8,128)S(1)}, f32[2,32,128]{2,1,0:T(8,128)S(1)}, u32[]{:S(2)}, u32[]{:S(2)}) %collective-permute-start.7) | collective-permute-done | bytes 32800 | tf_op jit(solution)/shard_map/ppermute | solution.py:259
  17.1 2.7 %collective-permute-start.8 = (f32[4,32,128]{2,1,0:T(8,128)S(1)}, f32[4,32,128]{2,1,0:T(8,128)S(1)}, u32[]{:S(2)}, u32[]{:S(2)}) collective-permute-start(f32[4,32,128]{2,1,0:T(8,128)S(1)} %get-tuple-element.49.refs_0_), channel_id=1, source_target_pairs={{1,33},{129,161},{257,289},{385,417}} | collective-permute-start | bytes 196616 | tf_op jit(solution)/shard_map/ppermute | solution.py:259
  19.9 3.4 %collective-permute-start.9 = (f32[4,32,128]{2,1,0:T(8,128)S(1)}, f32[4,32,128]{2,1,0:T(8,128)S(1)}, u32[]{:S(2)}, u32[]{:S(2)}) collective-permute-start(f32[4,32,128]{2,1,0:T(8,128)S(1)} %get-tuple-element.50), channel_id=1, source_target_pairs={{1,97},{129,225},{257,353},{385,481}} | collective-permute-start | bytes 196616 | tf_op jit(solution)/shard_map/ppermute | solution.py:259
  23.3 0.7 collective-permute-start.5
  23.9 1.3 %collective-permute-start.6 = (f32[2,32,128]{2,1,0:T(8,128)S(1)}, f32[2,32,128]{2,1,0:T(8,128)S(1)}, u32[]{:S(2)}, u32[]{:S(2)}) collective-permute-start(f32[2,32,128]{2,1,0:T(8,128)S(1)} %get-tuple-element.46), channel_id=1, source_target_pairs={{1,33},{65,97},{129,161},{193,225},{257,289},{321,353},{385,417},{... | collective-permute-start | bytes 98312 | tf_op jit(solution)/shard_map/ppermute | solution.py:259
  25.2 0.0 collective-permute-done.8.refs_1_
  25.2 0.0 collective-permute-done.9.refs_2_
  25.3 1.3 %collective-permute-start.11 = (f32[4,32,128]{2,1,0:T(8,128)S(1)}, f32[4,32,128]{2,1,0:T(8,128)S(1)}, u32[]{:S(2)}, u32[]{:S(2)}) collective-permute-start(f32[4,32,128]{2,1,0:T(8,128)S(1)} %hand_down_4.1.refs_5_.refs_0_), channel_id=1, source_target_pairs={{1,17},{33,49},{65,81},{97,113},{129,145},{161,177},{193,209},{225... | collective-permute-start | bytes 196616 | tf_op jit(solution)/shard_map/ppermute | solution.py:259
  26.6 0.7 collective-permute-start.12
  27.3 0.0 collective-permute-done.6.refs_4_
  27.3 0.0 collective-permute-done.5.refs_1_
  27.3 1.3 %collective-permute-start.10 = (f32[7,32,128]{2,1,0:T(8,128)S(1)}, f32[7,32,128]{2,1,0:T(8,128)S(1)}, u32[]{:S(2)}, u32[]{:S(2)}) collective-permute-start(f32[7,32,128]{2,1,0:T(8,128)S(1)} %get-tuple-element.52), channel_id=1, source_target_pairs={{0,1},{2,3},{4,5},{6,7},{8,9},{10,11},{12,13},{14,15},{16,17},{18,... | collective-permute-start | bytes 344072 | tf_op jit(solution)/shard_map/ppermute | solution.py:259
  28.6 0.0 collective-permute-done.11.refs_1_
  28.6 0.0 collective-permute-done.12.refs_2_
  28.7 1.9 %collective-permute-done.10.refs_3_ = f32[7,32,128]{2,1,0:T(8,128)S(1)} collective-permute-done((f32[7,32,128]{2,1,0:T(8,128)S(1)}, f32[7,32,128]{2,1,0:T(8,128)S(1)}, u32[]{:S(2)}, u32[]{:S(2)}) %collective-permute-start.10) | collective-permute-done | bytes 114720 | tf_op jit(solution)/shard_map/ppermute | solution.py:259
  30.6 1.7 %group_shares.1 = (f32[16,16,128]{2,1,0:T(8,128)}, f32[7,32,128]{2,1,0:T(8,128)S(1)}) custom-call(f32[8,128]{1,0:T(8,128)S(1)} %get-tuple-element.36.refs_6_.refs_0_, f32[12,32,128]{2,1,0:T(8,128)S(1)} %get-tuple-element.37.refs_0_.refs_1_, f32[5,32,128]{2,1,0:T(8,128)S(1)} %get-tuple-element.51.refs_2_, f32[7,32,128]{2,1,0:T(8,128)S(1)} %collective-permute-done.10.refs_3_, ...), custom_call_target="tpu_custom_call" | custom-call | flops 2147483648 | bytes 5368709 | tf_op jit(solution)/shard_map/group_shares/pallas_call | solution.py:237
  32.3 3.5 %all-to-all-start = ((f32[16,16,128]{2,1,0:T(8,128)}), f32[16,16,128]{2,1,0:T(8,128)S(1)}, u32[]{:S(2)}, u32[]{:S(2)}) async-start(f32[16,16,128]{2,1,0:T(8,128)} %get-tuple-element.53), calls=%async_computation | async-start | bytes 262144 | tf_op jit(solution)/shard_map/all_to_all | solution.py:604
  35.7 2.0 %collective-permute-start.13 = (f32[4,32,128]{2,1,0:T(8,128)S(1)}, f32[4,32,128]{2,1,0:T(8,128)S(1)}, u32[]{:S(2)}, u32[]{:S(2)}) collective-permute-start(f32[4,32,128]{2,1,0:T(8,128)S(1)} %get-tuple-element.55), channel_id=1, source_target_pairs={{1,17},{33,49},{65,81},{97,113},{129,145},{161,177},{193,209},{225... | collective-permute-start | bytes 196616 | tf_op jit(solution)/shard_map/ppermute | solution.py:259
  37.7 1.3 %collective-permute-done.13.refs_2_ = f32[4,32,128]{2,1,0:T(8,128)S(1)} collective-permute-done((f32[4,32,128]{2,1,0:T(8,128)S(1)}, f32[4,32,128]{2,1,0:T(8,128)S(1)}, u32[]{:S(2)}, u32[]{:S(2)}) %collective-permute-start.13) | collective-permute-done | bytes 65568 | tf_op jit(solution)/shard_map/ppermute | solution.py:259
  39.0 3.0 %all-to-all-done.refs_0_ = f32[16,16,128]{2,1,0:T(8,128)S(1)} async-done(((f32[16,16,128]{2,1,0:T(8,128)}), f32[16,16,128]{2,1,0:T(8,128)S(1)}, u32[]{:S(2)}, u32[]{:S(2)}) %all-to-all-start) | async-done | bytes 131104 | tf_op jit(solution)/shard_map/all_to_all | solution.py:604
  41.9 1.4 %column_shares.1 = (f32[8,16,128]{2,1,0:T(8,128)}, f32[4,8,128]{2,1,0:T(8,128)S(1)}, f32[5,32,128]{2,1,0:T(8,128)S(1)}) custom-call(f32[16,16,128]{2,1,0:T(8,128)S(1)} %all-to-all-done.refs_0_, f32[5,32,128]{2,1,0:T(8,128)S(1)} %get-tuple-element.54.refs_1_, f32[4,32,128]{2,1,0:T(8,128)S(1)} %collective-permute-done.13.refs_2_), custom_call_target="tpu_custom_call" | custom-call | flops 2147483648 | bytes 5368709 | tf_op jit(solution)/shard_map/column_shares/pallas_call | solution.py:237
  43.4 9.6 %all-to-all-start.1 = ((f32[8,16,128]{2,1,0:T(8,128)}), f32[8,16,128]{2,1,0:T(8,128)S(1)}, u32[]{:S(2)}, u32[]{:S(2)}) async-start(f32[8,16,128]{2,1,0:T(8,128)} %get-tuple-element.56.refs_2_), calls=%async_computation.1 | async-start | bytes 131072 | tf_op jit(solution)/shard_map/all_to_all | solution.py:613
  53.0 0.0 copy-start.1
  53.1 0.0 copy-start.7
  53.1 0.0 copy-start.9
  53.1 2.7 %collective-permute-start.15 = (f32[46,8,128]{2,1,0:T(8,128)S(1)}, f32[46,8,128]{2,1,0:T(8,128)S(1)}, u32[]{:S(2)}, u32[]{:S(2)}) collective-permute-start(f32[46,8,128]{2,1,0:T(8,128)S(1)} %get-tuple-element.62), channel_id=1, source_target_pairs={{0,1},{1,2},{2,3},{3,4},{4,5},{5,6},{6,7},{7,8},{8,9},{9,10},{10,1... | collective-permute-start | bytes 565256 | tf_op jit(solution)/shard_map/ppermute | solution.py:259
  55.8 1.9 %collective-permute-start.16 = (f32[46,8,128]{2,1,0:T(8,128)S(1)}, f32[46,8,128]{2,1,0:T(8,128)S(1)}, u32[]{:S(2)}, u32[]{:S(2)}) collective-permute-start(f32[46,8,128]{2,1,0:T(8,128)S(1)} %get-tuple-element.63), channel_id=1, source_target_pairs={{1,0},{2,1},{3,2},{4,3},{5,4},{6,5},{7,6},{8,7},{9,8},{10,9},{11,1... | collective-permute-start | bytes 565256 | tf_op jit(solution)/shard_map/ppermute | solution.py:259
  57.7 0.7 collective-permute-start.14
  58.4 0.0 collective-permute-done.14.refs_2_
  58.4 6.8 %all-to-all-done.1.refs_0_ = f32[8,16,128]{2,1,0:T(8,128)S(1)} async-done(((f32[8,16,128]{2,1,0:T(8,128)}), f32[8,16,128]{2,1,0:T(8,128)S(1)}, u32[]{:S(2)}, u32[]{:S(2)}) %all-to-all-start.1) | async-done | bytes 65568 | tf_op jit(solution)/shard_map/all_to_all | solution.py:613
  65.2 0.9 line_shares.1
  66.1 4.2 %all-to-all-start.2 = ((f32[4,8,128]{2,1,0:T(8,128)}), f32[4,8,128]{2,1,0:T(8,128)S(1)}, u32[]{:S(2)}, u32[]{:S(2)}) async-start(f32[4,8,128]{2,1,0:T(8,128)} %get-tuple-element.57.refs_6_), calls=%async_computation.2 | async-start | bytes 32768 | tf_op jit(solution)/shard_map/all_to_all | solution.py:632
  70.3 0.0 collective-permute-done.15.refs_3_
  70.3 0.0 collective-permute-done.16.refs_4_
  70.3 1.9 %far_field.1.refs_2_.refs_3_ = f32[30,8,128]{2,1,0:T(8,128)S(1)} custom-call(s32[3,30]{1,0:T(4,128)S(1)} %bitcast.10, s32[30]{0:T(128)S(1)} %copy-done.9, f32[30,8,128]{2,1,0:T(8,128)S(1)} %get-tuple-element.61.refs_1_.refs_2_, f32[46,8,128]{2,1,0:T(8,128)S(1)} %collective-permute-done.15.refs_3_, f32[46,8,128]{2,1,0:T(8,128)S(1)} %collective-permute-done.16.refs_4_, ...), custom_call_target="tpu_custom_call" | custom-call | flops 2147483648 | bytes 5368709 | tf_op jit(solution)/shard_map/far_field/pallas_call | solution.py:237
  72.2 1.2 %top_sums.1.refs_1_ = f32[136,128]{1,0:T(8,128)S(1)} custom-call(f32[5,32,128]{2,1,0:T(8,128)S(1)} %get-tuple-element.58.refs_0_, f32[4,32,128]{2,1,0:T(8,128)S(1)} %get-tuple-element.59.refs_1_, f32[3,8,128]{2,1,0:T(8,128)S(1)} %get-tuple-element.60.refs_2_), custom_call_target="tpu_custom_call" | custom-call | flops 1073741824 | bytes 2684354 | tf_op jit(solution)/shard_map/top_sums/pallas_call | solution.py:237
  73.4 1.1 %all-to-all-done.2.refs_0_ = f32[4,8,128]{2,1,0:T(8,128)S(1)} async-done(((f32[4,8,128]{2,1,0:T(8,128)}), f32[4,8,128]{2,1,0:T(8,128)S(1)}, u32[]{:S(2)}, u32[]{:S(2)}) %all-to-all-start.2) | async-done | bytes 16416 | tf_op jit(solution)/shard_map/all_to_all | solution.py:632
  74.5 1.6 %top_turn.1 = f32[16,8,128]{2,1,0:T(8,128)} custom-call(f32[4,8,128]{2,1,0:T(8,128)S(1)} %all-to-all-done.2.refs_0_, f32[136,128]{1,0:T(8,128)S(1)} %top_sums.1.refs_1_, f32[30,8,128]{2,1,0:T(8,128)S(1)} %far_field.1.refs_2_.refs_3_), custom_call_target="tpu_custom_call" | custom-call | flops 2147483648 | bytes 5368709 | tf_op jit(solution)/shard_map/top_turn/pallas_call | solution.py:237
  76.1 7.1 %all-to-all-start.3 = ((f32[16,8,128]{2,1,0:T(8,128)}), f32[16,8,128]{2,1,0:T(8,128)S(1)}, u32[]{:S(2)}, u32[]{:S(2)}) async-start(f32[16,8,128]{2,1,0:T(8,128)} %top_turn.1), calls=%async_computation.3 | async-start | bytes 131072 | tf_op jit(solution)/shard_map/all_to_all | solution.py:675
  83.2 1.5 %group_sums.1.refs_1_ = f32[40,128]{1,0:T(8,128)S(1)} custom-call(f32[4,8,128]{2,1,0:T(8,128)S(1)} %get-tuple-element.64.refs_0_, f32[12,32,128]{2,1,0:T(8,128)S(1)} %get-tuple-element.37.refs_0_.refs_1_, f32[7,32,128]{2,1,0:T(8,128)S(1)} %get-tuple-element.65.refs_2_), custom_call_target="tpu_custom_call" | custom-call | flops 1073741824 | bytes 2684354 | tf_op jit(solution)/shard_map/group_sums/pallas_call | solution.py:237
  84.8 0.6 copy-done.14
  85.4 1.7 %near_field.1.refs_5_ = f32[16,2048]{1,0:T(8,128)S(1)} custom-call(s32[2,16]{1,0:T(2,128)S(1)} %bitcast.11, s32[16]{0:T(128)S(1)} %copy-done.10, f32[16,2048]{1,0:T(8,128)S(1)} %copy-done.6, f32[46,8,128]{2,1,0:T(8,128)S(1)} %collective-permute-done.15.refs_3_, f32[46,8,128]{2,1,0:T(8,128)S(1)} %collective-permute-done.16.refs_4_, ...), custom_call_target="tpu_custom_call" | custom-call | flops 2147483648 | bytes 5368709 | tf_op jit(solution)/shard_map/near_field/pallas_call | solution.py:237
  87.1 0.7 copy-done.12
  87.8 1.3 %all-to-all-done.3.refs_0_ = f32[16,8,128]{2,1,0:T(8,128)S(1)} async-done(((f32[16,8,128]{2,1,0:T(8,128)}), f32[16,8,128]{2,1,0:T(8,128)S(1)}, u32[]{:S(2)}, u32[]{:S(2)}) %all-to-all-start.3) | async-done | bytes 65568 | tf_op jit(solution)/shard_map/all_to_all | solution.py:675
  89.1 0.6 copy-done.15
  89.7 4.5 %downward.1 = f32[16,2048]{1,0:T(8,128)} custom-call(f32[16,8,128]{2,1,0:T(8,128)} %copy-done.15, f32[40,128]{1,0:T(8,128)} %copy-done.14, bf16[30,64,128]{2,1,0:T(8,128)(2,1)} %copy-done.11, f32[30,8,128]{2,1,0:T(8,128)} %copy-done.13, f32[16,64,128]{2,1,0:T(8,128)} %refs_4_.1, f32[16,2048]{1,0:T(8,128)} %copy-done.12), custom_call_target="tpu_custom_call" | custom-call | flops 4294967296 | bytes 10737418 | tf_op jit(solution)/shard_map/downward/pallas_call | solution.py:237
  (28 shorter events, 0.2 us)
Async XLA Ops:
  0.0 1.0 %copy-start.4 = (f32[1,9,2,4096]{3,2,1,0:T(2,128)S(1)}, f32[1,9,2,4096]{3,2,1,0:T(2,128)}, u32[]{:S(2)}) copy-start(f32[1,9,2,4096]{3,2,1,0:T(2,128)} %param.18) | copy-start | bytes 884740
  1.0 0.9 copy-start.5
  1.9 11.3 %copy-start.2 = (f32[30,4096]{1,0:T(8,128)S(1)}, f32[30,4096]{1,0:T(8,128)}, u32[]{:S(2)}) copy-start(f32[30,4096]{1,0:T(8,128)} %refs_2_.2) | copy-start | bytes 1474564
  1.9 11.3 %copy-start.3 = (f32[16,64,128]{2,1,0:T(8,128)S(1)}, f32[16,64,128]{2,1,0:T(8,128)}, u32[]{:S(2)}) copy-start(f32[16,64,128]{2,1,0:T(8,128)} %refs_4_.1) | copy-start | bytes 1572868
  1.9 11.3 %copy-start.6 = (f32[16,2048]{1,0:T(8,128)S(1)}, f32[16,2048]{1,0:T(8,128)}, u32[]{:S(2)}) copy-start(f32[16,2048]{1,0:T(8,128)} %refs_2_.3) | copy-start | bytes 393220
  2.1 9.1 %collective-permute-start.1 = (f32[7,32,128]{2,1,0:T(8,128)S(1)}, f32[7,32,128]{2,1,0:T(8,128)S(1)}, u32[]{:S(2)}, u32[]{:S(2)}) collective-permute-start(f32[7,32,128]{2,1,0:T(8,128)S(1)} %get-tuple-element.39), channel_id=1, source_target_pairs={{0,1},{16,17},{32,33},{48,49},{64,65},{80,81},{96,97},{112,113},{1... | collective-permute-start | bytes 344072 | tf_op jit(solution)/shard_map/ppermute | solution.py:259
  3.5 2.0 %collective-permute-start = (f32[1,32,128]{2,1,0:T(8,128)S(1)}, f32[1,32,128]{2,1,0:T(8,128)S(1)}, u32[]{:S(2)}, u32[]{:S(2)}) collective-permute-start(f32[1,32,128]{2,1,0:T(8,128)S(1)} %get-tuple-element.38), channel_id=1, source_target_pairs={{0,8},{16,24},{32,40},{48,56},{64,72},{80,88},{96,104},{112,120},{... | collective-permute-start | bytes 49160 | tf_op jit(solution)/shard_map/ppermute | solution.py:259
  4.2 10.6 %collective-permute-start.3 = (f32[7,32,128]{2,1,0:T(8,128)S(1)}, f32[7,32,128]{2,1,0:T(8,128)S(1)}, u32[]{:S(2)}, u32[]{:S(2)}) collective-permute-start(f32[7,32,128]{2,1,0:T(8,128)S(1)} %get-tuple-element.42), channel_id=1, source_target_pairs={{0,1},{16,17},{32,33},{48,49},{64,65},{80,81},{96,97},{112,113},{1... | collective-permute-start | bytes 344072 | tf_op jit(solution)/shard_map/ppermute | solution.py:259
  11.2 3.6 %collective-permute-start.2 = (f32[3,32,128]{2,1,0:T(8,128)S(1)}, f32[3,32,128]{2,1,0:T(8,128)S(1)}, u32[]{:S(2)}, u32[]{:S(2)}) collective-permute-start(f32[3,32,128]{2,1,0:T(8,128)S(1)} %get-tuple-element.40), channel_id=1, source_target_pairs={{0,4},{8,12},{16,20},{24,28},{32,36},{40,44},{48,52},{56,60},{64,6... | collective-permute-start | bytes 147464 | tf_op jit(solution)/shard_map/ppermute | solution.py:259
  11.8 2.9 %collective-permute-start.4 = (f32[1,32,128]{2,1,0:T(8,128)S(1)}, f32[1,32,128]{2,1,0:T(8,128)S(1)}, u32[]{:S(2)}, u32[]{:S(2)}) collective-permute-start(f32[1,32,128]{2,1,0:T(8,128)S(1)} %get-tuple-element.43), channel_id=1, source_target_pairs={{1,257}} | collective-permute-start | bytes 49160 | tf_op jit(solution)/shard_map/ppermute | solution.py:259
  14.7 10.5 %copy-start.11 = (bf16[30,64,128]{2,1,0:T(8,128)(2,1)}, bf16[30,64,128]{2,1,0:T(8,128)(2,1)S(1)}, u32[]{:S(2)}) copy-start(bf16[30,64,128]{2,1,0:T(8,128)(2,1)S(1)} %get-tuple-element.66.refs_2_) | copy-start | bytes 1474564
  14.8 2.3 %collective-permute-start.7 = (f32[2,32,128]{2,1,0:T(8,128)S(1)}, f32[2,32,128]{2,1,0:T(8,128)S(1)}, u32[]{:S(2)}, u32[]{:S(2)}) collective-permute-start(f32[2,32,128]{2,1,0:T(8,128)S(1)} %get-tuple-element.47), channel_id=1, source_target_pairs={{1,129},{257,385}} | collective-permute-start | bytes 98312 | tf_op jit(solution)/shard_map/ppermute | solution.py:259
  17.1 8.1 %collective-permute-start.8 = (f32[4,32,128]{2,1,0:T(8,128)S(1)}, f32[4,32,128]{2,1,0:T(8,128)S(1)}, u32[]{:S(2)}, u32[]{:S(2)}) collective-permute-start(f32[4,32,128]{2,1,0:T(8,128)S(1)} %get-tuple-element.49.refs_0_), channel_id=1, source_target_pairs={{1,33},{129,161},{257,289},{385,417}} | collective-permute-start | bytes 196616 | tf_op jit(solution)/shard_map/ppermute | solution.py:259
  19.9 5.4 %collective-permute-start.9 = (f32[4,32,128]{2,1,0:T(8,128)S(1)}, f32[4,32,128]{2,1,0:T(8,128)S(1)}, u32[]{:S(2)}, u32[]{:S(2)}) collective-permute-start(f32[4,32,128]{2,1,0:T(8,128)S(1)} %get-tuple-element.50), channel_id=1, source_target_pairs={{1,97},{129,225},{257,353},{385,481}} | collective-permute-start | bytes 196616 | tf_op jit(solution)/shard_map/ppermute | solution.py:259
  23.3 4.0 %collective-permute-start.5 = (f32[5,32,128]{2,1,0:T(8,128)S(1)}, f32[5,32,128]{2,1,0:T(8,128)S(1)}, u32[]{:S(2)}, u32[]{:S(2)}) collective-permute-start(f32[5,32,128]{2,1,0:T(8,128)S(1)} %get-tuple-element.44), channel_id=1, source_target_pairs={{0,2},{4,6},{8,10},{12,14},{16,18},{20,22},{24,26},{28,30},{32,34}... | collective-permute-start | bytes 245768 | tf_op jit(solution)/shard_map/ppermute | solution.py:259
  23.9 3.3 %collective-permute-start.6 = (f32[2,32,128]{2,1,0:T(8,128)S(1)}, f32[2,32,128]{2,1,0:T(8,128)S(1)}, u32[]{:S(2)}, u32[]{:S(2)}) collective-permute-start(f32[2,32,128]{2,1,0:T(8,128)S(1)} %get-tuple-element.46), channel_id=1, source_target_pairs={{1,33},{65,97},{129,161},{193,225},{257,289},{321,353},{385,417},{... | collective-permute-start | bytes 98312 | tf_op jit(solution)/shard_map/ppermute | solution.py:259
  25.3 3.3 %collective-permute-start.11 = (f32[4,32,128]{2,1,0:T(8,128)S(1)}, f32[4,32,128]{2,1,0:T(8,128)S(1)}, u32[]{:S(2)}, u32[]{:S(2)}) collective-permute-start(f32[4,32,128]{2,1,0:T(8,128)S(1)} %hand_down_4.1.refs_5_.refs_0_), channel_id=1, source_target_pairs={{1,17},{33,49},{65,81},{97,113},{129,145},{161,177},{193,209},{225... | collective-permute-start | bytes 196616 | tf_op jit(solution)/shard_map/ppermute | solution.py:259
  26.6 2.0 %collective-permute-start.12 = (f32[4,32,128]{2,1,0:T(8,128)S(1)}, f32[4,32,128]{2,1,0:T(8,128)S(1)}, u32[]{:S(2)}, u32[]{:S(2)}) collective-permute-start(f32[4,32,128]{2,1,0:T(8,128)S(1)} %hand_down_4.1.refs_5_.refs_0_), channel_id=1, source_target_pairs={{97,65},{225,193},{353,321},{481,449}} | collective-permute-start | bytes 196616 | tf_op jit(solution)/shard_map/ppermute | solution.py:259
  27.3 3.2 %collective-permute-start.10 = (f32[7,32,128]{2,1,0:T(8,128)S(1)}, f32[7,32,128]{2,1,0:T(8,128)S(1)}, u32[]{:S(2)}, u32[]{:S(2)}) collective-permute-start(f32[7,32,128]{2,1,0:T(8,128)S(1)} %get-tuple-element.52), channel_id=1, source_target_pairs={{0,1},{2,3},{4,5},{6,7},{8,9},{10,11},{12,13},{14,15},{16,17},{18,... | collective-permute-start | bytes 344072 | tf_op jit(solution)/shard_map/ppermute | solution.py:259
  32.3 9.7 %all-to-all-start = ((f32[16,16,128]{2,1,0:T(8,128)}), f32[16,16,128]{2,1,0:T(8,128)S(1)}, u32[]{:S(2)}, u32[]{:S(2)}) async-start(f32[16,16,128]{2,1,0:T(8,128)} %get-tuple-element.53), calls=%async_computation | async-start | bytes 262144 | tf_op jit(solution)/shard_map/all_to_all | solution.py:604
  35.7 3.3 %collective-permute-start.13 = (f32[4,32,128]{2,1,0:T(8,128)S(1)}, f32[4,32,128]{2,1,0:T(8,128)S(1)}, u32[]{:S(2)}, u32[]{:S(2)}) collective-permute-start(f32[4,32,128]{2,1,0:T(8,128)S(1)} %get-tuple-element.55), channel_id=1, source_target_pairs={{1,17},{33,49},{65,81},{97,113},{129,145},{161,177},{193,209},{225... | collective-permute-start | bytes 196616 | tf_op jit(solution)/shard_map/ppermute | solution.py:259
  43.4 21.8 %all-to-all-start.1 = ((f32[8,16,128]{2,1,0:T(8,128)}), f32[8,16,128]{2,1,0:T(8,128)S(1)}, u32[]{:S(2)}, u32[]{:S(2)}) async-start(f32[8,16,128]{2,1,0:T(8,128)} %get-tuple-element.56.refs_2_), calls=%async_computation.1 | async-start | bytes 131072 | tf_op jit(solution)/shard_map/all_to_all | solution.py:613
  53.0 17.2 %copy-start.1 = (f32[30,3,4096]{2,0,1:T(8,128)S(1)}, f32[30,3,4096]{2,0,1:T(8,128)}, u32[]{:S(2)}) copy-start(f32[30,3,4096]{2,0,1:T(8,128)} %param.14) | copy-start | bytes 4423684
  53.1 17.2 %copy-start.7 = (s32[30,3]{0,1:T(4,128)S(1)}, s32[30,3]{0,1:T(4,128)}, u32[]{:S(2)}) copy-start(s32[30,3]{0,1:T(4,128)} %param.15) | copy-start | bytes 1084
  53.1 17.2 %copy-start.9 = (s32[30]{0:T(128)S(1)}, s32[30]{0:T(128)}, u32[]{:S(2)}) copy-start(s32[30]{0:T(128)} %refs_1_.4) | copy-start | bytes 364
  53.1 17.2 %collective-permute-start.15 = (f32[46,8,128]{2,1,0:T(8,128)S(1)}, f32[46,8,128]{2,1,0:T(8,128)S(1)}, u32[]{:S(2)}, u32[]{:S(2)}) collective-permute-start(f32[46,8,128]{2,1,0:T(8,128)S(1)} %get-tuple-element.62), channel_id=1, source_target_pairs={{0,1},{1,2},{2,3},{3,4},{4,5},{5,6},{6,7},{7,8},{8,9},{9,10},{10,1... | collective-permute-start | bytes 565256 | tf_op jit(solution)/shard_map/ppermute | solution.py:259
  55.8 14.5 %collective-permute-start.16 = (f32[46,8,128]{2,1,0:T(8,128)S(1)}, f32[46,8,128]{2,1,0:T(8,128)S(1)}, u32[]{:S(2)}, u32[]{:S(2)}) collective-permute-start(f32[46,8,128]{2,1,0:T(8,128)S(1)} %get-tuple-element.63), channel_id=1, source_target_pairs={{1,0},{2,1},{3,2},{4,3},{5,4},{6,5},{7,6},{8,7},{9,8},{10,9},{11,1... | collective-permute-start | bytes 565256 | tf_op jit(solution)/shard_map/ppermute | solution.py:259
  57.7 0.7 collective-permute-start.14
  66.1 8.4 %all-to-all-start.2 = ((f32[4,8,128]{2,1,0:T(8,128)}), f32[4,8,128]{2,1,0:T(8,128)S(1)}, u32[]{:S(2)}, u32[]{:S(2)}) async-start(f32[4,8,128]{2,1,0:T(8,128)} %get-tuple-element.57.refs_6_), calls=%async_computation.2 | async-start | bytes 32768 | tf_op jit(solution)/shard_map/all_to_all | solution.py:632
  72.2 3.9 %copy-start.13 = (f32[30,8,128]{2,1,0:T(8,128)}, f32[30,8,128]{2,1,0:T(8,128)S(1)}, u32[]{:S(2)}) copy-start(f32[30,8,128]{2,1,0:T(8,128)S(1)} %far_field.1.refs_2_.refs_3_) | copy-start | bytes 368644
  76.1 9.3 %copy-start = (f32[16,2,128,128]{3,2,1,0:T(8,128)S(1)}, f32[16,2,128,128]{3,2,1,0:T(8,128)}, u32[]{:S(2)}) copy-start(f32[16,2,128,128]{3,2,1,0:T(8,128)} %refs_5_.1) | copy-start | bytes 6291460
  76.1 9.3 %copy-start.8 = (s32[16,2]{0,1:T(2,128)S(1)}, s32[16,2]{0,1:T(2,128)}, u32[]{:S(2)}) copy-start(s32[16,2]{0,1:T(2,128)} %param.20) | copy-start | bytes 388
  76.1 9.3 %copy-start.10 = (s32[16]{0:T(128)S(1)}, s32[16]{0:T(128)}, u32[]{:S(2)}) copy-start(s32[16]{0:T(128)} %refs_1_.5) | copy-start | bytes 196
  76.1 13.0 %all-to-all-start.3 = ((f32[16,8,128]{2,1,0:T(8,128)}), f32[16,8,128]{2,1,0:T(8,128)S(1)}, u32[]{:S(2)}, u32[]{:S(2)}) async-start(f32[16,8,128]{2,1,0:T(8,128)} %top_turn.1), calls=%async_computation.3 | async-start | bytes 131072 | tf_op jit(solution)/shard_map/all_to_all | solution.py:675
  84.8 0.6 copy-start.14
  87.1 0.7 copy-start.12
  89.1 0.6 copy-start.15

commit v4 on v3

--- a/solution.py
+++ b/solution.py
@@ -17,7 +17,9 @@
 GROUP_BITS = 4
 TOP_BITS = 9
 GROUP = 1 << GROUP_BITS
+NEAR_ROWS = 16 * LEAVES
 PORTER = 1
+HIGH = 7
 LAYOUT = ((16, 0), (8, 16), (4, 24), (2, 28))
 VMEM_BYTES = 20 * 1024 * 1024
 WIDE_BYTES = 63 * 1024 * 1024
@@ -81,29 +83,26 @@
         ],
         axis=0,
     )
-    return split(full)
-
-
-def weave(even_odd):
+    return jnp.concatenate(split(full), axis=0)
+
+
+def times_t_raw(rows, forms):
+    out = dot_t(rows, forms)
+    return out[:32] + pltpu.roll(out[:32], 96, 1) + out[32:]
+
+
+def weave(raw, child):
     lane = lanes(8)
-    place = (lane % 64) // 2
-    wide = jnp.concatenate([even_odd] * 4, axis=1)
-    pick = [jnp.take_along_axis(wide[8 * k : 8 * k + 8], place, axis=1) for k in range(4)]
+    place = 64 * child + (lane % 64) // 2
+    pick = [jnp.take_along_axis(raw[8 * k : 8 * k + 8], place, axis=1) for k in range(4)]
     even = lane % 2 == 0
     return jnp.where(
         lane < 64, jnp.where(even, pick[0], pick[2]), jnp.where(even, pick[1], pick[3])
     )
 
 
-def times_t_raw(rows, high, low):
-    row_high, row_low = rows
-    both = dot_t(jnp.concatenate([row_high, row_low], axis=0), high)
-    return both[:32] + both[32:] + dot_t(row_high, low)
-
-
 def times_t(packed, table):
-    high, low = split(table)
-    return weave(times_t_raw(row_form(packed), high, low))
+    return weave(times_t_raw(row_form(packed), table_form(table)), 0)
 
 
 def unpack(packed):
@@ -155,7 +154,22 @@
         edge[LOCAL + 2 * place + 1] = entries[8:]
 
 
-def near_kernel(partner, count, own, low, high, block, out, leaves):
+def group_sums(sibling, raw, table, out):
+    terms = [
+        times(sibling[level], table[2 * GROUP_BITS - 2 - level]) for level in range(GROUP_BITS)
+    ]
+    value = terms[GROUP_BITS - 1]
+    product = raw[0]
+    for level in range(GROUP_BITS - 2, -1, -1):
+        value = times_t(value, raw[0] if level == 0 else table[level - 1]) + terms[level]
+    for level in range(1, GROUP_BITS):
+        product = times(product, table[level - 1])
+    out[NEAR_ROWS : NEAR_ROWS + 8] = value
+    out[NEAR_ROWS + 8 : NEAR_ROWS + 40] = product
+
+
+def near_kernel(partner, count, own, low, high, block, sibling, raw, table, out, leaves):
+    group_sums(sibling, raw, table, out)
     for leaf in range(LEAVES):
         leaves[REACH + leaf] = own[:, leaf * POINTS : (leaf + 1) * POINTS]
     for leaf in range(REACH):
@@ -174,10 +188,22 @@
             both = dot_t(jnp.concatenate([picked_high, picked_low], axis=0), block_high)
             value = both[:16] + both[16:] + dot_t(picked_high, block_low)
             total = value if total is None else total + value
-        out[:, leaf * POINTS : (leaf + 1) * POINTS] = total
-
-
-def far_kernel(partner, count, own, low, high, coupling, out, extended):
+        out[16 * leaf : 16 * leaf + 16] = total
+
+
+def top_sums(low, upper, sums, out):
+    value = times(sums[2], upper[3])
+    value = times_t(value, low[2]) + times(sums[1], low[1])
+    out[0:8] = times_t(value, low[4]) + times(sums[0], low[3])
+    out[8:40] = times(times(low[4], low[2]), low[0])
+    for entry in range(3):
+        out[40 + 32 * entry : 72 + 32 * entry] = upper[entry]
+
+
+def far_kernel(
+    partner, count, own, low, high, coupling, low_table, upper, sums, out, prepared, extended
+):
+    top_sums(low_table, upper, sums, prepared)
     device = place_of_device()[0]
     extended[0:LOCAL] = low[0:LOCAL]
     extended[LOCAL : 2 * LOCAL] = own[...]
@@ -263,19 +289,18 @@
     return shape(size, 32, 128)
 
 
-def prepare_kernel(transfers, couplings, group_raw, high_raw, low_raw, group_pay):
-
+def prepare_kernel(transfers, couplings, group_raw, top_raw, group_pay):
     def coupling(level, side):
         return couplings[level - 1, :, side, :]
 
     group_pay[0] = coupling(GROUP_BITS, 1)
-    high_raw[0] = transfers[7]
-    low_raw[0:3] = transfers[4:7]
+    top_raw[0:3] = transfers[4:7]
+    top_raw[HIGH] = transfers[7]
     for side in range(2):
         for level in range(7, 10):
-            high_raw[1 + 3 * side + level - 7] = coupling(level, side)
+            top_raw[HIGH + 1 + 3 * side + level - 7] = coupling(level, side)
         for level in range(5, 7):
-            low_raw[3 + 2 * side + level - 5] = coupling(level, side)
+            top_raw[3 + 2 * side + level - 5] = coupling(level, side)
         for level in range(1, 5):
             group_raw[4 + 4 * side + level - 1] = coupling(level, side)
     group_raw[0:4] = transfers[0:4]
@@ -305,60 +330,62 @@
     pay[1 + size] = raw[2 * GROUP_BITS + bit]
 
 
-def first_kernel(raw, arrived, high_raw, live, pay, high_pay):
+def first_kernel(raw, arrived, top_raw, live, pay):
     merge_group(raw, 3, None, arrived, live)
     group_payload(raw, 2, live, pay)
-    high_pay[0] = high_raw[6]
-
-
-def second_kernel(
-    raw, arrived, live, low_raw, high_raw, high_in, out, pay, high_live, high_pay, low_pay
-):
+
+    @pl.when(place_of_device()[1] == PORTER)
+    def _():
+        pay[0] = top_raw[HIGH + 6]
+
+
+def second_kernel(raw, arrived, live, top_raw, out, pay, ninth):
     merge_group(raw, 2, live, arrived, out)
     group_payload(raw, 1, out, pay)
-    _, _, group = place_of_device()
-    value = choose(((group >> 4) & 1) == 1, high_in[0], high_raw[3])
-    high_live[0] = value
-    high_pay[0] = value
-    high_pay[1] = high_raw[5]
-    low_pay[0] = low_raw[2]
-    low_pay[1] = low_raw[6]
-
-
-def line_kernel(high_raw, high_in, high_live, upper, high_pay):
-    _, _, group = place_of_device()
-    right_child = ((group >> 3) & 1) == 1
-    ninth = choose(right_child, high_in[0], high_live[0])
-    eighth = choose(right_child, high_in[1], high_raw[2])
-    for target, side in ((upper, 1), (high_pay, 4)):
-        target[0] = high_raw[0]
-        target[1] = ninth
-        target[2] = eighth
-        target[3] = high_raw[side]
-
-
-def third_kernel(raw, arrived, live, low_raw, low_in, out, pay, keep, low_pay):
+    _, member, group = place_of_device()
+    value = choose(((group >> 4) & 1) == 1, arrived[0], top_raw[HIGH + 3])
+    ninth[0] = value
+
+    @pl.when(member == PORTER)
+    def _():
+        pay[0] = value
+        pay[1] = top_raw[HIGH + 5]
+
+
+def third_kernel(raw, arrived, live, top_raw, ninth, out, pay, upper, near_pay, far_pay):
     merge_group(raw, 1, live, arrived, out)
     group_payload(raw, 0, out, pay)
     _, _, group = place_of_device()
-    second = ((group >> 1) & 1) == 1
-    sixth = choose(second, low_in[0], low_raw[2])
-    sixth_coupling = choose(second, low_in[1], low_raw[4])
-    for target, side in ((keep, 3), (low_pay, 5)):
-        target[0] = sixth
-        target[1] = sixth_coupling
-        target[2] = low_raw[1]
-        target[3] = low_raw[side]
-    keep[4] = low_raw[0]
-
-
-def fourth_kernel(upper, near_in, far_in, out):
+    right_child = ((group >> 3) & 1) == 1
+    values = (
+        top_raw[HIGH],
+        choose(right_child, arrived[0], ninth[0]),
+        choose(right_child, arrived[1], top_raw[HIGH + 2]),
+    )
+    for target, side in ((upper, 1), (near_pay, 1), (far_pay, 4)):
+        for entry in range(3):
+            target[entry] = values[entry]
+        target[3] = top_raw[HIGH + side]
+    near_pay[4] = top_raw[2]
+    near_pay[5] = top_raw[6]
+
+
+def fourth_kernel(top_raw, upper, near_in, far_in, out, keep, low_pay):
     _, _, group = place_of_device()
     place = group & 7
     for entry in range(4):
         out[entry] = choose(
             place == 2, near_in[entry], choose(place == 6, far_in[entry], upper[entry])
         )
+    second = ((group >> 1) & 1) == 1
+    sixth = choose(second, near_in[4], top_raw[2])
+    coupling = choose(second, near_in[5], top_raw[4])
+    for target, side in ((keep, 3), (low_pay, 5)):
+        target[0] = sixth
+        target[1] = coupling
+        target[2] = top_raw[1]
+        target[3] = top_raw[side]
+    keep[4] = top_raw[0]
 
 
 def share_kernel(root, raw, live, arrived, blocks, table, chain):
@@ -407,16 +434,16 @@
         blocks[other, 8:16] = value
 
 
-def fifth_kernel(upper, near_in, far_in, out):
+def fifth_kernel(upper, near_in, far_in, next_in, out):
     _, _, group = place_of_device()
     place = group & 7
     for entry in range(4):
-        out[entry] = choose(
-            (place & 1) == 1, near_in[entry], choose(place == 4, far_in[entry], upper[entry])
-        )
-
-
-def middle_kernel(given, upper, arrived, blocks, upper_out, sums):
+        even = choose(place == 4, far_in[entry], upper[entry])
+        odd = choose(place == 5, next_in[entry], near_in[entry])
+        out[entry] = choose((place & 1) == 1, odd, even)
+
+
+def middle_kernel(given, upper, blocks, sums):
     _, _, group = place_of_device()
     place, line = group & 7, group >> 3
     for level in range(3):
@@ -424,21 +451,9 @@
             [given[place ^ apart, 0:8] for apart in range(1 << level, 2 << level)]
         )
     value = total_of([given[other, 8:16] for other in range(8)])
-    table = upper_out
-    for entry in range(4):
-        table[entry] = choose(place == 5, arrived[entry], upper[entry])
-    raised = times(value, table[0])
+    raised = times(value, upper[0])
     for other in range(4):
         blocks[other] = choose((line ^ other) >= 2, raised, value)
-
-
-def top_sums_kernel(low, upper, sums, out):
-    value = times(sums[2], upper[3])
-    value = times_t(value, low[2]) + times(sums[1], low[1])
-    out[0:8] = times_t(value, low[4]) + times(sums[0], low[3])
-    out[8:40] = times(times(low[4], low[2]), low[0])
-    for entry in range(3):
-        out[40 + 32 * entry : 72 + 32 * entry] = upper[entry]
 
 
 def turn_kernel(given, prepared, out):
@@ -452,42 +467,28 @@
         out[other] = value
 
 
-def group_sums_kernel(sibling, raw, table, out):
-    terms = [
-        times(sibling[level], table[2 * GROUP_BITS - 2 - level]) for level in range(GROUP_BITS)
-    ]
-    value = terms[GROUP_BITS - 1]
-    product = raw[0]
-    for level in range(GROUP_BITS - 2, -1, -1):
-        value = times_t(value, raw[0] if level == 0 else table[level - 1]) + terms[level]
-    for level in range(1, GROUP_BITS):
-        product = times(product, table[level - 1])
-    out[0:8] = value
-    out[8:40] = product
-
-
-def down_kernel(given, prepared, forms, far, basis, near, out):
-    prepared = prepared()
-    value = times_t(given[PORTER], prepared[8:40]) + prepared[0:8]
+def down_kernel(given, near, forms, far, basis, out):
+    near = near()
+    value = times_t(given[PORTER], near[NEAR_ROWS + 8 : NEAR_ROWS + 40])
+    value = value + near[NEAR_ROWS : NEAR_ROWS + 8]
     parents = [value]
     forms, far = forms(), far()
     for clusters, offset in reversed(LAYOUT):
         following = []
         for parent in range(clusters // 2):
             first = offset + 2 * parent
-            high = jnp.concatenate([forms[first, 0:32], forms[first + 1, 0:32]], axis=0)
-            low = jnp.concatenate([forms[first, 32:64], forms[first + 1, 32:64]], axis=0)
-            out_pair = times_t_raw(row_form(parents[parent]), high, low)
-            following.append(weave(out_pair[:, 0:32]) + far[first])
-            following.append(weave(out_pair[:, 32:64]) + far[first + 1])
+            pair = jnp.concatenate([forms[first], forms[first + 1]], axis=0)
+            raw = times_t_raw(row_form(parents[parent]), pair)
+            following.append(weave(raw, 0) + far[first])
+            following.append(weave(raw, 1) + far[first + 1])
         parents = following
-    basis, near = basis(), near()
+    basis = basis()
     for leaf in range(LEAVES):
         high, low = split(unpack(parents[leaf]))
         basis_high, basis_low = split(basis[leaf])
         both = dot(jnp.concatenate([high, low], axis=0), basis_high)
         place = slice(leaf * POINTS, (leaf + 1) * POINTS)
-        out[:, place] = both[:16] + both[16:] + dot(high, basis_low) + near[:, place]
+        out[:, place] = both[:16] + both[16:] + dot(high, basis_low) + near[16 * leaf : 16 * leaf + 16]
 
 
 def on_device(
@@ -512,16 +513,15 @@
 
     transfers = top_transfer.reshape(TOP_BITS, 32, 128)
     couplings = top_coupling.reshape(TOP_BITS, 2, 32, 128).transpose(0, 2, 1, 3)
-    raw, high_raw, low_raw, pay = call(
+    raw, top_raw, pay = call(
         prepare_kernel,
         "top_tables",
-        [tables(12), tables(7), tables(7), tables(1)],
+        [tables(12), tables(14), tables(1)],
         [transfers, couplings],
         flops=1 << 30,
     )
-    high_raw = handed(high_raw, GROUP, 0, PORTER)
     group_in = handed(pay, 16, 0, 8)
-    low_raw = handed(low_raw, GROUP, 0, PORTER)
+    top_raw = handed(top_raw, GROUP, 0, PORTER)
 
     coefs, root, forms = call(
         up_kernel,
@@ -534,64 +534,54 @@
         [sources, leaf_cluster_basis, local_transfer],
         flops=2 << 30,
     )
-    live, pay, high_pay = call(
+    live, pay = call(
         first_kernel,
         "hand_down_1",
-        [tables(1), tables(3), tables(1)],
-        [raw, group_in, high_raw],
+        [tables(1), tables(3)],
+        [raw, group_in, top_raw],
         flops=1 << 29,
     )
-    group_in = handed(pay, 8, 0, 4)
-    high_in = handed(high_pay, 512, PORTER, 256 + PORTER)
-    live, pay, high_live, high_pay, low_pay = call(
+    pairs = [(i, i + 4) for i in range(0, count, 8)] + [(PORTER, 256 + PORTER)]
+    group_in = permute(pay, pairs)
+    live, pay, ninth = call(
         second_kernel,
         "hand_down_2",
-        [tables(3), tables(5), tables(1), tables(2), tables(2)],
-        [raw, group_in, live, low_raw, high_raw, high_in],
+        [tables(3), tables(5), tables(1)],
+        [raw, group_in, live, top_raw],
         after=[root],
         flops=1 << 29,
     )
-    group_in = handed(pay, 4, 0, 2)
-    high_in = handed(high_pay, 256, PORTER, 128 + PORTER)
-    low_in = handed(low_pay, 64, PORTER, 32 + PORTER)
-    upper, high_pay = call(
-        line_kernel,
-        "hand_down_line",
-        [tables(4), tables(4)],
-        [high_raw, high_in, high_live],
-        flops=1 << 29,
-    )
-    near_in = handed(upper, 128, PORTER, 32 + PORTER)
-    far_in = handed(high_pay, 128, PORTER, 96 + PORTER)
-    upper = call(
-        fourth_kernel, "hand_down_4", [tables(4)], [upper, near_in, far_in], flops=1 << 29
-    )
-    live, pay, keep, low_pay = call(
+    pairs = [(i, i + 2) for i in range(0, count, 4)]
+    pairs += [(i + PORTER, i + 128 + PORTER) for i in range(0, count, 256)]
+    group_in = permute(pay, pairs)
+    live, pay, upper, near_pay, far_pay = call(
         third_kernel,
         "hand_down_3",
-        [tables(5), tables(7), tables(5), tables(4)],
-        [raw, group_in, live, low_raw, low_in],
-        after=[upper],
+        [tables(5), tables(7), tables(4), tables(6), tables(4)],
+        [raw, group_in, live, top_raw, ninth],
         flops=1 << 29,
     )
     group_in = handed(pay, 2, 0, 1)
+    near_in = handed(near_pay, 64, PORTER, 32 + PORTER)
+    far_in = handed(far_pay, 128, PORTER, 96 + PORTER)
+    upper, keep, low_pay = call(
+        fourth_kernel,
+        "hand_down_4",
+        [tables(4), tables(5), tables(4)],
+        [top_raw, upper, near_in, far_in],
+        flops=1 << 29,
+    )
     low_in = handed(low_pay, 32, PORTER, 16 + PORTER)
     near_in = handed(upper, 32, PORTER, 16 + PORTER)
     far_in = handed(upper, 128, 96 + PORTER, 64 + PORTER)
-    upper = call(
-        fifth_kernel,
-        "hand_down_5",
-        [tables(4)],
-        [upper, near_in, far_in],
-        flops=1 << 29,
-    )
+    next_in = handed(upper, 128, 96 + PORTER, 80 + PORTER)
     shares, group_table = call(
         share_kernel,
         "group_shares",
         [shape(GROUP, 16, 128), tables(7)],
         [root, raw, live, group_in],
         scratch=[pltpu.VMEM((GROUP_BITS, 8, 128), F32)],
-        after=[upper],
+        after=[keep],
         flops=2 << 30,
     )
     in_group = [list(range(first, first + GROUP)) for first in range(0, count, GROUP)]
@@ -602,6 +592,14 @@
     ]
     in_line = [list(range(first, count, 128)) for first in range(128)]
     given = lax.all_to_all(shares, "leaf", 0, 0, axis_index_groups=in_group)
+    upper = call(
+        fifth_kernel,
+        "hand_down_5",
+        [tables(4)],
+        [upper, near_in, far_in, next_in],
+        after=[shares],
+        flops=1 << 29,
+    )
     blocks, sibling, low_table = call(
         rise_kernel,
         "column_shares",
@@ -621,12 +619,11 @@
     )
     low_edge = permute(low_edge, forward)
     high_edge = permute(high_edge, backward)
-    upper_in = handed(upper, 128, 64 + PORTER, 80 + PORTER)
-    blocks, upper, sums = call(
+    blocks, sums = call(
         middle_kernel,
         "line_shares",
-        [shape(4, 8, 128), tables(4), shape(3, 8, 128)],
-        [given, upper, upper_in],
+        [shape(4, 8, 128), shape(3, 8, 128)],
+        [given, upper],
         flops=1 << 30,
     )
     given = lax.all_to_all(blocks, "leaf", 0, 0, axis_index_groups=in_line)
@@ -634,43 +631,47 @@
     near = call(
         near_kernel,
         "near_field",
-        [shape(16, LEAVES * POINTS)],
-        [near_partner.T, near_count, sources, low_edge, high_edge, near_block],
+        [shape(NEAR_ROWS + 40, 128)],
+        [
+            near_partner.T,
+            near_count,
+            sources,
+            low_edge,
+            high_edge,
+            near_block,
+            sibling,
+            raw,
+            group_table,
+        ],
         scalars=2,
         scratch=[pltpu.VMEM((LEAVES + 2 * REACH, 16, POINTS), F32)],
         flops=2 << 30,
     )
-    far = call(
+    far, prepared = call(
         far_kernel,
         "far_field",
-        [shape(LOCAL, 8, 128)],
-        [far_partner.T, far_count, coefs, low_edge, high_edge, far_coupling.transpose(1, 0, 2)],
+        [shape(LOCAL, 8, 128), shape(136, 128)],
+        [
+            far_partner.T,
+            far_count,
+            coefs,
+            low_edge,
+            high_edge,
+            far_coupling.transpose(1, 0, 2),
+            low_table,
+            upper,
+            sums,
+        ],
         scalars=2,
         scratch=[pltpu.VMEM((3 * LOCAL, 8, 128), F32)],
-        after=[blocks],
         flops=2 << 30,
-    )
-    prepared = call(
-        top_sums_kernel,
-        "top_sums",
-        [shape(136, 128)],
-        [low_table, upper, sums],
-        flops=1 << 30,
     )
     turned = call(
         turn_kernel,
         "top_turn",
         [shape(GROUP, 8, 128)],
         [given, prepared],
-        after=[far],
         flops=2 << 30,
-    )
-    prepared = call(
-        group_sums_kernel,
-        "group_sums",
-        [shape(40, 128)],
-        [sibling, raw, group_table],
-        flops=1 << 30,
     )
     given = lax.all_to_all(turned, "leaf", 0, 0, axis_index_groups=in_group)
     return call(
@@ -678,7 +679,7 @@
         "downward",
         [shape(16, LEAVES * POINTS)],
         [given],
-        lazy=[prepared, forms, far, leaf_cluster_basis, near],
+        lazy=[near, forms, far, leaf_cluster_basis],
         flops=4 << 30,
     )
 

time: 95.1 us -> 92.5 us (0.973)
  waiting for transfers between devices: 22.1 us -> 20.3 us
    all_to_all x1, waiting for transfers between devices: 6.81 us -> 2.1 us  [on_device(): given = lax.all_to_all(blocks, 'leaf', 0, 0, axis_index_groups=in_column)]
    ppermute x17 -> x13, waiting for transfers between devices: 9.92 us -> 11.9 us  [permute(): return lax.ppermute(value, 'leaf', pairs)]
    ppermute x17 -> x13, starting transfers between devices: 25.2 us -> 23.4 us  [permute(): return lax.ppermute(value, 'leaf', pairs)]
    all_to_all x1, starting transfers between devices: 3.45 us -> 4.5 us  [on_device(): given = lax.all_to_all(shares, 'leaf', 0, 0, axis_index_groups=in_group)]
    pallas_call x18 -> x15, Pallas kernels: 18.4 us -> 17.7 us  [call(): pl.pallas_call(body, out_shape=list(outs), in_specs=[smem] * scalars + [v...]
    unnamed x32 -> x30, local copies, waits for them, and re-layouts: 3.84 us -> 3.87 us
  transfers between devices with their start and end apart: 21 -> 17, of which waited for: 8 -> 8; matrix products, arithmetic and copies ran while one was open for 0% -> 0% of each run, Pallas kernels for 9% -> 9%
where the time goes in v4:
time: 92.5 us; the launch traced here: 91.8 us
  starting transfers between devices  49.5 us (54%)
  waiting for transfers between devices  20.3 us (22%)
  Pallas kernels  17.7 us (19%)
  local copies, waits for them, and re-layouts  3.87 us (4%)
    ppermute x13, starting transfers between devices, permute(): return lax.ppermute(value, 'leaf', pairs)  23.4 us
    pallas_call x15, Pallas kernels, call(): pl.pallas_call(body, out_shape=list(outs), in_specs=[smem] * scalars + [v...  17.7 us
    ppermute x13, waiting for transfers between devices, permute(): return lax.ppermute(value, 'leaf', pairs)  11.9 us
    all_to_all x1, starting transfers between devices, on_device(): given = lax.all_to_all(blocks, 'leaf', 0, 0, axis_index_groups=in_column)  10.4 us
    all_to_all x1, starting transfers between devices, on_device(): given = lax.all_to_all(turned, 'leaf', 0, 0, axis_index_groups=in_group)  6.99 us
    all_to_all x1, starting transfers between devices, on_device(): given = lax.all_to_all(shares, 'leaf', 0, 0, axis_index_groups=in_group)  4.5 us
    all_to_all x1, starting transfers between devices, on_device(): given = lax.all_to_all(blocks, 'leaf', 0, 0, axis_index_groups=in_line)  4.18 us
    unnamed x30, local copies, waits for them, and re-layouts  3.87 us
  transfers between devices with their start and end apart: 17, of which 8 were waited for; matrix products, arithmetic and copies ran while one was open for 0% of the time, Pallas kernels for 9%

profile of v4, /device:TPU:1, one launch (start us, length us, event | category | flops | bytes accessed | tf_op | source)
XLA Modules:
  0.0 91.8 jit_solution(12826314983592058868)
XLA Ops:
  0.0 0.0 copy-start.4
  0.0 1.0 %copy-done.4 = f32[1,9,2,4096]{3,2,1,0:T(2,128)S(1)} copy-done((f32[1,9,2,4096]{3,2,1,0:T(2,128)S(1)}, f32[1,9,2,4096]{3,2,1,0:T(2,128)}, u32[]{:S(2)}) %copy-start.4) | copy-done | bytes 294936
  1.0 0.0 copy-start.5
  1.0 0.9 copy-done.5
  1.9 0.0 copy-start.2
  1.9 0.2 top_tables.1
  2.1 1.4 %collective-permute-start.1 = (f32[14,32,128]{2,1,0:T(8,128)S(1)}, f32[14,32,128]{2,1,0:T(8,128)S(1)}, u32[]{:S(2)}, u32[]{:S(2)}) collective-permute-start(f32[14,32,128]{2,1,0:T(8,128)S(1)} %get-tuple-element.38), channel_id=1, source_target_pairs={{0,1},{16,17},{32,33},{48,49},{64,65},{80,81},{96,97},{112,113},{1... | collective-permute-start | bytes 688136 | tf_op jit(solution)/shard_map/ppermute | solution.py:285
  3.5 0.7 collective-permute-start
  4.2 0.0 collective-permute-done.refs_1_
  4.2 7.2 %collective-permute-done.1.refs_2_.refs_3_.refs_0_ = f32[14,32,128]{2,1,0:T(8,128)S(1)} collective-permute-done((f32[14,32,128]{2,1,0:T(8,128)S(1)}, f32[14,32,128]{2,1,0:T(8,128)S(1)}, u32[]{:S(2)}, u32[]{:S(2)}) %collective-permute-start.1) | collective-permute-done | bytes 229408 | tf_op jit(solution)/shard_map/ppermute | solution.py:285
  11.3 1.3 %collective-permute-start.2 = (f32[3,32,128]{2,1,0:T(8,128)S(1)}, f32[3,32,128]{2,1,0:T(8,128)S(1)}, u32[]{:S(2)}, u32[]{:S(2)}) collective-permute-start(f32[3,32,128]{2,1,0:T(8,128)S(1)} %get-tuple-element.39), channel_id=1, source_target_pairs={{0,4},{8,12},{16,20},{24,28},{32,36},{40,44},{48,52},{56,60},{64,6... | collective-permute-start | bytes 147464 | tf_op jit(solution)/shard_map/ppermute | solution.py:285
  12.6 0.0 copy-done.2
  12.6 0.0 copy-done.3
  12.7 0.0 copy-done.6
  12.7 1.6 %upward.1 = (f32[30,8,128]{2,1,0:T(8,128)S(1)}, f32[8,128]{1,0:T(8,128)S(1)}, bf16[30,64,128]{2,1,0:T(8,128)(2,1)S(1)}) custom-call(f32[16,2048]{1,0:T(8,128)S(1)} %copy-done.6, f32[16,64,128]{2,1,0:T(8,128)S(1)} %copy-done.3, f32[30,4096]{1,0:T(8,128)S(1)} %copy-done.2), custom_call_target="tpu_custom_call" | custom-call | flops 2147483648 | bytes 5368709 | tf_op jit(solution)/shard_map/upward/pallas_call | solution.py:263
  14.2 0.0 collective-permute-done.2.refs_1_
  14.3 1.3 %collective-permute-start.3 = (f32[5,32,128]{2,1,0:T(8,128)S(1)}, f32[5,32,128]{2,1,0:T(8,128)S(1)}, u32[]{:S(2)}, u32[]{:S(2)}) collective-permute-start(f32[5,32,128]{2,1,0:T(8,128)S(1)} %get-tuple-element.41), channel_id=1, source_target_pairs={{0,2},{4,6},{8,10},{12,14},{16,18},{20,22},{24,26},{28,30},{32,34}... | collective-permute-start | bytes 245768 | tf_op jit(solution)/shard_map/ppermute | solution.py:285
  15.6 1.5 %collective-permute-done.3.refs_1_ = f32[5,32,128]{2,1,0:T(8,128)S(1)} collective-permute-done((f32[5,32,128]{2,1,0:T(8,128)S(1)}, f32[5,32,128]{2,1,0:T(8,128)S(1)}, u32[]{:S(2)}, u32[]{:S(2)}) %collective-permute-start.3) | collective-permute-done | bytes 81952 | tf_op jit(solution)/shard_map/ppermute | solution.py:285
  17.1 1.3 %collective-permute-start.5 = (f32[6,32,128]{2,1,0:T(8,128)S(1)}, f32[6,32,128]{2,1,0:T(8,128)S(1)}, u32[]{:S(2)}, u32[]{:S(2)}) collective-permute-start(f32[6,32,128]{2,1,0:T(8,128)S(1)} %get-tuple-element.47), channel_id=1, source_target_pairs={{1,33},{65,97},{129,161},{193,225},{257,289},{321,353},{385,417},{... | collective-permute-start | bytes 294920 | tf_op jit(solution)/shard_map/ppermute | solution.py:285
  18.4 4.8 %collective-permute-start.6 = (f32[4,32,128]{2,1,0:T(8,128)S(1)}, f32[4,32,128]{2,1,0:T(8,128)S(1)}, u32[]{:S(2)}, u32[]{:S(2)}) collective-permute-start(f32[4,32,128]{2,1,0:T(8,128)S(1)} %get-tuple-element.48), channel_id=1, source_target_pairs={{1,97},{129,225},{257,353},{385,481}} | collective-permute-start | bytes 196616 | tf_op jit(solution)/shard_map/ppermute | solution.py:285
  23.2 1.3 %collective-permute-start.4 = (f32[7,32,128]{2,1,0:T(8,128)S(1)}, f32[7,32,128]{2,1,0:T(8,128)S(1)}, u32[]{:S(2)}, u32[]{:S(2)}) collective-permute-start(f32[7,32,128]{2,1,0:T(8,128)S(1)} %get-tuple-element.45), channel_id=1, source_target_pairs={{0,1},{2,3},{4,5},{6,7},{8,9},{10,11},{12,13},{14,15},{16,17},{18,... | collective-permute-start | bytes 344072 | tf_op jit(solution)/shard_map/ppermute | solution.py:285
  24.5 0.0 collective-permute-done.6.refs_3_
  24.5 0.0 collective-permute-done.5.refs_2_
  24.6 0.0 copy-done.11
  24.6 1.9 %collective-permute-done.4.refs_3_ = f32[7,32,128]{2,1,0:T(8,128)S(1)} collective-permute-done((f32[7,32,128]{2,1,0:T(8,128)S(1)}, f32[7,32,128]{2,1,0:T(8,128)S(1)}, u32[]{:S(2)}, u32[]{:S(2)}) %collective-permute-start.4) | collective-permute-done | bytes 114720 | tf_op jit(solution)/shard_map/ppermute | solution.py:285
  26.4 1.7 %group_shares.1 = (f32[16,16,128]{2,1,0:T(8,128)}, f32[7,32,128]{2,1,0:T(8,128)S(1)}) custom-call(f32[8,128]{1,0:T(8,128)S(1)} %get-tuple-element.35.refs_4_.refs_0_, f32[12,32,128]{2,1,0:T(8,128)S(1)} %get-tuple-element.36.refs_0_.refs_1_.refs_7_, f32[5,32,128]{2,1,0:T(8,128)S(1)} %get-tuple-element.44.refs_2_, ...), custom_call_target="tpu_custom_call" | custom-call | flops 2147483648 | bytes 5368709 | tf_op jit(solution)/shard_map/group_shares/pallas_call | solution.py:263
  28.1 4.5 %all-to-all-start = ((f32[16,16,128]{2,1,0:T(8,128)}), f32[16,16,128]{2,1,0:T(8,128)S(1)}, u32[]{:S(2)}, u32[]{:S(2)}) async-start(f32[16,16,128]{2,1,0:T(8,128)} %get-tuple-element.50.refs_4_), calls=%async_computation | async-start | bytes 262144 | tf_op jit(solution)/shard_map/all_to_all | solution.py:594
  32.7 1.4 %collective-permute-start.7 = (f32[4,32,128]{2,1,0:T(8,128)S(1)}, f32[4,32,128]{2,1,0:T(8,128)S(1)}, u32[]{:S(2)}, u32[]{:S(2)}) collective-permute-start(f32[4,32,128]{2,1,0:T(8,128)S(1)} %get-tuple-element.51), channel_id=1, source_target_pairs={{1,17},{33,49},{65,81},{97,113},{129,145},{161,177},{193,209},{225... | collective-permute-start | bytes 196616 | tf_op jit(solution)/shard_map/ppermute | solution.py:285
  34.1 1.4 %collective-permute-done.7.refs_2_ = f32[4,32,128]{2,1,0:T(8,128)S(1)} collective-permute-done((f32[4,32,128]{2,1,0:T(8,128)S(1)}, f32[4,32,128]{2,1,0:T(8,128)S(1)}, u32[]{:S(2)}, u32[]{:S(2)}) %collective-permute-start.7) | collective-permute-done | bytes 65568 | tf_op jit(solution)/shard_map/ppermute | solution.py:285
  35.5 3.3 %all-to-all-done.refs_0_ = f32[16,16,128]{2,1,0:T(8,128)S(1)} async-done(((f32[16,16,128]{2,1,0:T(8,128)}), f32[16,16,128]{2,1,0:T(8,128)S(1)}, u32[]{:S(2)}, u32[]{:S(2)}) %all-to-all-start) | async-done | bytes 131104 | tf_op jit(solution)/shard_map/all_to_all | solution.py:594
  38.8 1.4 %column_shares.1 = (f32[8,16,128]{2,1,0:T(8,128)}, f32[4,8,128]{2,1,0:T(8,128)S(1)}, f32[5,32,128]{2,1,0:T(8,128)S(1)}) custom-call(f32[16,16,128]{2,1,0:T(8,128)S(1)} %all-to-all-done.refs_0_, f32[5,32,128]{2,1,0:T(8,128)S(1)} %get-tuple-element.49.refs_4_.refs_1_, f32[4,32,128]{2,1,0:T(8,128)S(1)} %collective-permute-done.7.refs_2_), custom_call_target="tpu_custom_call" | custom-call | flops 2147483648 | bytes 5368709 | tf_op jit(solution)/shard_map/column_shares/pallas_call | solution.py:263
  40.2 10.4 %all-to-all-start.1 = ((f32[8,16,128]{2,1,0:T(8,128)}), f32[8,16,128]{2,1,0:T(8,128)S(1)}, u32[]{:S(2)}, u32[]{:S(2)}) async-start(f32[8,16,128]{2,1,0:T(8,128)} %get-tuple-element.52.refs_2_), calls=%async_computation.1 | async-start | bytes 131072 | tf_op jit(solution)/shard_map/all_to_all | solution.py:611
  50.7 0.7 collective-permute-start.10
  51.3 0.7 collective-permute-start.9
  52.0 4.3 %collective-permute-start.8 = (f32[4,32,128]{2,1,0:T(8,128)S(1)}, f32[4,32,128]{2,1,0:T(8,128)S(1)}, u32[]{:S(2)}, u32[]{:S(2)}) collective-permute-start(f32[4,32,128]{2,1,0:T(8,128)S(1)} %get-tuple-element.53.refs_0_), channel_id=1, source_target_pairs={{1,17},{33,49},{65,81},{97,113},{129,145},{161,177},{193,209},{225... | collective-permute-start | bytes 196616 | tf_op jit(solution)/shard_map/ppermute | solution.py:285
  56.3 1.9 %collective-permute-start.11 = (f32[46,8,128]{2,1,0:T(8,128)S(1)}, f32[46,8,128]{2,1,0:T(8,128)S(1)}, u32[]{:S(2)}, u32[]{:S(2)}) collective-permute-start(f32[46,8,128]{2,1,0:T(8,128)S(1)} %get-tuple-element.56), channel_id=1, source_target_pairs={{0,1},{1,2},{2,3},{3,4},{4,5},{5,6},{6,7},{7,8},{8,9},{9,10},{10,1... | collective-permute-start | bytes 565256 | tf_op jit(solution)/shard_map/ppermute | solution.py:285
  58.2 2.4 %collective-permute-start.12 = (f32[46,8,128]{2,1,0:T(8,128)S(1)}, f32[46,8,128]{2,1,0:T(8,128)S(1)}, u32[]{:S(2)}, u32[]{:S(2)}) collective-permute-start(f32[46,8,128]{2,1,0:T(8,128)S(1)} %get-tuple-element.57), channel_id=1, source_target_pairs={{1,0},{2,1},{3,2},{4,3},{5,4},{6,5},{7,6},{8,7},{9,8},{10,9},{11,1... | collective-permute-start | bytes 565256 | tf_op jit(solution)/shard_map/ppermute | solution.py:285
  60.7 0.0 collective-permute-done.10.refs_3_
  60.7 0.0 collective-permute-done.9.refs_2_
  60.7 0.0 collective-permute-done.8.refs_1_
  60.7 0.0 copy-start.1
  60.7 0.0 copy-start.7
  60.7 0.0 copy-start.9
  60.8 2.1 %all-to-all-done.1.refs_0_ = f32[8,16,128]{2,1,0:T(8,128)S(1)} async-done(((f32[8,16,128]{2,1,0:T(8,128)}), f32[8,16,128]{2,1,0:T(8,128)S(1)}, u32[]{:S(2)}, u32[]{:S(2)}) %all-to-all-start.1) | async-done | bytes 65568 | tf_op jit(solution)/shard_map/all_to_all | solution.py:611
  62.9 0.9 line_shares.1
  63.7 4.2 %all-to-all-start.2 = ((f32[4,8,128]{2,1,0:T(8,128)}), f32[4,8,128]{2,1,0:T(8,128)S(1)}, u32[]{:S(2)}, u32[]{:S(2)}) async-start(f32[4,8,128]{2,1,0:T(8,128)} %get-tuple-element.54), calls=%async_computation.2 | async-start | bytes 32768 | tf_op jit(solution)/shard_map/all_to_all | solution.py:629
  67.9 0.0 collective-permute-done.11.refs_3_
  67.9 0.0 collective-permute-done.12.refs_4_
  67.9 0.0 copy-done.1
  67.9 0.0 copy-done.7
  67.9 0.0 copy-done.9
  68.0 2.7 %far_field.1 = (f32[30,8,128]{2,1,0:T(8,128)S(1)}, f32[136,128]{1,0:T(8,128)S(1)}) custom-call(s32[3,30]{1,0:T(4,128)S(1)} %bitcast.10, s32[30]{0:T(128)S(1)} %copy-done.9, f32[30,8,128]{2,1,0:T(8,128)S(1)} %get-tuple-element.55.refs_1_.refs_2_, f32[46,8,128]{2,1,0:T(8,128)S(1)} %collective-permute-done.11.refs_3_, ...), custom_call_target="tpu_custom_call" | custom-call | flops 2147483648 | bytes 5368709 | tf_op jit(solution)/shard_map/far_field/pallas_call | solution.py:263
  70.6 0.7 copy-done.13
  71.3 0.8 all-to-all-done.2.refs_0_
  72.1 1.6 %top_turn.1 = f32[16,8,128]{2,1,0:T(8,128)} custom-call(f32[4,8,128]{2,1,0:T(8,128)S(1)} %all-to-all-done.2.refs_0_, f32[136,128]{1,0:T(8,128)S(1)} %get-tuple-element.60.refs_1_), custom_call_target="tpu_custom_call" | custom-call | flops 2147483648 | bytes 5368709 | tf_op jit(solution)/shard_map/top_turn/pallas_call | solution.py:263
  73.7 7.0 %all-to-all-start.3 = ((f32[16,8,128]{2,1,0:T(8,128)}), f32[16,8,128]{2,1,0:T(8,128)S(1)}, u32[]{:S(2)}, u32[]{:S(2)}) async-start(f32[16,8,128]{2,1,0:T(8,128)} %top_turn.1), calls=%async_computation.3 | async-start | bytes 131072 | tf_op jit(solution)/shard_map/all_to_all | solution.py:676
  80.7 0.0 copy-done
  80.7 0.0 copy-done.8
  80.7 0.0 copy-done.10
  80.7 3.0 %near_field.1.refs_1_ = f32[296,128]{1,0:T(8,128)S(1)} custom-call(s32[2,16]{1,0:T(2,128)S(1)} %bitcast.11, s32[16]{0:T(128)S(1)} %copy-done.10, f32[16,2048]{1,0:T(8,128)S(1)} %copy-done.6, f32[46,8,128]{2,1,0:T(8,128)S(1)} %collective-permute-done.11.refs_3_, f32[46,8,128]{2,1,0:T(8,128)S(1)} %collective-permute-done.12.refs_4_, ...), custom_call_target="tpu_custom_call" | custom-call | flops 2147483648 | bytes 5368709 | tf_op jit(solution)/shard_map/near_field/pallas_call | solution.py:263
  83.7 0.7 copy-done.12
  84.4 2.2 %all-to-all-done.3.refs_0_ = f32[16,8,128]{2,1,0:T(8,128)S(1)} async-done(((f32[16,8,128]{2,1,0:T(8,128)}), f32[16,8,128]{2,1,0:T(8,128)S(1)}, u32[]{:S(2)}, u32[]{:S(2)}) %all-to-all-start.3) | async-done | bytes 65568 | tf_op jit(solution)/shard_map/all_to_all | solution.py:676
  86.6 0.6 copy-done.14
  87.2 4.6 %downward.1 = f32[16,2048]{1,0:T(8,128)} custom-call(f32[16,8,128]{2,1,0:T(8,128)} %copy-done.14, f32[296,128]{1,0:T(8,128)} %copy-done.12, bf16[30,64,128]{2,1,0:T(8,128)(2,1)} %copy-done.11, f32[30,8,128]{2,1,0:T(8,128)} %copy-done.13, f32[16,64,128]{2,1,0:T(8,128)} %refs_4_.1), custom_call_target="tpu_custom_call" | custom-call | flops 4294967296 | bytes 10737418 | tf_op jit(solution)/shard_map/downward/pallas_call | solution.py:263
  (15 shorter events, 0.2 us)
Async XLA Ops:
  0.0 1.0 %copy-start.4 = (f32[1,9,2,4096]{3,2,1,0:T(2,128)S(1)}, f32[1,9,2,4096]{3,2,1,0:T(2,128)}, u32[]{:S(2)}) copy-start(f32[1,9,2,4096]{3,2,1,0:T(2,128)} %param.18) | copy-start | bytes 884740
  1.0 0.9 copy-start.5
  1.9 10.8 %copy-start.2 = (f32[30,4096]{1,0:T(8,128)S(1)}, f32[30,4096]{1,0:T(8,128)}, u32[]{:S(2)}) copy-start(f32[30,4096]{1,0:T(8,128)} %refs_2_.2) | copy-start | bytes 1474564
  1.9 10.8 %copy-start.3 = (f32[16,64,128]{2,1,0:T(8,128)S(1)}, f32[16,64,128]{2,1,0:T(8,128)}, u32[]{:S(2)}) copy-start(f32[16,64,128]{2,1,0:T(8,128)} %refs_4_.1) | copy-start | bytes 1572868
  1.9 10.8 %copy-start.6 = (f32[16,2048]{1,0:T(8,128)S(1)}, f32[16,2048]{1,0:T(8,128)}, u32[]{:S(2)}) copy-start(f32[16,2048]{1,0:T(8,128)} %refs_2_.3) | copy-start | bytes 393220
  2.1 9.3 %collective-permute-start.1 = (f32[14,32,128]{2,1,0:T(8,128)S(1)}, f32[14,32,128]{2,1,0:T(8,128)S(1)}, u32[]{:S(2)}, u32[]{:S(2)}) collective-permute-start(f32[14,32,128]{2,1,0:T(8,128)S(1)} %get-tuple-element.38), channel_id=1, source_target_pairs={{0,1},{16,17},{32,33},{48,49},{64,65},{80,81},{96,97},{112,113},{1... | collective-permute-start | bytes 688136 | tf_op jit(solution)/shard_map/ppermute | solution.py:285
  3.5 0.7 collective-permute-start
  11.3 2.9 %collective-permute-start.2 = (f32[3,32,128]{2,1,0:T(8,128)S(1)}, f32[3,32,128]{2,1,0:T(8,128)S(1)}, u32[]{:S(2)}, u32[]{:S(2)}) collective-permute-start(f32[3,32,128]{2,1,0:T(8,128)S(1)} %get-tuple-element.39), channel_id=1, source_target_pairs={{0,4},{8,12},{16,20},{24,28},{32,36},{40,44},{48,52},{56,60},{64,6... | collective-permute-start | bytes 147464 | tf_op jit(solution)/shard_map/ppermute | solution.py:285
  14.2 10.3 %copy-start.11 = (bf16[30,64,128]{2,1,0:T(8,128)(2,1)}, bf16[30,64,128]{2,1,0:T(8,128)(2,1)S(1)}, u32[]{:S(2)}) copy-start(bf16[30,64,128]{2,1,0:T(8,128)(2,1)S(1)} %get-tuple-element.63.refs_2_) | copy-start | bytes 1474564
  14.3 2.8 %collective-permute-start.3 = (f32[5,32,128]{2,1,0:T(8,128)S(1)}, f32[5,32,128]{2,1,0:T(8,128)S(1)}, u32[]{:S(2)}, u32[]{:S(2)}) collective-permute-start(f32[5,32,128]{2,1,0:T(8,128)S(1)} %get-tuple-element.41), channel_id=1, source_target_pairs={{0,2},{4,6},{8,10},{12,14},{16,18},{20,22},{24,26},{28,30},{32,34}... | collective-permute-start | bytes 245768 | tf_op jit(solution)/shard_map/ppermute | solution.py:285
  17.1 7.4 %collective-permute-start.5 = (f32[6,32,128]{2,1,0:T(8,128)S(1)}, f32[6,32,128]{2,1,0:T(8,128)S(1)}, u32[]{:S(2)}, u32[]{:S(2)}) collective-permute-start(f32[6,32,128]{2,1,0:T(8,128)S(1)} %get-tuple-element.47), channel_id=1, source_target_pairs={{1,33},{65,97},{129,161},{193,225},{257,289},{321,353},{385,417},{... | collective-permute-start | bytes 294920 | tf_op jit(solution)/shard_map/ppermute | solution.py:285
  18.4 6.1 %collective-permute-start.6 = (f32[4,32,128]{2,1,0:T(8,128)S(1)}, f32[4,32,128]{2,1,0:T(8,128)S(1)}, u32[]{:S(2)}, u32[]{:S(2)}) collective-permute-start(f32[4,32,128]{2,1,0:T(8,128)S(1)} %get-tuple-element.48), channel_id=1, source_target_pairs={{1,97},{129,225},{257,353},{385,481}} | collective-permute-start | bytes 196616 | tf_op jit(solution)/shard_map/ppermute | solution.py:285
  23.2 3.2 %collective-permute-start.4 = (f32[7,32,128]{2,1,0:T(8,128)S(1)}, f32[7,32,128]{2,1,0:T(8,128)S(1)}, u32[]{:S(2)}, u32[]{:S(2)}) collective-permute-start(f32[7,32,128]{2,1,0:T(8,128)S(1)} %get-tuple-element.45), channel_id=1, source_target_pairs={{0,1},{2,3},{4,5},{6,7},{8,9},{10,11},{12,13},{14,15},{16,17},{18,... | collective-permute-start | bytes 344072 | tf_op jit(solution)/shard_map/ppermute | solution.py:285
  28.1 10.6 %all-to-all-start = ((f32[16,16,128]{2,1,0:T(8,128)}), f32[16,16,128]{2,1,0:T(8,128)S(1)}, u32[]{:S(2)}, u32[]{:S(2)}) async-start(f32[16,16,128]{2,1,0:T(8,128)} %get-tuple-element.50.refs_4_), calls=%async_computation | async-start | bytes 262144 | tf_op jit(solution)/shard_map/all_to_all | solution.py:594
  32.7 2.8 %collective-permute-start.7 = (f32[4,32,128]{2,1,0:T(8,128)S(1)}, f32[4,32,128]{2,1,0:T(8,128)S(1)}, u32[]{:S(2)}, u32[]{:S(2)}) collective-permute-start(f32[4,32,128]{2,1,0:T(8,128)S(1)} %get-tuple-element.51), channel_id=1, source_target_pairs={{1,17},{33,49},{65,81},{97,113},{129,145},{161,177},{193,209},{225... | collective-permute-start | bytes 196616 | tf_op jit(solution)/shard_map/ppermute | solution.py:285
  40.2 22.6 %all-to-all-start.1 = ((f32[8,16,128]{2,1,0:T(8,128)}), f32[8,16,128]{2,1,0:T(8,128)S(1)}, u32[]{:S(2)}, u32[]{:S(2)}) async-start(f32[8,16,128]{2,1,0:T(8,128)} %get-tuple-element.52.refs_2_), calls=%async_computation.1 | async-start | bytes 131072 | tf_op jit(solution)/shard_map/all_to_all | solution.py:611
  50.7 10.0 %collective-permute-start.10 = (f32[4,32,128]{2,1,0:T(8,128)S(1)}, f32[4,32,128]{2,1,0:T(8,128)S(1)}, u32[]{:S(2)}, u32[]{:S(2)}) collective-permute-start(f32[4,32,128]{2,1,0:T(8,128)S(1)} %get-tuple-element.53.refs_0_), channel_id=1, source_target_pairs={{97,81},{225,209},{353,337},{481,465}} | collective-permute-start | bytes 196616 | tf_op jit(solution)/shard_map/ppermute | solution.py:285
  51.3 9.3 %collective-permute-start.9 = (f32[4,32,128]{2,1,0:T(8,128)S(1)}, f32[4,32,128]{2,1,0:T(8,128)S(1)}, u32[]{:S(2)}, u32[]{:S(2)}) collective-permute-start(f32[4,32,128]{2,1,0:T(8,128)S(1)} %get-tuple-element.53.refs_0_), channel_id=1, source_target_pairs={{97,65},{225,193},{353,321},{481,449}} | collective-permute-start | bytes 196616 | tf_op jit(solution)/shard_map/ppermute | solution.py:285
  52.0 8.7 %collective-permute-start.8 = (f32[4,32,128]{2,1,0:T(8,128)S(1)}, f32[4,32,128]{2,1,0:T(8,128)S(1)}, u32[]{:S(2)}, u32[]{:S(2)}) collective-permute-start(f32[4,32,128]{2,1,0:T(8,128)S(1)} %get-tuple-element.53.refs_0_), channel_id=1, source_target_pairs={{1,17},{33,49},{65,81},{97,113},{129,145},{161,177},{193,209},{225... | collective-permute-start | bytes 196616 | tf_op jit(solution)/shard_map/ppermute | solution.py:285
  56.3 11.6 %collective-permute-start.11 = (f32[46,8,128]{2,1,0:T(8,128)S(1)}, f32[46,8,128]{2,1,0:T(8,128)S(1)}, u32[]{:S(2)}, u32[]{:S(2)}) collective-permute-start(f32[46,8,128]{2,1,0:T(8,128)S(1)} %get-tuple-element.56), channel_id=1, source_target_pairs={{0,1},{1,2},{2,3},{3,4},{4,5},{5,6},{6,7},{7,8},{8,9},{9,10},{10,1... | collective-permute-start | bytes 565256 | tf_op jit(solution)/shard_map/ppermute | solution.py:285
  58.2 9.7 %collective-permute-start.12 = (f32[46,8,128]{2,1,0:T(8,128)S(1)}, f32[46,8,128]{2,1,0:T(8,128)S(1)}, u32[]{:S(2)}, u32[]{:S(2)}) collective-permute-start(f32[46,8,128]{2,1,0:T(8,128)S(1)} %get-tuple-element.57), channel_id=1, source_target_pairs={{1,0},{2,1},{3,2},{4,3},{5,4},{6,5},{7,6},{8,7},{9,8},{10,9},{11,1... | collective-permute-start | bytes 565256 | tf_op jit(solution)/shard_map/ppermute | solution.py:285
  60.7 7.2 %copy-start.1 = (f32[30,3,4096]{2,0,1:T(8,128)S(1)}, f32[30,3,4096]{2,0,1:T(8,128)}, u32[]{:S(2)}) copy-start(f32[30,3,4096]{2,0,1:T(8,128)} %param.14) | copy-start | bytes 4423684
  60.7 7.2 %copy-start.7 = (s32[30,3]{0,1:T(4,128)S(1)}, s32[30,3]{0,1:T(4,128)}, u32[]{:S(2)}) copy-start(s32[30,3]{0,1:T(4,128)} %param.15) | copy-start | bytes 1084
  60.7 7.2 %copy-start.9 = (s32[30]{0:T(128)S(1)}, s32[30]{0:T(128)}, u32[]{:S(2)}) copy-start(s32[30]{0:T(128)} %refs_1_.4) | copy-start | bytes 364
  63.7 8.4 %all-to-all-start.2 = ((f32[4,8,128]{2,1,0:T(8,128)}), f32[4,8,128]{2,1,0:T(8,128)S(1)}, u32[]{:S(2)}, u32[]{:S(2)}) async-start(f32[4,8,128]{2,1,0:T(8,128)} %get-tuple-element.54), calls=%async_computation.2 | async-start | bytes 32768 | tf_op jit(solution)/shard_map/all_to_all | solution.py:629
  70.6 0.7 copy-start.13
  72.1 8.6 %copy-start = (f32[16,2,128,128]{3,2,1,0:T(8,128)S(1)}, f32[16,2,128,128]{3,2,1,0:T(8,128)}, u32[]{:S(2)}) copy-start(f32[16,2,128,128]{3,2,1,0:T(8,128)} %refs_5_.1) | copy-start | bytes 6291460
  72.1 8.6 %copy-start.8 = (s32[16,2]{0,1:T(2,128)S(1)}, s32[16,2]{0,1:T(2,128)}, u32[]{:S(2)}) copy-start(s32[16,2]{0,1:T(2,128)} %param.20) | copy-start | bytes 388
  72.1 8.6 %copy-start.10 = (s32[16]{0:T(128)S(1)}, s32[16]{0:T(128)}, u32[]{:S(2)}) copy-start(s32[16]{0:T(128)} %refs_1_.5) | copy-start | bytes 196
  73.7 12.9 %all-to-all-start.3 = ((f32[16,8,128]{2,1,0:T(8,128)}), f32[16,8,128]{2,1,0:T(8,128)S(1)}, u32[]{:S(2)}, u32[]{:S(2)}) async-start(f32[16,8,128]{2,1,0:T(8,128)} %top_turn.1), calls=%async_computation.3 | async-start | bytes 131072 | tf_op jit(solution)/shard_map/all_to_all | solution.py:676
  83.7 0.7 copy-start.12
  86.6 0.6 copy-start.14

commit v5 on v4

--- a/solution.py
+++ b/solution.py
@@ -71,7 +71,7 @@
 
 
 def row_form(packed):
-    left = lanes(8) < 64
+    left = lanes(packed.shape[0]) < 64
     turned = pltpu.roll(packed, 64, 1)
     zero = jnp.zeros_like(packed)
     full = jnp.concatenate(
@@ -88,13 +88,17 @@
 
 def times_t_raw(rows, forms):
     out = dot_t(rows, forms)
-    return out[:32] + pltpu.roll(out[:32], 96, 1) + out[32:]
+    half = out.shape[0] // 2
+    return out[:half] + pltpu.roll(out[:half], 96, 1) + out[half:]
 
 
 def weave(raw, child):
-    lane = lanes(8)
+    rows = raw.shape[0] // 4
+    lane = lanes(rows)
     place = 64 * child + (lane % 64) // 2
-    pick = [jnp.take_along_axis(raw[8 * k : 8 * k + 8], place, axis=1) for k in range(4)]
+    pick = [
+        jnp.take_along_axis(raw[rows * k : rows * k + rows], place, axis=1) for k in range(4)
+    ]
     even = lane % 2 == 0
     return jnp.where(
         lane < 64, jnp.where(even, pick[0], pick[2]), jnp.where(even, pick[1], pick[3])
@@ -144,14 +148,19 @@
                 root[...] = value
 
 
-def edge_kernel(sources, coefs, forward, backward):
-    forward[0:LOCAL] = coefs[...]
-    backward[0:LOCAL] = coefs[...]
-    for leaf in range(LEAVES):
-        edge, place = (backward, leaf) if leaf < REACH else (forward, leaf - REACH)
-        entries = sources[:, leaf * POINTS : (leaf + 1) * POINTS]
-        edge[LOCAL + 2 * place] = entries[:8]
-        edge[LOCAL + 2 * place + 1] = entries[8:]
+def edge_kernel(sources, coefs, inner, outer):
+    odd = (place_of_device()[0] & 1) == 1
+    inner[0:LOCAL] = coefs[...]
+    outer[0:LOCAL] = coefs[...]
+    for place in range(REACH):
+        first = sources[:, place * POINTS : (place + 1) * POINTS]
+        last = sources[:, (REACH + place) * POINTS : (REACH + place + 1) * POINTS]
+        for edge, value in (
+            (inner, jnp.where(odd, first, last)),
+            (outer, jnp.where(odd, last, first)),
+        ):
+            edge[LOCAL + 2 * place] = value[:8]
+            edge[LOCAL + 2 * place + 1] = value[8:]
 
 
 def group_sums(sibling, raw, table, out):
@@ -168,15 +177,17 @@
     out[NEAR_ROWS + 8 : NEAR_ROWS + 40] = product
 
 
-def near_kernel(partner, count, own, low, high, block, sibling, raw, table, out, leaves):
+def near_kernel(partner, count, own, inner, outer, block, sibling, raw, table, out, leaves):
     group_sums(sibling, raw, table, out)
+    odd = (place_of_device()[0] & 1) == 1
     for leaf in range(LEAVES):
         leaves[REACH + leaf] = own[:, leaf * POINTS : (leaf + 1) * POINTS]
     for leaf in range(REACH):
         for half in range(2):
             rows = slice(8 * half, 8 * half + 8)
-            leaves[leaf, rows] = low[LOCAL + 2 * leaf + half]
-            leaves[REACH + LEAVES + leaf, rows] = high[LOCAL + 2 * leaf + half]
+            place = LOCAL + 2 * leaf + half
+            leaves[leaf, rows] = jnp.where(odd, inner[place], outer[place])
+            leaves[REACH + LEAVES + leaf, rows] = jnp.where(odd, outer[place], inner[place])
     first = place_of_device()[0] * LEAVES - REACH
     for leaf in range(LEAVES):
         total = None
@@ -192,7 +203,8 @@
 
 
 def top_sums(low, upper, sums, out):
-    value = times(sums[2], upper[3])
+    second_half = ((place_of_device()[2] >> 2) & 1) == 1
+    value = times(sums[2], choose(second_half, upper[4], upper[3]))
     value = times_t(value, low[2]) + times(sums[1], low[1])
     out[0:8] = times_t(value, low[4]) + times(sums[0], low[3])
     out[8:40] = times(times(low[4], low[2]), low[0])
@@ -201,13 +213,14 @@
 
 
 def far_kernel(
-    partner, count, own, low, high, coupling, low_table, upper, sums, out, prepared, extended
+    partner, count, own, inner, outer, coupling, low_table, upper, sums, out, prepared, extended
 ):
     top_sums(low_table, upper, sums, prepared)
     device = place_of_device()[0]
-    extended[0:LOCAL] = low[0:LOCAL]
+    odd = (device & 1) == 1
+    extended[0:LOCAL] = jnp.where(odd, inner[0:LOCAL], outer[0:LOCAL])
     extended[LOCAL : 2 * LOCAL] = own[...]
-    extended[2 * LOCAL : 3 * LOCAL] = high[0:LOCAL]
+    extended[2 * LOCAL : 3 * LOCAL] = jnp.where(odd, outer[0:LOCAL], inner[0:LOCAL])
     tables = [coupling[slot].reshape(LOCAL, 32, 128) for slot in range(SLOTS)]
     for clusters, offset in LAYOUT:
         for cluster in range(clusters):
@@ -337,6 +350,7 @@
     @pl.when(place_of_device()[1] == PORTER)
     def _():
         pay[0] = top_raw[HIGH + 6]
+        pay[1] = top_raw[HIGH]
 
 
 def second_kernel(raw, arrived, live, top_raw, out, pay, ninth):
@@ -345,41 +359,49 @@
     _, member, group = place_of_device()
     value = choose(((group >> 4) & 1) == 1, arrived[0], top_raw[HIGH + 3])
     ninth[0] = value
+    ninth[1] = arrived[1]
 
     @pl.when(member == PORTER)
     def _():
         pay[0] = value
         pay[1] = top_raw[HIGH + 5]
-
-
-def third_kernel(raw, arrived, live, top_raw, ninth, out, pay, upper, near_pay, far_pay):
+        pay[2] = arrived[1]
+
+
+def third_kernel(raw, arrived, live, top_raw, ninth, out, pay, upper, near_pay):
     merge_group(raw, 1, live, arrived, out)
     group_payload(raw, 0, out, pay)
-    _, _, group = place_of_device()
+    _, member, group = place_of_device()
     right_child = ((group >> 3) & 1) == 1
-    values = (
-        top_raw[HIGH],
-        choose(right_child, arrived[0], ninth[0]),
-        choose(right_child, arrived[1], top_raw[HIGH + 2]),
-    )
-    for target, side in ((upper, 1), (near_pay, 1), (far_pay, 4)):
-        for entry in range(3):
-            target[entry] = values[entry]
-        target[3] = top_raw[HIGH + side]
-    near_pay[4] = top_raw[2]
-    near_pay[5] = top_raw[6]
+    upper[...] = jnp.zeros_like(upper)
+
+    @pl.when((member == PORTER) & ((group & 7) == 0))
+    def _():
+        own = top_raw[HIGH]
+        across = choose(right_child, arrived[0], ninth[0])
+        upper[0] = times_t(times(ninth[1], across), own)
+        upper[1] = times_t(times(arrived[2], across), own)
+        upper[2] = choose(right_child, arrived[1], top_raw[HIGH + 2])
+
+    upper[3] = top_raw[HIGH + 1]
+    upper[4] = top_raw[HIGH + 4]
+    near_pay[0:5] = upper[...]
+    near_pay[5] = top_raw[2]
+    near_pay[6] = top_raw[6]
 
 
 def fourth_kernel(top_raw, upper, near_in, far_in, out, keep, low_pay):
     _, _, group = place_of_device()
     place = group & 7
-    for entry in range(4):
-        out[entry] = choose(
+    for entry in range(5):
+        value = choose(
             place == 2, near_in[entry], choose(place == 6, far_in[entry], upper[entry])
         )
+        out[entry] = value
+        low_pay[4 + entry] = value
     second = ((group >> 1) & 1) == 1
-    sixth = choose(second, near_in[4], top_raw[2])
-    coupling = choose(second, near_in[5], top_raw[4])
+    sixth = choose(second, near_in[5], top_raw[2])
+    coupling = choose(second, near_in[6], top_raw[4])
     for target, side in ((keep, 3), (low_pay, 5)):
         target[0] = sixth
         target[1] = coupling
@@ -434,34 +456,32 @@
         blocks[other, 8:16] = value
 
 
-def fifth_kernel(upper, near_in, far_in, next_in, out):
+def fifth_kernel(upper, low_in, far_in, out):
     _, _, group = place_of_device()
     place = group & 7
-    for entry in range(4):
-        even = choose(place == 4, far_in[entry], upper[entry])
-        odd = choose(place == 5, next_in[entry], near_in[entry])
-        out[entry] = choose((place & 1) == 1, odd, even)
-
-
-def middle_kernel(given, upper, blocks, sums):
+    for entry in range(5):
+        value = choose((place & 1) == 1, low_in[4 + entry], upper[entry])
+        out[entry] = choose((place == 4) | (place == 5), far_in[entry], value)
+
+
+def middle_kernel(given, blocks, sums):
     _, _, group = place_of_device()
-    place, line = group & 7, group >> 3
+    place = group & 7
+    value = total_of([given[other, 8:16] for other in range(8)])
+    for other in range(4):
+        blocks[other] = value
     for level in range(3):
         sums[level] = total_of(
             [given[place ^ apart, 0:8] for apart in range(1 << level, 2 << level)]
         )
-    value = total_of([given[other, 8:16] for other in range(8)])
-    raised = times(value, upper[0])
-    for other in range(4):
-        blocks[other] = choose((line ^ other) >= 2, raised, value)
 
 
 def turn_kernel(given, prepared, out):
     _, _, group = place_of_device()
     line = group >> 3
-    seventh = times(given[line ^ 1], prepared[104:136])
-    eighth = times(given[line ^ 2] + given[line ^ 3], prepared[72:104])
-    value = times_t(eighth, prepared[40:72]) + seventh
+    left = [coef_form(given[line ^ apart]) for apart in (2, 3, 1)]
+    right = [table_form(prepared[40 + 32 * entry : 72 + 32 * entry]) for entry in range(3)]
+    value = fold(dot(jnp.concatenate(left, axis=1), jnp.concatenate(right, axis=0)))
     value = times_t(value, prepared[8:40]) + prepared[0:8]
     for other in range(GROUP):
         out[other] = value
@@ -505,8 +525,7 @@
     near_count,
 ):
     count = lax.axis_size("leaf")
-    forward = [(i, i + 1) for i in range(count - 1)]
-    backward = [(i + 1, i) for i in range(count - 1)]
+    forward = [(i, i + 1) for i in range(1, count - 1, 2)]
 
     def handed(value, period, first, second):
         return permute(value, [(i + first, i + second) for i in range(0, count, period)])
@@ -541,40 +560,41 @@
         [raw, group_in, top_raw],
         flops=1 << 29,
     )
-    pairs = [(i, i + 4) for i in range(0, count, 8)] + [(PORTER, 256 + PORTER)]
+    pairs = [(i, i + 4) for i in range(0, count, 8)]
+    pairs += [(i + PORTER, (i ^ 256) + PORTER) for i in range(0, count, 128)]
     group_in = permute(pay, pairs)
     live, pay, ninth = call(
         second_kernel,
         "hand_down_2",
-        [tables(3), tables(5), tables(1)],
+        [tables(3), tables(5), tables(2)],
         [raw, group_in, live, top_raw],
         after=[root],
         flops=1 << 29,
     )
     pairs = [(i, i + 2) for i in range(0, count, 4)]
-    pairs += [(i + PORTER, i + 128 + PORTER) for i in range(0, count, 256)]
+    pairs += [(i + PORTER, (i ^ 128) + PORTER) for i in range(0, count, 128)]
     group_in = permute(pay, pairs)
-    live, pay, upper, near_pay, far_pay = call(
+    live, pay, upper, near_pay = call(
         third_kernel,
         "hand_down_3",
-        [tables(5), tables(7), tables(4), tables(6), tables(4)],
+        [tables(5), tables(7), tables(5), tables(7)],
         [raw, group_in, live, top_raw, ninth],
         flops=1 << 29,
     )
     group_in = handed(pay, 2, 0, 1)
     near_in = handed(near_pay, 64, PORTER, 32 + PORTER)
-    far_in = handed(far_pay, 128, PORTER, 96 + PORTER)
+    far_in = handed(upper, 128, PORTER, 96 + PORTER)
     upper, keep, low_pay = call(
         fourth_kernel,
         "hand_down_4",
-        [tables(4), tables(5), tables(4)],
+        [tables(5), tables(5), tables(9)],
         [top_raw, upper, near_in, far_in],
         flops=1 << 29,
     )
     low_in = handed(low_pay, 32, PORTER, 16 + PORTER)
-    near_in = handed(upper, 32, PORTER, 16 + PORTER)
-    far_in = handed(upper, 128, 96 + PORTER, 64 + PORTER)
-    next_in = handed(upper, 128, 96 + PORTER, 80 + PORTER)
+    pairs = [(i + 32 + PORTER, i + 64 + PORTER) for i in range(0, count, 128)]
+    pairs += [(i + 96 + PORTER, i + 80 + PORTER) for i in range(0, count, 128)]
+    far_in = permute(upper, pairs)
     shares, group_table = call(
         share_kernel,
         "group_shares",
@@ -592,14 +612,6 @@
     ]
     in_line = [list(range(first, count, 128)) for first in range(128)]
     given = lax.all_to_all(shares, "leaf", 0, 0, axis_index_groups=in_group)
-    upper = call(
-        fifth_kernel,
-        "hand_down_5",
-        [tables(4)],
-        [upper, near_in, far_in, next_in],
-        after=[shares],
-        flops=1 << 29,
-    )
     blocks, sibling, low_table = call(
         rise_kernel,
         "column_shares",
@@ -609,7 +621,7 @@
         flops=2 << 30,
     )
     given = lax.all_to_all(blocks, "leaf", 0, 0, axis_index_groups=in_column)
-    low_edge, high_edge = call(
+    inner, outer = call(
         edge_kernel,
         "edges",
         [shape(LOCAL + 2 * REACH, 8, 128)] * 2,
@@ -617,14 +629,22 @@
         after=[blocks],
         flops=1 << 29,
     )
-    low_edge = permute(low_edge, forward)
-    high_edge = permute(high_edge, backward)
+    inner = permute(inner, [(i, i ^ 1) for i in range(count)])
+    outer = permute(outer, forward + [(second, first) for first, second in forward])
     blocks, sums = call(
         middle_kernel,
         "line_shares",
         [shape(4, 8, 128), shape(3, 8, 128)],
-        [given, upper],
+        [given],
         flops=1 << 30,
+    )
+    upper = call(
+        fifth_kernel,
+        "hand_down_5",
+        [tables(5)],
+        [upper, low_in, far_in],
+        after=[blocks],
+        flops=1 << 29,
     )
     given = lax.all_to_all(blocks, "leaf", 0, 0, axis_index_groups=in_line)
 
@@ -636,8 +656,8 @@
             near_partner.T,
             near_count,
             sources,
-            low_edge,
-            high_edge,
+            inner,
+            outer,
             near_block,
             sibling,
             raw,
@@ -655,8 +675,8 @@
             far_partner.T,
             far_count,
             coefs,
-            low_edge,
-            high_edge,
+            inner,
+            outer,
             far_coupling.transpose(1, 0, 2),
             low_table,
             upper,

time: 92.5 us -> 91.9 us (level)
  starting transfers between devices: 49.5 us -> 39.7 us
  waiting for transfers between devices: 20.3 us -> 29.6 us
    ppermute x13 -> x11, starting transfers between devices: 23.4 us -> 16.7 us  [permute(): return lax.ppermute(value, 'leaf', pairs)]
    ppermute x13 -> x11, waiting for transfers between devices: 11.9 us -> 17.5 us  [permute(): return lax.ppermute(value, 'leaf', pairs)]
    all_to_all x1, waiting for transfers between devices: 2.1 us -> 6.54 us  [on_device(): given = lax.all_to_all(blocks, 'leaf', 0, 0, axis_index_groups=in_column)]
    all_to_all x1, starting transfers between devices: 10.4 us -> 8.45 us  [on_device(): given = lax.all_to_all(blocks, 'leaf', 0, 0, axis_index_groups=in_column)]
    all_to_all x1, starting transfers between devices: 4.5 us -> 3.45 us  [on_device(): given = lax.all_to_all(shares, 'leaf', 0, 0, axis_index_groups=in_group)]
  transfers between devices with their start and end apart: 17 -> 15, of which waited for: 8 -> 10; matrix products, arithmetic and copies ran while one was open for 0% -> 0% of each run, Pallas kernels for 9% -> 9%
where the time goes in v5:
time: 91.9 us; the launch traced here: 91.2 us
  starting transfers between devices  39.7 us (43%)
  waiting for transfers between devices  29.6 us (32%)
  Pallas kernels  17.8 us (19%)
  local copies, waits for them, and re-layouts  3.88 us (4%)
    pallas_call x15, Pallas kernels, call(): pl.pallas_call(body, out_shape=list(outs), in_specs=[smem] * scalars + [v...  17.8 us
    ppermute x11, waiting for transfers between devices, permute(): return lax.ppermute(value, 'leaf', pairs)  17.5 us
    ppermute x11, starting transfers between devices, permute(): return lax.ppermute(value, 'leaf', pairs)  16.7 us
    all_to_all x1, starting transfers between devices, on_device(): given = lax.all_to_all(blocks, 'leaf', 0, 0, axis_index_groups=in_column)  8.45 us
    all_to_all x1, starting transfers between devices, on_device(): given = lax.all_to_all(turned, 'leaf', 0, 0, axis_index_groups=in_group)  6.99 us
    all_to_all x1, waiting for transfers between devices, on_device(): given = lax.all_to_all(blocks, 'leaf', 0, 0, axis_index_groups=in_column)  6.54 us
    all_to_all x1, starting transfers between devices, on_device(): given = lax.all_to_all(blocks, 'leaf', 0, 0, axis_index_groups=in_line)  4.18 us
    unnamed x30, local copies, waits for them, and re-layouts  3.88 us
  transfers between devices with their start and end apart: 15, of which 10 were waited for; matrix products, arithmetic and copies ran while one was open for 0% of the time, Pallas kernels for 9%

profile of v5, /device:TPU:1, one launch (start us, length us, event | category | flops | bytes accessed | tf_op | source)
XLA Modules:
  0.0 91.2 jit_solution(11931126879773145461)
XLA Ops:
  0.0 0.0 copy-start.4
  0.0 1.0 %copy-done.4 = f32[1,9,2,4096]{3,2,1,0:T(2,128)S(1)} copy-done((f32[1,9,2,4096]{3,2,1,0:T(2,128)S(1)}, f32[1,9,2,4096]{3,2,1,0:T(2,128)}, u32[]{:S(2)}) %copy-start.4) | copy-done | bytes 294936
  1.0 0.0 copy-start.5
  1.0 0.9 copy-done.5
  1.9 0.0 copy-start.2
  1.9 0.0 copy-start.3
  1.9 0.0 copy-start.6
  1.9 0.2 top_tables.1
  2.1 1.4 %collective-permute-start.1 = (f32[14,32,128]{2,1,0:T(8,128)S(1)}, f32[14,32,128]{2,1,0:T(8,128)S(1)}, u32[]{:S(2)}, u32[]{:S(2)}) collective-permute-start(f32[14,32,128]{2,1,0:T(8,128)S(1)} %get-tuple-element.37), channel_id=1, source_target_pairs={{0,1},{16,17},{32,33},{48,49},{64,65},{80,81},{96,97},{112,113},{1... | collective-permute-start | bytes 688136 | tf_op jit(solution)/shard_map/ppermute | solution.py:298
  3.5 0.7 collective-permute-start
  4.2 0.0 collective-permute-done.refs_1_
  4.2 7.2 %collective-permute-done.1.refs_2_.refs_3_.refs_0_ = f32[14,32,128]{2,1,0:T(8,128)S(1)} collective-permute-done((f32[14,32,128]{2,1,0:T(8,128)S(1)}, f32[14,32,128]{2,1,0:T(8,128)S(1)}, u32[]{:S(2)}, u32[]{:S(2)}) %collective-permute-start.1) | collective-permute-done | bytes 229408 | tf_op jit(solution)/shard_map/ppermute | solution.py:298
  11.3 1.9 %collective-permute-start.2 = (f32[3,32,128]{2,1,0:T(8,128)S(1)}, f32[3,32,128]{2,1,0:T(8,128)S(1)}, u32[]{:S(2)}, u32[]{:S(2)}) collective-permute-start(f32[3,32,128]{2,1,0:T(8,128)S(1)} %get-tuple-element.38), channel_id=1, source_target_pairs={{0,4},{8,12},{16,20},{24,28},{32,36},{40,44},{48,52},{56,60},{64,6... | collective-permute-start | bytes 147464 | tf_op jit(solution)/shard_map/ppermute | solution.py:298
  13.3 0.0 copy-done.2
  13.3 0.0 copy-done.3
  13.3 0.0 copy-done.6
  13.3 1.6 %upward.1 = (f32[30,8,128]{2,1,0:T(8,128)S(1)}, f32[8,128]{1,0:T(8,128)S(1)}, bf16[30,64,128]{2,1,0:T(8,128)(2,1)S(1)}) custom-call(f32[16,2048]{1,0:T(8,128)S(1)} %copy-done.6, f32[16,64,128]{2,1,0:T(8,128)S(1)} %copy-done.3, f32[30,4096]{1,0:T(8,128)S(1)} %copy-done.2), custom_call_target="tpu_custom_call" | custom-call | flops 2147483648 | bytes 5368709 | tf_op jit(solution)/shard_map/upward/pallas_call | solution.py:276
  14.9 0.0 copy-start.11
  14.9 2.8 %collective-permute-done.2.refs_1_ = f32[3,32,128]{2,1,0:T(8,128)S(1)} collective-permute-done((f32[3,32,128]{2,1,0:T(8,128)S(1)}, f32[3,32,128]{2,1,0:T(8,128)S(1)}, u32[]{:S(2)}, u32[]{:S(2)}) %collective-permute-start.2) | collective-permute-done | bytes 49184 | tf_op jit(solution)/shard_map/ppermute | solution.py:298
  17.7 1.9 %collective-permute-start.3 = (f32[5,32,128]{2,1,0:T(8,128)S(1)}, f32[5,32,128]{2,1,0:T(8,128)S(1)}, u32[]{:S(2)}, u32[]{:S(2)}) collective-permute-start(f32[5,32,128]{2,1,0:T(8,128)S(1)} %get-tuple-element.40), channel_id=1, source_target_pairs={{0,2},{4,6},{8,10},{12,14},{16,18},{20,22},{24,26},{28,30},{32,34}... | collective-permute-start | bytes 245768 | tf_op jit(solution)/shard_map/ppermute | solution.py:298
  19.6 3.3 %collective-permute-done.3.refs_1_ = f32[5,32,128]{2,1,0:T(8,128)S(1)} collective-permute-done((f32[5,32,128]{2,1,0:T(8,128)S(1)}, f32[5,32,128]{2,1,0:T(8,128)S(1)}, u32[]{:S(2)}, u32[]{:S(2)}) %collective-permute-start.3) | collective-permute-done | bytes 81952 | tf_op jit(solution)/shard_map/ppermute | solution.py:298
  22.9 0.7 hand_down_3.1
  23.6 1.3 %collective-permute-start.5 = (f32[7,32,128]{2,1,0:T(8,128)S(1)}, f32[7,32,128]{2,1,0:T(8,128)S(1)}, u32[]{:S(2)}, u32[]{:S(2)}) collective-permute-start(f32[7,32,128]{2,1,0:T(8,128)S(1)} %get-tuple-element.46), channel_id=1, source_target_pairs={{1,33},{65,97},{129,161},{193,225},{257,289},{321,353},{385,417},{... | collective-permute-start | bytes 344072 | tf_op jit(solution)/shard_map/ppermute | solution.py:298
  24.9 1.3 %collective-permute-start.6 = (f32[5,32,128]{2,1,0:T(8,128)S(1)}, f32[5,32,128]{2,1,0:T(8,128)S(1)}, u32[]{:S(2)}, u32[]{:S(2)}) collective-permute-start(f32[5,32,128]{2,1,0:T(8,128)S(1)} %get-tuple-element.45.refs_1_), channel_id=1, source_target_pairs={{1,97},{129,225},{257,353},{385,481}} | collective-permute-start | bytes 245768 | tf_op jit(solution)/shard_map/ppermute | solution.py:298
  26.2 1.3 %collective-permute-start.4 = (f32[7,32,128]{2,1,0:T(8,128)S(1)}, f32[7,32,128]{2,1,0:T(8,128)S(1)}, u32[]{:S(2)}, u32[]{:S(2)}) collective-permute-start(f32[7,32,128]{2,1,0:T(8,128)S(1)} %get-tuple-element.44), channel_id=1, source_target_pairs={{0,1},{2,3},{4,5},{6,7},{8,9},{10,11},{12,13},{14,15},{16,17},{18,... | collective-permute-start | bytes 344072 | tf_op jit(solution)/shard_map/ppermute | solution.py:298
  27.5 0.2 collective-permute-done.6.refs_3_
  27.6 0.0 collective-permute-done.5.refs_2_
  27.7 0.0 copy-done.11
  27.7 1.7 %collective-permute-done.4.refs_3_ = f32[7,32,128]{2,1,0:T(8,128)S(1)} collective-permute-done((f32[7,32,128]{2,1,0:T(8,128)S(1)}, f32[7,32,128]{2,1,0:T(8,128)S(1)}, u32[]{:S(2)}, u32[]{:S(2)}) %collective-permute-start.4) | collective-permute-done | bytes 114720 | tf_op jit(solution)/shard_map/ppermute | solution.py:298
  29.4 1.7 %group_shares.1 = (f32[16,16,128]{2,1,0:T(8,128)}, f32[7,32,128]{2,1,0:T(8,128)S(1)}) custom-call(f32[8,128]{1,0:T(8,128)S(1)} %get-tuple-element.34.refs_4_.refs_0_, f32[12,32,128]{2,1,0:T(8,128)S(1)} %get-tuple-element.35.refs_0_.refs_1_.refs_7_, f32[5,32,128]{2,1,0:T(8,128)S(1)} %get-tuple-element.43.refs_2_, ...), custom_call_target="tpu_custom_call" | custom-call | flops 2147483648 | bytes 5368709 | tf_op jit(solution)/shard_map/group_shares/pallas_call | solution.py:276
  31.1 3.5 %all-to-all-start = ((f32[16,16,128]{2,1,0:T(8,128)}), f32[16,16,128]{2,1,0:T(8,128)S(1)}, u32[]{:S(2)}, u32[]{:S(2)}) async-start(f32[16,16,128]{2,1,0:T(8,128)} %get-tuple-element.48), calls=%async_computation | async-start | bytes 262144 | tf_op jit(solution)/shard_map/all_to_all | solution.py:614
  34.6 1.3 %collective-permute-start.7 = (f32[9,32,128]{2,1,0:T(8,128)S(1)}, f32[9,32,128]{2,1,0:T(8,128)S(1)}, u32[]{:S(2)}, u32[]{:S(2)}) collective-permute-start(f32[9,32,128]{2,1,0:T(8,128)S(1)} %get-tuple-element.49), channel_id=1, source_target_pairs={{1,17},{33,49},{65,81},{97,113},{129,145},{161,177},{193,209},{225... | collective-permute-start | bytes 442376 | tf_op jit(solution)/shard_map/ppermute | solution.py:298
  35.9 2.4 %collective-permute-done.7.refs_2_.refs_1_ = f32[9,32,128]{2,1,0:T(8,128)S(1)} collective-permute-done((f32[9,32,128]{2,1,0:T(8,128)S(1)}, f32[9,32,128]{2,1,0:T(8,128)S(1)}, u32[]{:S(2)}, u32[]{:S(2)}) %collective-permute-start.7) | collective-permute-done | bytes 147488 | tf_op jit(solution)/shard_map/ppermute | solution.py:298
  38.3 2.5 %all-to-all-done.refs_0_ = f32[16,16,128]{2,1,0:T(8,128)S(1)} async-done(((f32[16,16,128]{2,1,0:T(8,128)}), f32[16,16,128]{2,1,0:T(8,128)S(1)}, u32[]{:S(2)}, u32[]{:S(2)}) %all-to-all-start) | async-done | bytes 131104 | tf_op jit(solution)/shard_map/all_to_all | solution.py:614
  40.8 1.4 %column_shares.1 = (f32[8,16,128]{2,1,0:T(8,128)}, f32[4,8,128]{2,1,0:T(8,128)S(1)}, f32[5,32,128]{2,1,0:T(8,128)S(1)}) custom-call(f32[16,16,128]{2,1,0:T(8,128)S(1)} %all-to-all-done.refs_0_, f32[5,32,128]{2,1,0:T(8,128)S(1)} %get-tuple-element.47.refs_4_.refs_1_, f32[9,32,128]{2,1,0:T(8,128)S(1)} %collective-permute-done.7.refs_2_.refs_1_), custom_call_target="tpu_custom_call" | custom-call | flops 2147483648 | bytes 5368709 | tf_op jit(solution)/shard_map/column_shares/pallas_call | solution.py:276
  42.2 8.4 %all-to-all-start.1 = ((f32[8,16,128]{2,1,0:T(8,128)}), f32[8,16,128]{2,1,0:T(8,128)S(1)}, u32[]{:S(2)}, u32[]{:S(2)}) async-start(f32[8,16,128]{2,1,0:T(8,128)} %get-tuple-element.50.refs_2_), calls=%async_computation.1 | async-start | bytes 131072 | tf_op jit(solution)/shard_map/all_to_all | solution.py:623
  50.7 2.8 %collective-permute-start.8 = (f32[46,8,128]{2,1,0:T(8,128)S(1)}, f32[46,8,128]{2,1,0:T(8,128)S(1)}, u32[]{:S(2)}, u32[]{:S(2)}) collective-permute-start(f32[46,8,128]{2,1,0:T(8,128)S(1)} %get-tuple-element.53), channel_id=1, source_target_pairs={{0,1},{1,0},{2,3},{3,2},{4,5},{5,4},{6,7},{7,6},{8,9},{9,8},{10,11... | collective-permute-start | bytes 565256 | tf_op jit(solution)/shard_map/ppermute | solution.py:298
  53.6 1.9 %collective-permute-start.9 = (f32[46,8,128]{2,1,0:T(8,128)S(1)}, f32[46,8,128]{2,1,0:T(8,128)S(1)}, u32[]{:S(2)}, u32[]{:S(2)}) collective-permute-start(f32[46,8,128]{2,1,0:T(8,128)S(1)} %get-tuple-element.54), channel_id=1, source_target_pairs={{1,2},{3,4},{5,6},{7,8},{9,10},{11,12},{13,14},{15,16},{17,18},{19... | collective-permute-start | bytes 565256 | tf_op jit(solution)/shard_map/ppermute | solution.py:298
  55.5 0.0 copy-start.1
  55.5 0.0 copy-start.7
  55.5 0.0 copy-start.9
  55.5 0.8 collective-permute-start.10
  56.3 6.5 %all-to-all-done.1.refs_0_ = f32[8,16,128]{2,1,0:T(8,128)S(1)} async-done(((f32[8,16,128]{2,1,0:T(8,128)}), f32[8,16,128]{2,1,0:T(8,128)S(1)}, u32[]{:S(2)}, u32[]{:S(2)}) %all-to-all-start.1) | async-done | bytes 65568 | tf_op jit(solution)/shard_map/all_to_all | solution.py:623
  62.9 0.6 line_shares.1
  63.5 4.2 %all-to-all-start.2 = ((f32[4,8,128]{2,1,0:T(8,128)}), f32[4,8,128]{2,1,0:T(8,128)S(1)}, u32[]{:S(2)}, u32[]{:S(2)}) async-start(f32[4,8,128]{2,1,0:T(8,128)} %get-tuple-element.51.refs_3_), calls=%async_computation.2 | async-start | bytes 32768 | tf_op jit(solution)/shard_map/all_to_all | solution.py:649
  67.7 0.0 collective-permute-done.10.refs_2_
  67.7 0.0 collective-permute-done.8.refs_3_
  67.7 0.0 collective-permute-done.9.refs_4_
  67.7 0.0 copy-done.1
  67.7 0.0 copy-done.7
  67.7 0.0 copy-done.9
  67.7 2.7 %far_field.1 = (f32[30,8,128]{2,1,0:T(8,128)S(1)}, f32[136,128]{1,0:T(8,128)S(1)}) custom-call(s32[3,30]{1,0:T(4,128)S(1)} %bitcast.10, s32[30]{0:T(128)S(1)} %copy-done.9, f32[30,8,128]{2,1,0:T(8,128)S(1)} %get-tuple-element.52.refs_1_.refs_2_, f32[46,8,128]{2,1,0:T(8,128)S(1)} %collective-permute-done.8.refs_3_, ...), custom_call_target="tpu_custom_call" | custom-call | flops 2147483648 | bytes 5368709 | tf_op jit(solution)/shard_map/far_field/pallas_call | solution.py:276
  70.4 0.7 copy-done.13
  71.1 0.8 all-to-all-done.2.refs_0_
  71.9 1.2 %top_turn.1 = f32[16,8,128]{2,1,0:T(8,128)} custom-call(f32[4,8,128]{2,1,0:T(8,128)S(1)} %all-to-all-done.2.refs_0_, f32[136,128]{1,0:T(8,128)S(1)} %get-tuple-element.58.refs_1_), custom_call_target="tpu_custom_call" | custom-call | flops 2147483648 | bytes 5368709 | tf_op jit(solution)/shard_map/top_turn/pallas_call | solution.py:276
  73.1 7.0 %all-to-all-start.3 = ((f32[16,8,128]{2,1,0:T(8,128)}), f32[16,8,128]{2,1,0:T(8,128)S(1)}, u32[]{:S(2)}, u32[]{:S(2)}) async-start(f32[16,8,128]{2,1,0:T(8,128)} %top_turn.1), calls=%async_computation.3 | async-start | bytes 131072 | tf_op jit(solution)/shard_map/all_to_all | solution.py:696
  80.1 0.0 copy-done
  80.1 0.0 copy-done.8
  80.1 0.0 copy-done.10
  80.2 3.0 %near_field.1.refs_1_ = f32[296,128]{1,0:T(8,128)S(1)} custom-call(s32[2,16]{1,0:T(2,128)S(1)} %bitcast.11, s32[16]{0:T(128)S(1)} %copy-done.10, f32[16,2048]{1,0:T(8,128)S(1)} %copy-done.6, f32[46,8,128]{2,1,0:T(8,128)S(1)} %collective-permute-done.8.refs_3_, f32[46,8,128]{2,1,0:T(8,128)S(1)} %collective-permute-done.9.refs_4_, ...), custom_call_target="tpu_custom_call" | custom-call | flops 2147483648 | bytes 5368709 | tf_op jit(solution)/shard_map/near_field/pallas_call | solution.py:276
  83.1 0.7 copy-done.12
  83.8 2.2 %all-to-all-done.3.refs_0_ = f32[16,8,128]{2,1,0:T(8,128)S(1)} async-done(((f32[16,8,128]{2,1,0:T(8,128)}), f32[16,8,128]{2,1,0:T(8,128)S(1)}, u32[]{:S(2)}, u32[]{:S(2)}) %all-to-all-start.3) | async-done | bytes 65568 | tf_op jit(solution)/shard_map/all_to_all | solution.py:696
  86.0 0.6 copy-done.14
  86.7 4.6 %downward.1 = f32[16,2048]{1,0:T(8,128)} custom-call(f32[16,8,128]{2,1,0:T(8,128)} %copy-done.14, f32[296,128]{1,0:T(8,128)} %copy-done.12, bf16[30,64,128]{2,1,0:T(8,128)(2,1)} %copy-done.11, f32[30,8,128]{2,1,0:T(8,128)} %copy-done.13, f32[16,64,128]{2,1,0:T(8,128)} %refs_4_.1), custom_call_target="tpu_custom_call" | custom-call | flops 4294967296 | bytes 10737418 | tf_op jit(solution)/shard_map/downward/pallas_call | solution.py:276
  (11 shorter events, 0.1 us)
Async XLA Ops:
  0.0 1.0 %copy-start.4 = (f32[1,9,2,4096]{3,2,1,0:T(2,128)S(1)}, f32[1,9,2,4096]{3,2,1,0:T(2,128)}, u32[]{:S(2)}) copy-start(f32[1,9,2,4096]{3,2,1,0:T(2,128)} %param.18) | copy-start | bytes 884740
  1.0 0.9 copy-start.5
  1.9 11.4 %copy-start.2 = (f32[30,4096]{1,0:T(8,128)S(1)}, f32[30,4096]{1,0:T(8,128)}, u32[]{:S(2)}) copy-start(f32[30,4096]{1,0:T(8,128)} %refs_2_.2) | copy-start | bytes 1474564
  1.9 11.4 %copy-start.3 = (f32[16,64,128]{2,1,0:T(8,128)S(1)}, f32[16,64,128]{2,1,0:T(8,128)}, u32[]{:S(2)}) copy-start(f32[16,64,128]{2,1,0:T(8,128)} %refs_4_.1) | copy-start | bytes 1572868
  1.9 11.4 %copy-start.6 = (f32[16,2048]{1,0:T(8,128)S(1)}, f32[16,2048]{1,0:T(8,128)}, u32[]{:S(2)}) copy-start(f32[16,2048]{1,0:T(8,128)} %refs_2_.3) | copy-start | bytes 393220
  2.1 9.3 %collective-permute-start.1 = (f32[14,32,128]{2,1,0:T(8,128)S(1)}, f32[14,32,128]{2,1,0:T(8,128)S(1)}, u32[]{:S(2)}, u32[]{:S(2)}) collective-permute-start(f32[14,32,128]{2,1,0:T(8,128)S(1)} %get-tuple-element.37), channel_id=1, source_target_pairs={{0,1},{16,17},{32,33},{48,49},{64,65},{80,81},{96,97},{112,113},{1... | collective-permute-start | bytes 688136 | tf_op jit(solution)/shard_map/ppermute | solution.py:298
  3.5 0.7 collective-permute-start
  11.3 6.3 %collective-permute-start.2 = (f32[3,32,128]{2,1,0:T(8,128)S(1)}, f32[3,32,128]{2,1,0:T(8,128)S(1)}, u32[]{:S(2)}, u32[]{:S(2)}) collective-permute-start(f32[3,32,128]{2,1,0:T(8,128)S(1)} %get-tuple-element.38), channel_id=1, source_target_pairs={{0,4},{8,12},{16,20},{24,28},{32,36},{40,44},{48,52},{56,60},{64,6... | collective-permute-start | bytes 147464 | tf_op jit(solution)/shard_map/ppermute | solution.py:298
  14.9 12.8 %copy-start.11 = (bf16[30,64,128]{2,1,0:T(8,128)(2,1)}, bf16[30,64,128]{2,1,0:T(8,128)(2,1)S(1)}, u32[]{:S(2)}) copy-start(bf16[30,64,128]{2,1,0:T(8,128)(2,1)S(1)} %get-tuple-element.61.refs_2_) | copy-start | bytes 1474564
  17.7 5.2 %collective-permute-start.3 = (f32[5,32,128]{2,1,0:T(8,128)S(1)}, f32[5,32,128]{2,1,0:T(8,128)S(1)}, u32[]{:S(2)}, u32[]{:S(2)}) collective-permute-start(f32[5,32,128]{2,1,0:T(8,128)S(1)} %get-tuple-element.40), channel_id=1, source_target_pairs={{0,2},{4,6},{8,10},{12,14},{16,18},{20,22},{24,26},{28,30},{32,34}... | collective-permute-start | bytes 245768 | tf_op jit(solution)/shard_map/ppermute | solution.py:298
  23.6 4.1 %collective-permute-start.5 = (f32[7,32,128]{2,1,0:T(8,128)S(1)}, f32[7,32,128]{2,1,0:T(8,128)S(1)}, u32[]{:S(2)}, u32[]{:S(2)}) collective-permute-start(f32[7,32,128]{2,1,0:T(8,128)S(1)} %get-tuple-element.46), channel_id=1, source_target_pairs={{1,33},{65,97},{129,161},{193,225},{257,289},{321,353},{385,417},{... | collective-permute-start | bytes 344072 | tf_op jit(solution)/shard_map/ppermute | solution.py:298
  24.9 2.8 %collective-permute-start.6 = (f32[5,32,128]{2,1,0:T(8,128)S(1)}, f32[5,32,128]{2,1,0:T(8,128)S(1)}, u32[]{:S(2)}, u32[]{:S(2)}) collective-permute-start(f32[5,32,128]{2,1,0:T(8,128)S(1)} %get-tuple-element.45.refs_1_), channel_id=1, source_target_pairs={{1,97},{129,225},{257,353},{385,481}} | collective-permute-start | bytes 245768 | tf_op jit(solution)/shard_map/ppermute | solution.py:298
  26.2 3.2 %collective-permute-start.4 = (f32[7,32,128]{2,1,0:T(8,128)S(1)}, f32[7,32,128]{2,1,0:T(8,128)S(1)}, u32[]{:S(2)}, u32[]{:S(2)}) collective-permute-start(f32[7,32,128]{2,1,0:T(8,128)S(1)} %get-tuple-element.44), channel_id=1, source_target_pairs={{0,1},{2,3},{4,5},{6,7},{8,9},{10,11},{12,13},{14,15},{16,17},{18,... | collective-permute-start | bytes 344072 | tf_op jit(solution)/shard_map/ppermute | solution.py:298
  31.1 9.7 %all-to-all-start = ((f32[16,16,128]{2,1,0:T(8,128)}), f32[16,16,128]{2,1,0:T(8,128)S(1)}, u32[]{:S(2)}, u32[]{:S(2)}) async-start(f32[16,16,128]{2,1,0:T(8,128)} %get-tuple-element.48), calls=%async_computation | async-start | bytes 262144 | tf_op jit(solution)/shard_map/all_to_all | solution.py:614
  34.6 3.7 %collective-permute-start.7 = (f32[9,32,128]{2,1,0:T(8,128)S(1)}, f32[9,32,128]{2,1,0:T(8,128)S(1)}, u32[]{:S(2)}, u32[]{:S(2)}) collective-permute-start(f32[9,32,128]{2,1,0:T(8,128)S(1)} %get-tuple-element.49), channel_id=1, source_target_pairs={{1,17},{33,49},{65,81},{97,113},{129,145},{161,177},{193,209},{225... | collective-permute-start | bytes 442376 | tf_op jit(solution)/shard_map/ppermute | solution.py:298
  42.2 20.6 %all-to-all-start.1 = ((f32[8,16,128]{2,1,0:T(8,128)}), f32[8,16,128]{2,1,0:T(8,128)S(1)}, u32[]{:S(2)}, u32[]{:S(2)}) async-start(f32[8,16,128]{2,1,0:T(8,128)} %get-tuple-element.50.refs_2_), calls=%async_computation.1 | async-start | bytes 131072 | tf_op jit(solution)/shard_map/all_to_all | solution.py:623
  50.7 17.0 %collective-permute-start.8 = (f32[46,8,128]{2,1,0:T(8,128)S(1)}, f32[46,8,128]{2,1,0:T(8,128)S(1)}, u32[]{:S(2)}, u32[]{:S(2)}) collective-permute-start(f32[46,8,128]{2,1,0:T(8,128)S(1)} %get-tuple-element.53), channel_id=1, source_target_pairs={{0,1},{1,0},{2,3},{3,2},{4,5},{5,4},{6,7},{7,6},{8,9},{9,8},{10,11... | collective-permute-start | bytes 565256 | tf_op jit(solution)/shard_map/ppermute | solution.py:298
  53.6 14.1 %collective-permute-start.9 = (f32[46,8,128]{2,1,0:T(8,128)S(1)}, f32[46,8,128]{2,1,0:T(8,128)S(1)}, u32[]{:S(2)}, u32[]{:S(2)}) collective-permute-start(f32[46,8,128]{2,1,0:T(8,128)S(1)} %get-tuple-element.54), channel_id=1, source_target_pairs={{1,2},{3,4},{5,6},{7,8},{9,10},{11,12},{13,14},{15,16},{17,18},{19... | collective-permute-start | bytes 565256 | tf_op jit(solution)/shard_map/ppermute | solution.py:298
  55.5 12.2 %copy-start.1 = (f32[30,3,4096]{2,0,1:T(8,128)S(1)}, f32[30,3,4096]{2,0,1:T(8,128)}, u32[]{:S(2)}) copy-start(f32[30,3,4096]{2,0,1:T(8,128)} %param.14) | copy-start | bytes 4423684
  55.5 12.2 %copy-start.7 = (s32[30,3]{0,1:T(4,128)S(1)}, s32[30,3]{0,1:T(4,128)}, u32[]{:S(2)}) copy-start(s32[30,3]{0,1:T(4,128)} %param.15) | copy-start | bytes 1084
  55.5 12.2 %copy-start.9 = (s32[30]{0:T(128)S(1)}, s32[30]{0:T(128)}, u32[]{:S(2)}) copy-start(s32[30]{0:T(128)} %refs_1_.4) | copy-start | bytes 364
  55.5 12.1 %collective-permute-start.10 = (f32[5,32,128]{2,1,0:T(8,128)S(1)}, f32[5,32,128]{2,1,0:T(8,128)S(1)}, u32[]{:S(2)}, u32[]{:S(2)}) collective-permute-start(f32[5,32,128]{2,1,0:T(8,128)S(1)} %get-tuple-element.56.refs_0_), channel_id=1, source_target_pairs={{33,65},{161,193},{289,321},{417,449},{97,81},{225,209},{353,337},... | collective-permute-start | bytes 245768 | tf_op jit(solution)/shard_map/ppermute | solution.py:298
  63.5 8.4 %all-to-all-start.2 = ((f32[4,8,128]{2,1,0:T(8,128)}), f32[4,8,128]{2,1,0:T(8,128)S(1)}, u32[]{:S(2)}, u32[]{:S(2)}) async-start(f32[4,8,128]{2,1,0:T(8,128)} %get-tuple-element.51.refs_3_), calls=%async_computation.2 | async-start | bytes 32768 | tf_op jit(solution)/shard_map/all_to_all | solution.py:649
  70.4 0.7 copy-start.13
  71.9 8.3 %copy-start = (f32[16,2,128,128]{3,2,1,0:T(8,128)S(1)}, f32[16,2,128,128]{3,2,1,0:T(8,128)}, u32[]{:S(2)}) copy-start(f32[16,2,128,128]{3,2,1,0:T(8,128)} %refs_5_.1) | copy-start | bytes 6291460
  71.9 8.3 %copy-start.8 = (s32[16,2]{0,1:T(2,128)S(1)}, s32[16,2]{0,1:T(2,128)}, u32[]{:S(2)}) copy-start(s32[16,2]{0,1:T(2,128)} %param.20) | copy-start | bytes 388
  71.9 8.3 %copy-start.10 = (s32[16]{0:T(128)S(1)}, s32[16]{0:T(128)}, u32[]{:S(2)}) copy-start(s32[16]{0:T(128)} %refs_1_.5) | copy-start | bytes 196
  73.1 12.9 %all-to-all-start.3 = ((f32[16,8,128]{2,1,0:T(8,128)}), f32[16,8,128]{2,1,0:T(8,128)S(1)}, u32[]{:S(2)}, u32[]{:S(2)}) async-start(f32[16,8,128]{2,1,0:T(8,128)} %top_turn.1), calls=%async_computation.3 | async-start | bytes 131072 | tf_op jit(solution)/shard_map/all_to_all | solution.py:696
  83.1 0.7 copy-start.12
  86.0 0.6 copy-start.14

commit v6 on v5

--- a/solution.py
+++ b/solution.py
@@ -242,6 +242,8 @@
     smem = pl.BlockSpec(memory_space=pltpu.SMEM)
     spare = pl.BlockSpec(memory_space=pl.ANY)
     given, slow, spares = len(args), len(lazy), len(after)
+    parts = [(start, size) for _, start, size in lazy]
+    lazy = [item for item, _, _ in lazy]
 
     def body(*refs):
         own = refs[given + slow + spares :]
@@ -250,9 +252,8 @@
         if slow:
             own, targets, semaphores = own[: -slow - 1], own[-slow - 1 : -1], own[-1]
             for i, target in enumerate(targets):
-                copies.append(
-                    pltpu.make_async_copy(refs[given + i], target, semaphores.at[i])
-                )
+                source = refs[given + i].at[pl.ds(parts[i][0], parts[i][1])]
+                copies.append(pltpu.make_async_copy(source, target, semaphores.at[i]))
                 copies[-1].start()
             waiting = set(range(slow))
 
@@ -270,7 +271,10 @@
         for get in getters:
             get()
 
-    buffers = [pltpu.VMEM(item.shape, item.dtype) for item in lazy]
+    buffers = [
+        pltpu.VMEM((size, *item.shape[1:]), item.dtype)
+        for item, (_, size) in zip(lazy, parts)
+    ]
     if lazy:
         buffers.append(pltpu.SemaphoreType.DMA((slow,)))
     result = pl.pallas_call(
@@ -487,10 +491,9 @@
         out[other] = value
 
 
-def down_kernel(given, near, forms, far, basis, out):
-    near = near()
-    value = times_t(given[PORTER], near[NEAR_ROWS + 8 : NEAR_ROWS + 40])
-    value = value + near[NEAR_ROWS : NEAR_ROWS + 8]
+def down_kernel(given, prepared, far, forms, basis, near, out):
+    prepared = prepared()
+    value = times_t(given[PORTER], prepared[8:40]) + prepared[0:8]
     parents = [value]
     forms, far = forms(), far()
     for clusters, offset in reversed(LAYOUT):
@@ -502,7 +505,7 @@
             following.append(weave(raw, 0) + far[first])
             following.append(weave(raw, 1) + far[first + 1])
         parents = following
-    basis = basis()
+    basis, near = basis(), near()
     for leaf in range(LEAVES):
         high, low = split(unpack(parents[leaf]))
         basis_high, basis_low = split(basis[leaf])
@@ -699,7 +702,13 @@
         "downward",
         [shape(16, LEAVES * POINTS)],
         [given],
-        lazy=[near, forms, far, leaf_cluster_basis],
+        lazy=[
+            (near, NEAR_ROWS, 40),
+            (far, 0, LOCAL),
+            (forms, 0, LOCAL),
+            (leaf_cluster_basis, 0, LEAVES),
+            (near, 0, NEAR_ROWS),
+        ],
         flops=4 << 30,
     )
 

time: 91.9 us -> 91.8 us (level)
  no operation moved by 1% of the time
where the time goes in v6:
time: 91.8 us; the launch traced here: 91.1 us
  starting transfers between devices  39.7 us (43%)
  waiting for transfers between devices  29.6 us (32%)
  Pallas kernels  17.7 us (19%)
  local copies, waits for them, and re-layouts  3.88 us (4%)
    pallas_call x15, Pallas kernels, call(): pl.pallas_call(body, out_shape=list(outs), in_specs=[smem] * scalars + [v...  17.7 us
    ppermute x11, waiting for transfers between devices, permute(): return lax.ppermute(value, 'leaf', pairs)  17.5 us
    ppermute x11, starting transfers between devices, permute(): return lax.ppermute(value, 'leaf', pairs)  16.7 us
    all_to_all x1, starting transfers between devices, on_device(): given = lax.all_to_all(blocks, 'leaf', 0, 0, axis_index_groups=in_column)  8.45 us
    all_to_all x1, starting transfers between devices, on_device(): given = lax.all_to_all(turned, 'leaf', 0, 0, axis_index_groups=in_group)  6.99 us
    all_to_all x1, waiting for transfers between devices, on_device(): given = lax.all_to_all(blocks, 'leaf', 0, 0, axis_index_groups=in_column)  6.54 us
    all_to_all x1, starting transfers between devices, on_device(): given = lax.all_to_all(blocks, 'leaf', 0, 0, axis_index_groups=in_line)  4.18 us
    unnamed x30, local copies, waits for them, and re-layouts  3.88 us
  transfers between devices with their start and end apart: 15, of which 10 were waited for; matrix products, arithmetic and copies ran while one was open for 0% of the time, Pallas kernels for 9%

profile of v6, /device:TPU:1, one launch (start us, length us, event | category | flops | bytes accessed | tf_op | source)
XLA Modules:
  0.0 91.1 jit_solution(15925261191462218937)
XLA Ops:
  0.0 0.0 copy-start.4
  0.0 1.0 %copy-done.4 = f32[1,9,2,4096]{3,2,1,0:T(2,128)S(1)} copy-done((f32[1,9,2,4096]{3,2,1,0:T(2,128)S(1)}, f32[1,9,2,4096]{3,2,1,0:T(2,128)}, u32[]{:S(2)}) %copy-start.4) | copy-done | bytes 294936
  1.0 0.0 copy-start.5
  1.0 0.9 copy-done.5
  1.9 0.0 copy-start.3
  1.9 0.0 copy-start.6
  1.9 0.2 top_tables.1
  2.1 1.4 %collective-permute-start.1 = (f32[14,32,128]{2,1,0:T(8,128)S(1)}, f32[14,32,128]{2,1,0:T(8,128)S(1)}, u32[]{:S(2)}, u32[]{:S(2)}) collective-permute-start(f32[14,32,128]{2,1,0:T(8,128)S(1)} %get-tuple-element.37), channel_id=1, source_target_pairs={{0,1},{16,17},{32,33},{48,49},{64,65},{80,81},{96,97},{112,113},{1... | collective-permute-start | bytes 688136 | tf_op jit(solution)/shard_map/ppermute | solution.py:302
  3.5 0.7 collective-permute-start
  4.2 0.0 collective-permute-done.refs_1_
  4.2 7.2 %collective-permute-done.1.refs_2_.refs_3_.refs_0_ = f32[14,32,128]{2,1,0:T(8,128)S(1)} collective-permute-done((f32[14,32,128]{2,1,0:T(8,128)S(1)}, f32[14,32,128]{2,1,0:T(8,128)S(1)}, u32[]{:S(2)}, u32[]{:S(2)}) %collective-permute-start.1) | collective-permute-done | bytes 229408 | tf_op jit(solution)/shard_map/ppermute | solution.py:302
  11.3 1.9 %collective-permute-start.2 = (f32[3,32,128]{2,1,0:T(8,128)S(1)}, f32[3,32,128]{2,1,0:T(8,128)S(1)}, u32[]{:S(2)}, u32[]{:S(2)}) collective-permute-start(f32[3,32,128]{2,1,0:T(8,128)S(1)} %get-tuple-element.38), channel_id=1, source_target_pairs={{0,4},{8,12},{16,20},{24,28},{32,36},{40,44},{48,52},{56,60},{64,6... | collective-permute-start | bytes 147464 | tf_op jit(solution)/shard_map/ppermute | solution.py:302
  13.3 0.0 copy-done.2
  13.3 0.0 copy-done.3
  13.3 0.0 copy-done.6
  13.3 1.6 %upward.1 = (f32[30,8,128]{2,1,0:T(8,128)S(1)}, f32[8,128]{1,0:T(8,128)S(1)}, bf16[30,64,128]{2,1,0:T(8,128)(2,1)S(1)}) custom-call(f32[16,2048]{1,0:T(8,128)S(1)} %copy-done.6, f32[16,64,128]{2,1,0:T(8,128)S(1)} %copy-done.3, f32[30,4096]{1,0:T(8,128)S(1)} %copy-done.2), custom_call_target="tpu_custom_call" | custom-call | flops 2147483648 | bytes 5368709 | tf_op jit(solution)/shard_map/upward/pallas_call | solution.py:280
  14.9 0.0 copy-start.11
  14.9 2.8 %collective-permute-done.2.refs_1_ = f32[3,32,128]{2,1,0:T(8,128)S(1)} collective-permute-done((f32[3,32,128]{2,1,0:T(8,128)S(1)}, f32[3,32,128]{2,1,0:T(8,128)S(1)}, u32[]{:S(2)}, u32[]{:S(2)}) %collective-permute-start.2) | collective-permute-done | bytes 49184 | tf_op jit(solution)/shard_map/ppermute | solution.py:302
  17.7 1.9 %collective-permute-start.3 = (f32[5,32,128]{2,1,0:T(8,128)S(1)}, f32[5,32,128]{2,1,0:T(8,128)S(1)}, u32[]{:S(2)}, u32[]{:S(2)}) collective-permute-start(f32[5,32,128]{2,1,0:T(8,128)S(1)} %get-tuple-element.40), channel_id=1, source_target_pairs={{0,2},{4,6},{8,10},{12,14},{16,18},{20,22},{24,26},{28,30},{32,34}... | collective-permute-start | bytes 245768 | tf_op jit(solution)/shard_map/ppermute | solution.py:302
  19.6 3.3 %collective-permute-done.3.refs_1_ = f32[5,32,128]{2,1,0:T(8,128)S(1)} collective-permute-done((f32[5,32,128]{2,1,0:T(8,128)S(1)}, f32[5,32,128]{2,1,0:T(8,128)S(1)}, u32[]{:S(2)}, u32[]{:S(2)}) %collective-permute-start.3) | collective-permute-done | bytes 81952 | tf_op jit(solution)/shard_map/ppermute | solution.py:302
  22.9 0.7 hand_down_3.1
  23.6 1.3 %collective-permute-start.5 = (f32[7,32,128]{2,1,0:T(8,128)S(1)}, f32[7,32,128]{2,1,0:T(8,128)S(1)}, u32[]{:S(2)}, u32[]{:S(2)}) collective-permute-start(f32[7,32,128]{2,1,0:T(8,128)S(1)} %get-tuple-element.46), channel_id=1, source_target_pairs={{1,33},{65,97},{129,161},{193,225},{257,289},{321,353},{385,417},{... | collective-permute-start | bytes 344072 | tf_op jit(solution)/shard_map/ppermute | solution.py:302
  24.9 1.3 %collective-permute-start.6 = (f32[5,32,128]{2,1,0:T(8,128)S(1)}, f32[5,32,128]{2,1,0:T(8,128)S(1)}, u32[]{:S(2)}, u32[]{:S(2)}) collective-permute-start(f32[5,32,128]{2,1,0:T(8,128)S(1)} %get-tuple-element.45.refs_1_), channel_id=1, source_target_pairs={{1,97},{129,225},{257,353},{385,481}} | collective-permute-start | bytes 245768 | tf_op jit(solution)/shard_map/ppermute | solution.py:302
  26.2 1.3 %collective-permute-start.4 = (f32[7,32,128]{2,1,0:T(8,128)S(1)}, f32[7,32,128]{2,1,0:T(8,128)S(1)}, u32[]{:S(2)}, u32[]{:S(2)}) collective-permute-start(f32[7,32,128]{2,1,0:T(8,128)S(1)} %get-tuple-element.44), channel_id=1, source_target_pairs={{0,1},{2,3},{4,5},{6,7},{8,9},{10,11},{12,13},{14,15},{16,17},{18,... | collective-permute-start | bytes 344072 | tf_op jit(solution)/shard_map/ppermute | solution.py:302
  27.5 0.2 collective-permute-done.6.refs_3_
  27.6 0.0 collective-permute-done.5.refs_2_
  27.7 0.0 copy-done.11
  27.7 1.7 %collective-permute-done.4.refs_3_ = f32[7,32,128]{2,1,0:T(8,128)S(1)} collective-permute-done((f32[7,32,128]{2,1,0:T(8,128)S(1)}, f32[7,32,128]{2,1,0:T(8,128)S(1)}, u32[]{:S(2)}, u32[]{:S(2)}) %collective-permute-start.4) | collective-permute-done | bytes 114720 | tf_op jit(solution)/shard_map/ppermute | solution.py:302
  29.4 1.7 %group_shares.1 = (f32[16,16,128]{2,1,0:T(8,128)}, f32[7,32,128]{2,1,0:T(8,128)S(1)}) custom-call(f32[8,128]{1,0:T(8,128)S(1)} %get-tuple-element.34.refs_4_.refs_0_, f32[12,32,128]{2,1,0:T(8,128)S(1)} %get-tuple-element.35.refs_0_.refs_1_.refs_7_, f32[5,32,128]{2,1,0:T(8,128)S(1)} %get-tuple-element.43.refs_2_, ...), custom_call_target="tpu_custom_call" | custom-call | flops 2147483648 | bytes 5368709 | tf_op jit(solution)/shard_map/group_shares/pallas_call | solution.py:280
  31.1 3.5 %all-to-all-start = ((f32[16,16,128]{2,1,0:T(8,128)}), f32[16,16,128]{2,1,0:T(8,128)S(1)}, u32[]{:S(2)}, u32[]{:S(2)}) async-start(f32[16,16,128]{2,1,0:T(8,128)} %get-tuple-element.48), calls=%async_computation | async-start | bytes 262144 | tf_op jit(solution)/shard_map/all_to_all | solution.py:617
  34.6 1.3 %collective-permute-start.7 = (f32[9,32,128]{2,1,0:T(8,128)S(1)}, f32[9,32,128]{2,1,0:T(8,128)S(1)}, u32[]{:S(2)}, u32[]{:S(2)}) collective-permute-start(f32[9,32,128]{2,1,0:T(8,128)S(1)} %get-tuple-element.49), channel_id=1, source_target_pairs={{1,17},{33,49},{65,81},{97,113},{129,145},{161,177},{193,209},{225... | collective-permute-start | bytes 442376 | tf_op jit(solution)/shard_map/ppermute | solution.py:302
  35.9 2.4 %collective-permute-done.7.refs_2_.refs_1_ = f32[9,32,128]{2,1,0:T(8,128)S(1)} collective-permute-done((f32[9,32,128]{2,1,0:T(8,128)S(1)}, f32[9,32,128]{2,1,0:T(8,128)S(1)}, u32[]{:S(2)}, u32[]{:S(2)}) %collective-permute-start.7) | collective-permute-done | bytes 147488 | tf_op jit(solution)/shard_map/ppermute | solution.py:302
  38.3 2.5 %all-to-all-done.refs_0_ = f32[16,16,128]{2,1,0:T(8,128)S(1)} async-done(((f32[16,16,128]{2,1,0:T(8,128)}), f32[16,16,128]{2,1,0:T(8,128)S(1)}, u32[]{:S(2)}, u32[]{:S(2)}) %all-to-all-start) | async-done | bytes 131104 | tf_op jit(solution)/shard_map/all_to_all | solution.py:617
  40.8 1.4 %column_shares.1 = (f32[8,16,128]{2,1,0:T(8,128)}, f32[4,8,128]{2,1,0:T(8,128)S(1)}, f32[5,32,128]{2,1,0:T(8,128)S(1)}) custom-call(f32[16,16,128]{2,1,0:T(8,128)S(1)} %all-to-all-done.refs_0_, f32[5,32,128]{2,1,0:T(8,128)S(1)} %get-tuple-element.47.refs_4_.refs_1_, f32[9,32,128]{2,1,0:T(8,128)S(1)} %collective-permute-done.7.refs_2_.refs_1_), custom_call_target="tpu_custom_call" | custom-call | flops 2147483648 | bytes 5368709 | tf_op jit(solution)/shard_map/column_shares/pallas_call | solution.py:280
  42.2 8.4 %all-to-all-start.1 = ((f32[8,16,128]{2,1,0:T(8,128)}), f32[8,16,128]{2,1,0:T(8,128)S(1)}, u32[]{:S(2)}, u32[]{:S(2)}) async-start(f32[8,16,128]{2,1,0:T(8,128)} %get-tuple-element.50.refs_2_), calls=%async_computation.1 | async-start | bytes 131072 | tf_op jit(solution)/shard_map/all_to_all | solution.py:626
  50.7 2.8 %collective-permute-start.8 = (f32[46,8,128]{2,1,0:T(8,128)S(1)}, f32[46,8,128]{2,1,0:T(8,128)S(1)}, u32[]{:S(2)}, u32[]{:S(2)}) collective-permute-start(f32[46,8,128]{2,1,0:T(8,128)S(1)} %get-tuple-element.53), channel_id=1, source_target_pairs={{0,1},{1,0},{2,3},{3,2},{4,5},{5,4},{6,7},{7,6},{8,9},{9,8},{10,11... | collective-permute-start | bytes 565256 | tf_op jit(solution)/shard_map/ppermute | solution.py:302
  53.6 1.9 %collective-permute-start.9 = (f32[46,8,128]{2,1,0:T(8,128)S(1)}, f32[46,8,128]{2,1,0:T(8,128)S(1)}, u32[]{:S(2)}, u32[]{:S(2)}) collective-permute-start(f32[46,8,128]{2,1,0:T(8,128)S(1)} %get-tuple-element.54), channel_id=1, source_target_pairs={{1,2},{3,4},{5,6},{7,8},{9,10},{11,12},{13,14},{15,16},{17,18},{19... | collective-permute-start | bytes 565256 | tf_op jit(solution)/shard_map/ppermute | solution.py:302
  55.5 0.0 copy-start.1
  55.5 0.0 copy-start.7
  55.5 0.0 copy-start.9
  55.5 0.8 collective-permute-start.10
  56.3 6.5 %all-to-all-done.1.refs_0_ = f32[8,16,128]{2,1,0:T(8,128)S(1)} async-done(((f32[8,16,128]{2,1,0:T(8,128)}), f32[8,16,128]{2,1,0:T(8,128)S(1)}, u32[]{:S(2)}, u32[]{:S(2)}) %all-to-all-start.1) | async-done | bytes 65568 | tf_op jit(solution)/shard_map/all_to_all | solution.py:626
  62.9 0.6 line_shares.1
  63.5 4.2 %all-to-all-start.2 = ((f32[4,8,128]{2,1,0:T(8,128)}), f32[4,8,128]{2,1,0:T(8,128)S(1)}, u32[]{:S(2)}, u32[]{:S(2)}) async-start(f32[4,8,128]{2,1,0:T(8,128)} %get-tuple-element.51.refs_3_), calls=%async_computation.2 | async-start | bytes 32768 | tf_op jit(solution)/shard_map/all_to_all | solution.py:652
  67.7 0.0 collective-permute-done.10.refs_2_
  67.7 0.0 collective-permute-done.8.refs_3_
  67.7 0.0 collective-permute-done.9.refs_4_
  67.7 0.0 copy-done.1
  67.7 0.0 copy-done.7
  67.7 0.0 copy-done.9
  67.7 2.7 %far_field.1 = (f32[30,8,128]{2,1,0:T(8,128)S(1)}, f32[136,128]{1,0:T(8,128)S(1)}) custom-call(s32[3,30]{1,0:T(4,128)S(1)} %bitcast.10, s32[30]{0:T(128)S(1)} %copy-done.9, f32[30,8,128]{2,1,0:T(8,128)S(1)} %get-tuple-element.52.refs_1_.refs_2_, f32[46,8,128]{2,1,0:T(8,128)S(1)} %collective-permute-done.8.refs_3_, ...), custom_call_target="tpu_custom_call" | custom-call | flops 2147483648 | bytes 5368709 | tf_op jit(solution)/shard_map/far_field/pallas_call | solution.py:280
  70.4 0.0 copy-start.13
  70.4 0.7 copy-done.13
  71.1 0.8 all-to-all-done.2.refs_0_
  71.9 1.2 %top_turn.1 = f32[16,8,128]{2,1,0:T(8,128)} custom-call(f32[4,8,128]{2,1,0:T(8,128)S(1)} %all-to-all-done.2.refs_0_, f32[136,128]{1,0:T(8,128)S(1)} %get-tuple-element.58.refs_1_), custom_call_target="tpu_custom_call" | custom-call | flops 2147483648 | bytes 5368709 | tf_op jit(solution)/shard_map/top_turn/pallas_call | solution.py:280
  73.1 7.0 %all-to-all-start.3 = ((f32[16,8,128]{2,1,0:T(8,128)}), f32[16,8,128]{2,1,0:T(8,128)S(1)}, u32[]{:S(2)}, u32[]{:S(2)}) async-start(f32[16,8,128]{2,1,0:T(8,128)} %top_turn.1), calls=%async_computation.3 | async-start | bytes 131072 | tf_op jit(solution)/shard_map/all_to_all | solution.py:699
  80.1 0.0 copy-done
  80.1 0.0 copy-done.8
  80.1 0.0 copy-done.10
  80.2 3.0 %near_field.1.refs_1_.refs_5_ = f32[296,128]{1,0:T(8,128)S(1)} custom-call(s32[2,16]{1,0:T(2,128)S(1)} %bitcast.11, s32[16]{0:T(128)S(1)} %copy-done.10, f32[16,2048]{1,0:T(8,128)S(1)} %copy-done.6, f32[46,8,128]{2,1,0:T(8,128)S(1)} %collective-permute-done.8.refs_3_, f32[46,8,128]{2,1,0:T(8,128)S(1)} %collective-permute-done.9.refs_4_, ...), custom_call_target="tpu_custom_call" | custom-call | flops 2147483648 | bytes 5368709 | tf_op jit(solution)/shard_map/near_field/pallas_call | solution.py:280
  83.1 0.7 copy-done.12
  83.8 2.2 %all-to-all-done.3.refs_0_ = f32[16,8,128]{2,1,0:T(8,128)S(1)} async-done(((f32[16,8,128]{2,1,0:T(8,128)}), f32[16,8,128]{2,1,0:T(8,128)S(1)}, u32[]{:S(2)}, u32[]{:S(2)}) %all-to-all-start.3) | async-done | bytes 65568 | tf_op jit(solution)/shard_map/all_to_all | solution.py:699
  86.0 0.6 copy-done.14
  86.7 4.5 %downward.1 = f32[16,2048]{1,0:T(8,128)} custom-call(f32[16,8,128]{2,1,0:T(8,128)} %copy-done.14, f32[296,128]{1,0:T(8,128)} %copy-done.12, f32[30,8,128]{2,1,0:T(8,128)} %copy-done.13, bf16[30,64,128]{2,1,0:T(8,128)(2,1)} %copy-done.11, f32[16,64,128]{2,1,0:T(8,128)} %refs_4_.1, f32[296,128]{1,0:T(8,128)} %copy-done.12), custom_call_target="tpu_custom_call" | custom-call | flops 4294967296 | bytes 10737418 | tf_op jit(solution)/shard_map/downward/pallas_call | solution.py:280
  (11 shorter events, 0.1 us)
Async XLA Ops:
  0.0 1.0 %copy-start.4 = (f32[1,9,2,4096]{3,2,1,0:T(2,128)S(1)}, f32[1,9,2,4096]{3,2,1,0:T(2,128)}, u32[]{:S(2)}) copy-start(f32[1,9,2,4096]{3,2,1,0:T(2,128)} %param.18) | copy-start | bytes 884740
  1.0 0.9 copy-start.5
  1.9 11.4 %copy-start.2 = (f32[30,4096]{1,0:T(8,128)S(1)}, f32[30,4096]{1,0:T(8,128)}, u32[]{:S(2)}) copy-start(f32[30,4096]{1,0:T(8,128)} %refs_2_.2) | copy-start | bytes 1474564
  1.9 11.4 %copy-start.3 = (f32[16,64,128]{2,1,0:T(8,128)S(1)}, f32[16,64,128]{2,1,0:T(8,128)}, u32[]{:S(2)}) copy-start(f32[16,64,128]{2,1,0:T(8,128)} %refs_4_.1) | copy-start | bytes 1572868
  1.9 11.4 %copy-start.6 = (f32[16,2048]{1,0:T(8,128)S(1)}, f32[16,2048]{1,0:T(8,128)}, u32[]{:S(2)}) copy-start(f32[16,2048]{1,0:T(8,128)} %refs_2_.3) | copy-start | bytes 393220
  2.1 9.3 %collective-permute-start.1 = (f32[14,32,128]{2,1,0:T(8,128)S(1)}, f32[14,32,128]{2,1,0:T(8,128)S(1)}, u32[]{:S(2)}, u32[]{:S(2)}) collective-permute-start(f32[14,32,128]{2,1,0:T(8,128)S(1)} %get-tuple-element.37), channel_id=1, source_target_pairs={{0,1},{16,17},{32,33},{48,49},{64,65},{80,81},{96,97},{112,113},{1... | collective-permute-start | bytes 688136 | tf_op jit(solution)/shard_map/ppermute | solution.py:302
  3.5 0.7 collective-permute-start
  11.3 6.3 %collective-permute-start.2 = (f32[3,32,128]{2,1,0:T(8,128)S(1)}, f32[3,32,128]{2,1,0:T(8,128)S(1)}, u32[]{:S(2)}, u32[]{:S(2)}) collective-permute-start(f32[3,32,128]{2,1,0:T(8,128)S(1)} %get-tuple-element.38), channel_id=1, source_target_pairs={{0,4},{8,12},{16,20},{24,28},{32,36},{40,44},{48,52},{56,60},{64,6... | collective-permute-start | bytes 147464 | tf_op jit(solution)/shard_map/ppermute | solution.py:302
  14.9 12.8 %copy-start.11 = (bf16[30,64,128]{2,1,0:T(8,128)(2,1)}, bf16[30,64,128]{2,1,0:T(8,128)(2,1)S(1)}, u32[]{:S(2)}) copy-start(bf16[30,64,128]{2,1,0:T(8,128)(2,1)S(1)} %get-tuple-element.62.refs_3_) | copy-start | bytes 1474564
  17.7 5.2 %collective-permute-start.3 = (f32[5,32,128]{2,1,0:T(8,128)S(1)}, f32[5,32,128]{2,1,0:T(8,128)S(1)}, u32[]{:S(2)}, u32[]{:S(2)}) collective-permute-start(f32[5,32,128]{2,1,0:T(8,128)S(1)} %get-tuple-element.40), channel_id=1, source_target_pairs={{0,2},{4,6},{8,10},{12,14},{16,18},{20,22},{24,26},{28,30},{32,34}... | collective-permute-start | bytes 245768 | tf_op jit(solution)/shard_map/ppermute | solution.py:302
  23.6 4.1 %collective-permute-start.5 = (f32[7,32,128]{2,1,0:T(8,128)S(1)}, f32[7,32,128]{2,1,0:T(8,128)S(1)}, u32[]{:S(2)}, u32[]{:S(2)}) collective-permute-start(f32[7,32,128]{2,1,0:T(8,128)S(1)} %get-tuple-element.46), channel_id=1, source_target_pairs={{1,33},{65,97},{129,161},{193,225},{257,289},{321,353},{385,417},{... | collective-permute-start | bytes 344072 | tf_op jit(solution)/shard_map/ppermute | solution.py:302
  24.9 2.8 %collective-permute-start.6 = (f32[5,32,128]{2,1,0:T(8,128)S(1)}, f32[5,32,128]{2,1,0:T(8,128)S(1)}, u32[]{:S(2)}, u32[]{:S(2)}) collective-permute-start(f32[5,32,128]{2,1,0:T(8,128)S(1)} %get-tuple-element.45.refs_1_), channel_id=1, source_target_pairs={{1,97},{129,225},{257,353},{385,481}} | collective-permute-start | bytes 245768 | tf_op jit(solution)/shard_map/ppermute | solution.py:302
  26.2 3.2 %collective-permute-start.4 = (f32[7,32,128]{2,1,0:T(8,128)S(1)}, f32[7,32,128]{2,1,0:T(8,128)S(1)}, u32[]{:S(2)}, u32[]{:S(2)}) collective-permute-start(f32[7,32,128]{2,1,0:T(8,128)S(1)} %get-tuple-element.44), channel_id=1, source_target_pairs={{0,1},{2,3},{4,5},{6,7},{8,9},{10,11},{12,13},{14,15},{16,17},{18,... | collective-permute-start | bytes 344072 | tf_op jit(solution)/shard_map/ppermute | solution.py:302
  31.1 9.7 %all-to-all-start = ((f32[16,16,128]{2,1,0:T(8,128)}), f32[16,16,128]{2,1,0:T(8,128)S(1)}, u32[]{:S(2)}, u32[]{:S(2)}) async-start(f32[16,16,128]{2,1,0:T(8,128)} %get-tuple-element.48), calls=%async_computation | async-start | bytes 262144 | tf_op jit(solution)/shard_map/all_to_all | solution.py:617
  34.6 3.7 %collective-permute-start.7 = (f32[9,32,128]{2,1,0:T(8,128)S(1)}, f32[9,32,128]{2,1,0:T(8,128)S(1)}, u32[]{:S(2)}, u32[]{:S(2)}) collective-permute-start(f32[9,32,128]{2,1,0:T(8,128)S(1)} %get-tuple-element.49), channel_id=1, source_target_pairs={{1,17},{33,49},{65,81},{97,113},{129,145},{161,177},{193,209},{225... | collective-permute-start | bytes 442376 | tf_op jit(solution)/shard_map/ppermute | solution.py:302
  42.2 20.6 %all-to-all-start.1 = ((f32[8,16,128]{2,1,0:T(8,128)}), f32[8,16,128]{2,1,0:T(8,128)S(1)}, u32[]{:S(2)}, u32[]{:S(2)}) async-start(f32[8,16,128]{2,1,0:T(8,128)} %get-tuple-element.50.refs_2_), calls=%async_computation.1 | async-start | bytes 131072 | tf_op jit(solution)/shard_map/all_to_all | solution.py:626
  50.7 17.0 %collective-permute-start.8 = (f32[46,8,128]{2,1,0:T(8,128)S(1)}, f32[46,8,128]{2,1,0:T(8,128)S(1)}, u32[]{:S(2)}, u32[]{:S(2)}) collective-permute-start(f32[46,8,128]{2,1,0:T(8,128)S(1)} %get-tuple-element.53), channel_id=1, source_target_pairs={{0,1},{1,0},{2,3},{3,2},{4,5},{5,4},{6,7},{7,6},{8,9},{9,8},{10,11... | collective-permute-start | bytes 565256 | tf_op jit(solution)/shard_map/ppermute | solution.py:302
  53.6 14.1 %collective-permute-start.9 = (f32[46,8,128]{2,1,0:T(8,128)S(1)}, f32[46,8,128]{2,1,0:T(8,128)S(1)}, u32[]{:S(2)}, u32[]{:S(2)}) collective-permute-start(f32[46,8,128]{2,1,0:T(8,128)S(1)} %get-tuple-element.54), channel_id=1, source_target_pairs={{1,2},{3,4},{5,6},{7,8},{9,10},{11,12},{13,14},{15,16},{17,18},{19... | collective-permute-start | bytes 565256 | tf_op jit(solution)/shard_map/ppermute | solution.py:302
  55.5 12.2 %copy-start.1 = (f32[30,3,4096]{2,0,1:T(8,128)S(1)}, f32[30,3,4096]{2,0,1:T(8,128)}, u32[]{:S(2)}) copy-start(f32[30,3,4096]{2,0,1:T(8,128)} %param.14) | copy-start | bytes 4423684
  55.5 12.2 %copy-start.7 = (s32[30,3]{0,1:T(4,128)S(1)}, s32[30,3]{0,1:T(4,128)}, u32[]{:S(2)}) copy-start(s32[30,3]{0,1:T(4,128)} %param.15) | copy-start | bytes 1084
  55.5 12.2 %copy-start.9 = (s32[30]{0:T(128)S(1)}, s32[30]{0:T(128)}, u32[]{:S(2)}) copy-start(s32[30]{0:T(128)} %refs_1_.4) | copy-start | bytes 364
  55.5 12.1 %collective-permute-start.10 = (f32[5,32,128]{2,1,0:T(8,128)S(1)}, f32[5,32,128]{2,1,0:T(8,128)S(1)}, u32[]{:S(2)}, u32[]{:S(2)}) collective-permute-start(f32[5,32,128]{2,1,0:T(8,128)S(1)} %get-tuple-element.56.refs_0_), channel_id=1, source_target_pairs={{33,65},{161,193},{289,321},{417,449},{97,81},{225,209},{353,337},... | collective-permute-start | bytes 245768 | tf_op jit(solution)/shard_map/ppermute | solution.py:302
  63.5 8.4 %all-to-all-start.2 = ((f32[4,8,128]{2,1,0:T(8,128)}), f32[4,8,128]{2,1,0:T(8,128)S(1)}, u32[]{:S(2)}, u32[]{:S(2)}) async-start(f32[4,8,128]{2,1,0:T(8,128)} %get-tuple-element.51.refs_3_), calls=%async_computation.2 | async-start | bytes 32768 | tf_op jit(solution)/shard_map/all_to_all | solution.py:652
  70.4 0.7 copy-start.13
  71.9 8.3 %copy-start = (f32[16,2,128,128]{3,2,1,0:T(8,128)S(1)}, f32[16,2,128,128]{3,2,1,0:T(8,128)}, u32[]{:S(2)}) copy-start(f32[16,2,128,128]{3,2,1,0:T(8,128)} %refs_5_.1) | copy-start | bytes 6291460
  71.9 8.3 %copy-start.8 = (s32[16,2]{0,1:T(2,128)S(1)}, s32[16,2]{0,1:T(2,128)}, u32[]{:S(2)}) copy-start(s32[16,2]{0,1:T(2,128)} %param.20) | copy-start | bytes 388
  71.9 8.3 %copy-start.10 = (s32[16]{0:T(128)S(1)}, s32[16]{0:T(128)}, u32[]{:S(2)}) copy-start(s32[16]{0:T(128)} %refs_1_.5) | copy-start | bytes 196
  73.1 12.9 %all-to-all-start.3 = ((f32[16,8,128]{2,1,0:T(8,128)}), f32[16,8,128]{2,1,0:T(8,128)S(1)}, u32[]{:S(2)}, u32[]{:S(2)}) async-start(f32[16,8,128]{2,1,0:T(8,128)} %top_turn.1), calls=%async_computation.3 | async-start | bytes 131072 | tf_op jit(solution)/shard_map/all_to_all | solution.py:699
  83.1 0.7 copy-start.12
  86.0 0.6 copy-start.14
